TPU v7x, 32 devices: a whole 2x2x4 slice. The times are simulated.
32 devices in a mesh: seq: 16 (over z, y, core), ch: 2 (over x).
Axes of the slice: x: 2, y: 2, z: 4, core: 2. Of those that a mesh axis runs over, the one named last changes fastest.
Arguments:
- grad_out: bfloat16 [4096, 4096], P('seq', 'ch'), may hold values from -6 to 6
- saved_in: bfloat16 [4096, 4096], P('seq', 'ch'), may hold values from -6 to 6
- filter_taps: bfloat16 [256, 4096], P(None, 'ch'), may hold values from -0.375 to 0.375
- skip_gain: float32 [4096], P('ch'), may hold values from 0.5 to 1.5
- projection: bfloat16 [4096, 4096], P('seq', 'ch'), may hold values from -0.09375 to 0.09375
Outputs:
- grad_in: bfloat16 [4096, 4096], P('seq', 'ch')
- filter_grad: float32 [256, 4096], P('seq', 'ch')
All inputs are finite; a program needn't handle non-finite values.
Results may differ from a plain program's by a relative error of at most 0.015.
Values may be sent and summed in bfloat16 or wider, within the bound.
No kernel may reach another device: no remote copies, remote signals or barrier semaphores. Data moves between devices by JAX's collectives and lax.ppermute only.
A program may use at most 64 MiB of HBM per device.

v0:
```python
import math

import jax
import jax.numpy as jnp
from jax import lax
from jax.sharding import PartitionSpec as P


def passed_along(value, axis, steps):
    count = lax.axis_size(axis)
    leading, last = (max(0, -steps), min(count, count - steps))
    return lax.ppermute(value, axis, [(source, source + steps) for source in range(leading, last)])


def swapped(x, axis, stride):
    return lax.ppermute(x, axis, [(i, i ^ 1 << stride) for i in range(lax.axis_size(axis))])


def window(signal, kernel):
    result = lax.conv_general_dilated(
        signal[None],
        kernel[:, None, :],
        (1,),
        [(0, 0)],
        dimension_numbers=("NWC", "WIO", "NWC"),
        feature_group_count=signal.shape[1],
        preferred_element_type=jnp.float32,
    )
    return result[0]


def neighbours(upper_pair, lower_pair):
    from_above = passed_along(upper_pair, "seq", -1)
    from_below = passed_along(lower_pair, "seq", 1)
    return (from_above, from_below)


def mirror_inputs(stacked):
    bit_count = lax.axis_size(("seq", "ch")).bit_length() - 1
    for bit_index in range(bit_count):
        stacked = swapped(stacked, ("seq", "ch"), bit_index)
    return stacked


def mirror_result(values):
    bit_count = lax.axis_size(("seq", "ch")).bit_length() - 1
    for bit_index in range(bit_count):
        values = swapped(values, ("seq", "ch"), bit_index)
    return values


def seq_total(partials):
    return (lax.psum_scatter(partials[0], "seq", scatter_dimension=0, tiled=True),)


def body(grad_out, saved_in, filter_taps, skip_gain, projection):
    tok_rows = grad_out.shape[0]
    edge = 2 * tok_rows - 1
    mirrored = mirror_inputs(jnp.stack([grad_out, saved_in]))
    rc_grad = mirrored[0, ::-1, ::-1]
    rc_input = mirrored[1, ::-1, ::-1]
    upper_rows, lower_rows = neighbours(
        jnp.stack([grad_out, rc_grad]), jnp.stack([saved_in, rc_input])
    )
    conv_forward = window(jnp.concatenate([grad_out, upper_rows[0]], axis=0)[:edge], filter_taps)
    conv_mirror = window(jnp.concatenate([rc_grad, upper_rows[1]], axis=0)[:edge], filter_taps)
    taps_forward = window(jnp.concatenate([lower_rows[0], saved_in], axis=0)[1:], grad_out)[::-1]
    taps_mirror = window(jnp.concatenate([lower_rows[1], rc_input], axis=0)[1:], rc_grad)[::-1]
    returned = mirror_result(conv_mirror[::-1, ::-1])
    conv_sum = conv_forward + returned
    filter_part = seq_total((taps_forward + taps_mirror,))[0]
    grad_conv = (conv_sum + skip_gain[None, :] * grad_out.astype(jnp.float32)).astype(jnp.bfloat16)
    partial_value = lax.dot_general(
        grad_conv,
        lax.all_gather(projection, "seq", axis=0, tiled=True),
        (((1,), (1,)), ((), ())),
        preferred_element_type=jnp.float32,
    )
    grad_in = lax.psum_scatter(
        partial_value.astype(jnp.bfloat16), "ch", scatter_dimension=1, tiled=True
    )
    total_rows = tok_rows * lax.axis_size("seq")
    filter_grad = filter_part * (1.0 / math.sqrt(total_rows))
    return (grad_in, filter_grad)


def solution(mesh):
    placed = (P("seq", "ch"), P("seq", "ch"), P(None, "ch"), P("ch"), P("seq", "ch"))
    return jax.shard_map(
        body,
        mesh=mesh,
        in_specs=placed,
        out_specs=(P("seq", "ch"), P("seq", "ch")),
        check_vma=False,
    )
```

profile of v0, /device:TPU:0, one launch (start us, length us, event | category | flops | bytes accessed | tf_op | source)
XLA Modules:
  0.0 819.6 jit_solution(12761841215992801447)
XLA Ops:
  12.0 45.6 %collective-permute-done = bf16[2,256,2048]{2,1,0:T(8,128)(2,1)S(1)} collective-permute-done((bf16[2,256,2048]{2,1,0:T(8,128)(2,1)S(1)}, bf16[2,256,2048]{2,1,0:T(8,128)(2,1)S(1)}, u32[]{:S(2)}, u32[]{:S(2)}) %collective-permute-start) | collective-permute-done | bytes 2097184 | tf_op jit(solution)/shard_map/ppermute | solution.py:16
  57.7 4.2 collective-permute-done.1
  63.6 45.9 %collective-permute-done.2 = bf16[2,256,2048]{2,1,0:T(8,128)(2,1)S(1)} collective-permute-done((bf16[2,256,2048]{2,1,0:T(8,128)(2,1)S(1)}, bf16[2,256,2048]{2,1,0:T(8,128)(2,1)S(1)}, u32[]{:S(2)}, u32[]{:S(2)}) %collective-permute-start.2) | collective-permute-done | bytes 2097184 | tf_op jit(solution)/shard_map/ppermute | solution.py:16
  111.3 45.2 %collective-permute-done.3 = bf16[2,256,2048]{2,1,0:T(8,128)(2,1)} collective-permute-done((bf16[2,256,2048]{2,1,0:T(8,128)(2,1)S(1)}, bf16[2,256,2048]{2,1,0:T(8,128)(2,1)}, u32[]{:S(2)}, u32[]{:S(2)}) %collective-permute-start.3) | collective-permute-done | bytes 2097184 | tf_op jit(solution)/shard_map/ppermute | solution.py:16
  159.4 173.6 %collective-permute-done.4 = bf16[2,256,2048]{2,1,0:T(8,128)(2,1)S(1)} collective-permute-done((bf16[2,256,2048]{2,1,0:T(8,128)(2,1)}, bf16[2,256,2048]{2,1,0:T(8,128)(2,1)S(1)}, u32[]{:S(2)}, u32[]{:S(2)}) %collective-permute-start.4) | collective-permute-done | bytes 2097184 | tf_op jit(solution)/shard_map/ppermute | solution.py:16
  334.5 14.0 %rev.15 = bf16[1,256,2048]{2,1,0:T(8,128)(2,1)S(1)} reverse(bf16[1,256,2048]{2,1,0:T(8,128)(2,1)} %get-tuple-element.5), dimensions={1,2} | reverse | bytes 2097152 | tf_op jit(solution)/shard_map/rev | solution.py:60
  350.0 5.4 collective-permute-done.5
  356.7 54.2 %fusion.4 = f32[1,256,2048]{2,0,1:T(1,128)S(1)} fusion(bf16[1,511,2048]{2,1,0:T(8,128)(2,1)S(1)} %fusion.10, bf16[256,1,2048]{2,0,1:T(8,128)(2,1)S(1)} %bitcast.41), kind=kOutput, calls=%fused_computation.5 | convolution fusion | flops 268435456 | bytes 5238784 | tf_op jit(solution)/shard_map/conv_general_dilated | solution.py:20
  413.1 17.6 %rev.16 = f32[256,2048]{1,0:T(8,128)} reverse(f32[256,2048]{1,0:T(8,128)} %bitcast.50), dimensions={0,1} | reverse | bytes 4194304 | tf_op jit(solution)/shard_map/rev | solution.py:69
  432.2 13.9 %rev.17 = bf16[1,256,2048]{2,1,0:T(8,128)(2,1)S(1)} reverse(bf16[1,256,2048]{2,1,0:T(8,128)(2,1)} %get-tuple-element.4), dimensions={1,2} | reverse | bytes 2097152 | tf_op jit(solution)/shard_map/rev | solution.py:61
  447.5 22.7 %collective-permute-start.11 = (bf16[2,256,2048]{2,1,0:T(8,128)(2,1)S(1)}, bf16[2,256,2048]{2,1,0:T(8,128)(2,1)S(1)}, u32[]{:S(2)}, u32[]{:S(2)}) collective-permute-start(bf16[2,256,2048]{2,1,0:T(8,128)(2,1)S(1)} %pad_maximum_fusion.6), channel_id=1, source_target_pairs={{0,2},{2,4},{4,6},{6,8},{8,10},{10,12},{12,14},{14,16},{16,18},{18... | collective-permute-start | bytes 6291464 | tf_op jit(solution)/shard_map/ppermute | solution.py:12
  470.3 9.0 %collective-permute-start.7 = (f32[256,2048]{1,0:T(8,128)}, f32[256,2048]{1,0:T(8,128)S(1)}, u32[]{:S(2)}, u32[]{:S(2)}) collective-permute-start(f32[256,2048]{1,0:T(8,128)} %collective-permute-done.6), channel_id=1, source_target_pairs={{0,2},{1,3},{2,0},{3,1},{4,6},{5,7},{6,4},{7,5},{8,10},{9,11},{10,... | collective-permute-start | bytes 6291464 | tf_op jit(solution)/shard_map/ppermute | solution.py:16
  483.3 19.0 %collective-permute-start.8 = (f32[256,2048]{1,0:T(8,128)S(1)}, f32[256,2048]{1,0:T(8,128)}, u32[]{:S(2)}, u32[]{:S(2)}) collective-permute-start(f32[256,2048]{1,0:T(8,128)S(1)} %collective-permute-done.7), channel_id=1, source_target_pairs={{0,4},{1,5},{2,6},{3,7},{4,0},{5,1},{6,2},{7,3},{8,12},{9,13},{10,... | collective-permute-start | bytes 6291464 | tf_op jit(solution)/shard_map/ppermute | solution.py:16
  502.3 54.2 %fusion = f32[1,256,2048]{2,0,1:T(1,128)S(1)} fusion(bf16[1,511,2048]{2,1,0:T(8,128)(2,1)S(1)} %get-tuple-element.8, bf16[256,1,2048]{2,0,1:T(8,128)(2,1)S(1)} %bitcast.43), kind=kOutput, calls=%fused_computation.1 | convolution fusion | flops 268435456 | bytes 5238784 | tf_op jit(solution)/shard_map/conv_general_dilated | solution.py:20
  556.8 54.6 %fusion.2 = f32[1,256,2048]{2,0,1:T(1,128)} fusion(bf16[1,511,2048]{2,1,0:T(8,128)(2,1)S(1)} %get-tuple-element.9, bf16[256,1,2048]{2,0,1:T(8,128)(2,1)S(1)} %bitcast.46), kind=kOutput, calls=%fused_computation.3 | convolution fusion | flops 268435456 | bytes 5238784 | tf_op jit(solution)/shard_map/conv_general_dilated | solution.py:20
  613.6 16.6 %rev.19 = f32[256,2048]{1,0:T(8,128)} reverse(f32[256,2048]{1,0:T(8,128)} %bitcast.51), dimensions={0} | reverse | bytes 4194304 | tf_op jit(solution)/shard_map/rev | solution.py:68
  630.2 3.9 copy.69
  634.1 16.6 %rev.18 = f32[256,2048]{1,0:T(8,128)} reverse(f32[256,2048]{1,0:T(8,128)} %bitcast.52), dimensions={0} | reverse | bytes 4194304 | tf_op jit(solution)/shard_map/rev | solution.py:67
  650.7 3.9 add.15
  659.7 54.6 %fusion.6 = f32[1,256,2048]{2,0,1:T(1,128)} fusion(bf16[1,511,2048]{2,1,0:T(8,128)(2,1)S(1)} %fusion.11, bf16[256,1,2048]{2,0,1:T(8,128)(2,1)S(1)} %bitcast.40), kind=kOutput, calls=%fused_computation.7 | convolution fusion | flops 268435456 | bytes 5238784 | tf_op jit(solution)/shard_map/conv_general_dilated | solution.py:20
  714.3 44.8 %collective-permute-done.10 = f32[256,2048]{1,0:T(8,128)} collective-permute-done((f32[256,2048]{1,0:T(8,128)}, f32[256,2048]{1,0:T(8,128)}, u32[]{:S(2)}, u32[]{:S(2)}) %collective-permute-start.10) | collective-permute-done | bytes 2097184 | tf_op jit(solution)/shard_map/ppermute | solution.py:16
  759.1 11.2 %convolution_convert_fusion = bf16[256,4096]{1,0:T(8,128)(2,1)} fusion(bf16[4096,2048]{1,0:T(8,128)(2,1)} %all-gather.2.cloned.1.call-done, f32[256,2048]{1,0:T(8,128)} %collective-permute-done.10, f32[1,256,2048]{2,0,1:T(1,128)} %fusion.6, bf16[256,2048]{1,0:T(8,128)(2,1)S(1)} %copy-done.2, f32[2048]{0:T(1024)S(1)} %copy-done.5), kind=kOutput, calls=%fused_computation | convolution fusion | flops 4298637312 | bytes 24125440 | tf_op jit(solution)/shard_map/dot_general | solution.py:73
  770.3 9.0 %reduce-scatter.5.cloned.1.call-done = f32[16,2048]{1,0:T(8,128)} async-done(((f32[256,2048]{1,0:T(8,128)}), f32[16,2048]{1,0:T(8,128)}) %reduce-scatter.5.cloned.1.call-update) | async-done | bytes 131088 | tf_op jit(solution)/shard_map/reduce_scatter | solution.py:53
  780.8 32.2 %reduce-scatter.3.cloned.1.call-done = bf16[256,2048]{1,0:T(8,128)(2,1)} async-done(((bf16[256,4096]{1,0:T(8,128)(2,1)}), bf16[256,2048]{1,0:T(8,128)(2,1)}) %reduce-scatter.3.cloned.1.call-update) | async-done | bytes 1048592 | tf_op jit(solution)/shard_map/reduce_scatter | solution.py:79
  (45 shorter events, 33.8 us)
Async XLA Ops:
  7.2 349.5 %copy-start = (bf16[256,2048]{1,0:T(8,128)(2,1)S(1)}, bf16[256,2048]{1,0:T(8,128)(2,1)}, u32[]{:S(2)}) copy-start(bf16[256,2048]{1,0:T(8,128)(2,1)} %param.7) | copy-start | bytes 3145732
  7.2 751.9 %all-gather.2.cloned.1.call-start = ((), (), s32[]{:S(2)}) async-start(), calls=%async_computation.2 | async-start | bytes 17825792 | tf_op jit(solution)/shard_map/all_gather | solution.py:75
  9.0 48.6 %collective-permute-start = (bf16[2,256,2048]{2,1,0:T(8,128)(2,1)S(1)}, bf16[2,256,2048]{2,1,0:T(8,128)(2,1)S(1)}, u32[]{:S(2)}, u32[]{:S(2)}) collective-permute-start(bf16[2,256,2048]{2,1,0:T(8,128)(2,1)S(1)} %pad_maximum_fusion), channel_id=1, source_target_pairs={{0,1},{1,0},{2,3},{3,2},{4,5},{5,4},{6,7},{7,6},{8,9},{9,8},{10,11... | collective-permute-start | bytes 6291464 | tf_op jit(solution)/shard_map/ppermute | solution.py:16
  57.7 4.2 collective-permute-start.1
  61.8 47.7 %collective-permute-start.2 = (bf16[2,256,2048]{2,1,0:T(8,128)(2,1)S(1)}, bf16[2,256,2048]{2,1,0:T(8,128)(2,1)S(1)}, u32[]{:S(2)}, u32[]{:S(2)}) collective-permute-start(bf16[2,256,2048]{2,1,0:T(8,128)(2,1)S(1)} %collective-permute-done.1), channel_id=1, source_target_pairs={{0,4},{1,5},{2,6},{3,7},{4,0},{5,1},{6,2},{7,3},{8,12},{9,13},{10,... | collective-permute-start | bytes 6291464 | tf_op jit(solution)/shard_map/ppermute | solution.py:16
  109.5 47.0 %collective-permute-start.3 = (bf16[2,256,2048]{2,1,0:T(8,128)(2,1)S(1)}, bf16[2,256,2048]{2,1,0:T(8,128)(2,1)}, u32[]{:S(2)}, u32[]{:S(2)}) collective-permute-start(bf16[2,256,2048]{2,1,0:T(8,128)(2,1)S(1)} %collective-permute-done.2), channel_id=1, source_target_pairs={{0,8},{1,9},{2,10},{3,11},{4,12},{5,13},{6,14},{7,15},{8,0},{9,1},... | collective-permute-start | bytes 6291464 | tf_op jit(solution)/shard_map/ppermute | solution.py:16
  156.5 176.5 %collective-permute-start.4 = (bf16[2,256,2048]{2,1,0:T(8,128)(2,1)}, bf16[2,256,2048]{2,1,0:T(8,128)(2,1)S(1)}, u32[]{:S(2)}, u32[]{:S(2)}) collective-permute-start(bf16[2,256,2048]{2,1,0:T(8,128)(2,1)} %collective-permute-done.3), channel_id=1, source_target_pairs={{0,16},{1,17},{2,18},{3,19},{4,20},{5,21},{6,22},{7,23},{8,24},{9,... | collective-permute-start | bytes 6291464 | tf_op jit(solution)/shard_map/ppermute | solution.py:16
  159.3 619.9 %reduce-scatter.5.cloned.1.call-start = ((), (), s32[]{:S(2)}) async-start(), calls=%async_computation.4 | async-start | bytes 2228224 | tf_op jit(solution)/shard_map/reduce_scatter | solution.py:53
  334.5 14.0 %copy-start.1 = (bf16[256,2048]{1,0:T(8,128)(2,1)S(1)}, bf16[256,2048]{1,0:T(8,128)(2,1)}, u32[]{:S(2)}) copy-start(bf16[256,2048]{1,0:T(8,128)(2,1)} %param.5) | copy-start | bytes 3145732
  348.7 6.7 collective-permute-start.5
  430.7 39.6 %collective-permute-start.6 = (f32[256,2048]{1,0:T(8,128)}, f32[256,2048]{1,0:T(8,128)}, u32[]{:S(2)}, u32[]{:S(2)}) collective-permute-start(f32[256,2048]{1,0:T(8,128)} %rev.16), channel_id=1, source_target_pairs={{0,1},{1,0},{2,3},{3,2},{4,5},{5,4},{6,7},{7,6},{8,9},{9,8},{10,11... | collective-permute-start | bytes 6291464 | tf_op jit(solution)/shard_map/ppermute | solution.py:16
  447.5 32.0 %copy-start.3 = (bf16[256,2048]{1,0:T(8,128)(2,1)S(1)}, bf16[256,2048]{1,0:T(8,128)(2,1)}, u32[]{:S(2)}) copy-start(bf16[256,2048]{1,0:T(8,128)(2,1)} %param.6) | copy-start | bytes 3145732
  447.5 31.8 %collective-permute-start.11 = (bf16[2,256,2048]{2,1,0:T(8,128)(2,1)S(1)}, bf16[2,256,2048]{2,1,0:T(8,128)(2,1)S(1)}, u32[]{:S(2)}, u32[]{:S(2)}) collective-permute-start(bf16[2,256,2048]{2,1,0:T(8,128)(2,1)S(1)} %pad_maximum_fusion.6), channel_id=1, source_target_pairs={{0,2},{2,4},{4,6},{6,8},{8,10},{10,12},{12,14},{14,16},{16,18},{18... | collective-permute-start | bytes 6291464 | tf_op jit(solution)/shard_map/ppermute | solution.py:12
  470.3 13.0 %collective-permute-start.7 = (f32[256,2048]{1,0:T(8,128)}, f32[256,2048]{1,0:T(8,128)S(1)}, u32[]{:S(2)}, u32[]{:S(2)}) collective-permute-start(f32[256,2048]{1,0:T(8,128)} %collective-permute-done.6), channel_id=1, source_target_pairs={{0,2},{1,3},{2,0},{3,1},{4,6},{5,7},{6,4},{7,5},{8,10},{9,11},{10,... | collective-permute-start | bytes 6291464 | tf_op jit(solution)/shard_map/ppermute | solution.py:16
  483.3 73.2 %collective-permute-start.8 = (f32[256,2048]{1,0:T(8,128)S(1)}, f32[256,2048]{1,0:T(8,128)}, u32[]{:S(2)}, u32[]{:S(2)}) collective-permute-start(f32[256,2048]{1,0:T(8,128)S(1)} %collective-permute-done.7), channel_id=1, source_target_pairs={{0,4},{1,5},{2,6},{3,7},{4,0},{5,1},{6,2},{7,3},{8,12},{9,13},{10,... | collective-permute-start | bytes 6291464 | tf_op jit(solution)/shard_map/ppermute | solution.py:16
  502.3 54.5 %copy-start.2 = (bf16[256,2048]{1,0:T(8,128)(2,1)S(1)}, bf16[256,2048]{1,0:T(8,128)(2,1)}, u32[]{:S(2)}) copy-start(bf16[256,2048]{1,0:T(8,128)(2,1)} %param.5) | copy-start | bytes 3145732
  556.5 99.6 %collective-permute-start.9 = (f32[256,2048]{1,0:T(8,128)}, f32[256,2048]{1,0:T(8,128)}, u32[]{:S(2)}, u32[]{:S(2)}) collective-permute-start(f32[256,2048]{1,0:T(8,128)} %collective-permute-done.8), channel_id=1, source_target_pairs={{0,8},{1,9},{2,10},{3,11},{4,12},{5,13},{6,14},{7,15},{8,0},{9,1},... | collective-permute-start | bytes 6291464 | tf_op jit(solution)/shard_map/ppermute | solution.py:16
  654.7 1.2 copy-start.4
  654.7 158.4 %reduce-scatter.3.cloned.1.call-start = ((), (), s32[]{:S(2)}) async-start(), calls=%async_computation.3 | async-start | bytes 3145728 | tf_op jit(solution)/shard_map/reduce_scatter | solution.py:79
  656.1 103.0 %copy-start.5 = (f32[2048]{0:T(1024)S(1)}, f32[2048]{0:T(1024)}, u32[]{:S(2)}) copy-start(f32[2048]{0:T(1024)} %param.8) | copy-start | bytes 24580
  656.1 103.0 %collective-permute-start.10 = (f32[256,2048]{1,0:T(8,128)}, f32[256,2048]{1,0:T(8,128)}, u32[]{:S(2)}, u32[]{:S(2)}) collective-permute-start(f32[256,2048]{1,0:T(8,128)} %collective-permute-done.9), channel_id=1, source_target_pairs={{0,16},{1,17},{2,18},{3,19},{4,20},{5,21},{6,22},{7,23},{8,24},{9,... | collective-permute-start | bytes 6291464 | tf_op jit(solution)/shard_map/ppermute | solution.py:16
Sparse Core Ops, SparseCore 0:
  159.4 193.6 all-gather.1
  654.8 124.3 reduce-scatter.4
  782.2 30.8 reduce-scatter.2
where the time goes:
time: 826 us; the launch traced here: 820 us
  waiting for transfers between devices  408 us (49%)
  matrix products  229 us (28%)
  local copies, waits for them, and re-layouts  90.8 us (11%)
  starting transfers between devices  67.2 us (8%)
  between operations  13.9 us (2%)
  other arithmetic  10.7 us (1%)
    ppermute x10, waiting for transfers between devices, swapped(): lax.ppermute(x, axis, [(i, i ^ 1 << stride) for i in range(lax.axis_size(...  362 us
    conv_general_dilated x4, matrix products, window(): lax.conv_general_dilated(signal[None], kernel[:, None, :], (1,), [(0, 0)]...  218 us
    ppermute x10, starting transfers between devices, swapped(): lax.ppermute(x, axis, [(i, i ^ 1 << stride) for i in range(lax.axis_size(...  42.8 us
    reduce_scatter x1, waiting for transfers between devices, body(): lax.psum_scatter(partial_value.astype(jnp.bfloat16), 'ch', scatter_dimens...  32.2 us
    ppermute x2, starting transfers between devices, passed_along(): lax.ppermute(value, axis, [(source, source + steps) for source in range(l...  24 us
    rev x1, local copies, waits for them, and re-layouts, body(): returned = mirror_result(conv_mirror[::-1, ::-1])  17.6 us
    rev x1, local copies, waits for them, and re-layouts, body(): window(jnp.concatenate([lower_rows[0], saved_in], axis=0)[1:], grad_out)  16.6 us
    rev x1, local copies, waits for them, and re-layouts, body(): window(jnp.concatenate([lower_rows[1], rc_input], axis=0)[1:], rc_grad)  16.6 us
  transfers between devices with their start and end apart: 15, of which 10 were waited for; matrix products, arithmetic and copies ran while one was open for 40% of the time, Pallas kernels for 0%

commit v1 on v0

v1 whole, which is shorter than its diff:
```python
import math

import jax
import jax.numpy as jnp
import numpy as np
from jax import lax
from jax.experimental import pallas as pl
from jax.experimental.pallas import tpu as pltpu
from jax.sharding import PartitionSpec as P

INNER = 4
F32, BF16 = jnp.float32, jnp.bfloat16
VMEM = pl.BlockSpec(memory_space=pltpu.VMEM)
ANY = pl.BlockSpec(memory_space=pl.ANY)
MIB = 1 << 20
SMALL = pl.CostEstimate(flops=1000, bytes_accessed=1000, transcendentals=0)


def cost(us):
    return pl.CostEstimate(flops=int(us * 1e9), bytes_accessed=int(us * 1e6), transcendentals=0)


def params(mib):
    return pltpu.CompilerParams(vmem_limit_bytes=mib * MIB)


def shape(dims, dtype):
    return jax.ShapeDtypeStruct(dims, dtype)


def swap_seq(value, k):
    count = lax.axis_size("seq")
    return lax.ppermute(value, "seq", [(i, i ^ k) for i in range(count)])


def mirror_ch(value):
    count = lax.axis_size("ch")
    return lax.ppermute(value, "ch", [(i, count - 1 - i) for i in range(count)])


def group_index():
    return lax.rem(lax.axis_index("seq"), INNER)


def columns(block, width):
    return pl.ds(pl.multiple_of(block * width, width), width)


def dot(a, b):
    return jnp.dot(a, b, preferred_element_type=F32)


def dot_nt(a, b):
    return lax.dot_general(a, b, (((1,), (1,)), ((), ())), preferred_element_type=F32)


BLOCKS = INNER + 2
PAIRS = BLOCKS // 2


def angles(j):
    return [2 * math.pi * (j + 0.5) * b / BLOCKS for b in range(BLOCKS)]


def exact(value):
    return 0.0 if abs(value) < 1e-9 else float(value)


def transforms(rows):
    window = BLOCKS * rows
    into, at_taps = [], []
    for j in range(PAIRS):
        upper, lower = [], []
        for index, sign in ((j, 1.0), (BLOCKS - 1 - j, -1.0)):
            k = np.arange(index, window // 2, BLOCKS)
            angle = 2 * np.pi * (k + 0.5)[:, None] * np.arange(rows)[None, :] / window
            c, s = np.cos(angle), np.sin(angle)
            upper += [np.concatenate([c, sign * s], 1), np.concatenate([-s, sign * c], 1)]
            lower += [c, s]
        into.append(np.concatenate(upper, 0))
        at_taps.append(np.concatenate(lower, 0))
    into, at_taps = np.stack(into), np.stack(at_taps)
    cast = lambda a: np.ascontiguousarray(a).astype(np.float32).astype(BF16)
    turn = lambda a: a.transpose(0, 2, 1)
    return {
        "into": cast(into),
        "back": cast(turn(into)),
        "taps": cast(at_taps),
        "lags": cast(turn(at_taps)),
    }


def reversal(count):
    return np.eye(count, dtype=np.float32)[::-1].astype(BF16)


def tie(value, *deps):
    def kernel(*refs):
        pass

    return pl.pallas_call(
        kernel,
        out_shape=shape(value.shape, value.dtype),
        in_specs=[ANY] * (1 + len(deps)),
        out_specs=ANY,
        input_output_aliases={0: 0},
        cost_estimate=SMALL,
        name="tie",
    )(value, *deps)


def quarters(value, deps=(), mirror=None):
    rows, width = value.shape
    cq = width // INNER
    n_in = 1 + (mirror is not None)

    def kernel(*refs):
        q = group_index()
        outs = refs[n_in + len(deps) :]
        for k in range(INNER):
            outs[k][...] = refs[0][:, columns(q ^ k, cq)]
        if mirror is not None:
            outs[INNER][...] = refs[1][:, columns(INNER - 1 - q, cq)]

    out_shape = [shape((rows, cq), value.dtype)] * INNER
    inputs = [value]
    if mirror is not None:
        inputs.append(mirror)
        out_shape.append(shape((mirror.shape[0], cq), mirror.dtype))
    return pl.pallas_call(
        kernel,
        out_shape=out_shape,
        in_specs=[VMEM] * n_in + [ANY] * len(deps),
        out_specs=[VMEM] * len(out_shape),
        compiler_params=params(16),
        cost_estimate=cost(1),
        name="quarters",
    )(*inputs, *deps)


def halves_of_quarters(value, deps):
    rows, width = value.shape
    cq = width // INNER

    def kernel(*refs):
        q = group_index()
        own, near, far = refs[1 + len(deps) :]
        own[...] = refs[0][:, columns(q, cq)]
        near[...] = refs[0][:, columns(q ^ 1, cq)]
        far[0] = refs[0][:, columns(q ^ 2, cq)]
        far[1] = refs[0][:, columns(q ^ 3, cq)]

    dims = [(rows, cq), (rows, cq), (2, rows, cq)]
    return pl.pallas_call(
        kernel,
        out_shape=[shape(d, value.dtype) for d in dims],
        in_specs=[VMEM] + [ANY] * len(deps),
        out_specs=[VMEM] * 3,
        compiler_params=params(16),
        cost_estimate=cost(1),
        name="halves_of_quarters",
    )(value, *deps)


def spread(pieces):
    return [pieces[0]] + [swap_seq(pieces[k], k) for k in range(1, INNER)]


def combined(blocks, first, j):
    re, im = 0.0, 0.0
    for i, block in enumerate(blocks):
        angle = angles(j)[first + i]
        c, s = exact(math.cos(angle)), exact(-math.sin(angle))
        if c:
            re = re + c * block
        if s:
            im = im + s * block
    return jnp.concatenate([re.astype(BF16), im.astype(BF16)], 0)


def complex_rows(value, n):
    return [(value[2 * i * n : (2 * i + 1) * n], value[(2 * i + 1) * n : (2 * i + 2) * n]) for i in range(2)]


def chunk_of(cq):
    return min(256, cq)


def filtered(pieces, before, after, own_taps, mirrored, gain, const, deps):
    rows, cq = pieces[0].shape
    taps = own_taps.shape[0]
    chunk = chunk_of(cq)
    n = rows // 2
    scale = 2.0 / (BLOCKS * rows)

    def kernel(*refs):
        before_ref, after_ref, taps_ref, mirror_ref, gain_ref, into, back, at_taps = refs[INNER : INNER + 8]
        spectrum, conv, ordered = refs[INNER + 8 + len(deps) :]
        q = group_index()
        for k in range(INNER):
            ordered[q ^ k] = refs[k][...].astype(F32)
        blocks = [before_ref[...].astype(F32)] + [ordered[i] for i in range(INNER)] + [after_ref[...].astype(F32)]
        direct = gain_ref[...]
        outs = [0.0] * INNER
        for j in range(PAIRS):
            g = dot(into[j], combined(blocks, 0, j))
            spectrum[j] = g.astype(BF16)
            own, other = dot(at_taps[j], taps_ref[...]), dot(at_taps[j], mirror_ref[...])
            product = []
            for (gr, gi), (ar, ai), (br, bi) in zip(
                complex_rows(g, n), complex_rows(own, n), complex_rows(other, n)
            ):
                hr, hi = (ar + br + direct) * scale, (ai - bi) * scale
                product += [(gr * hr - gi * hi).astype(BF16), (gr * hi + gi * hr).astype(BF16)]
            w = dot(back[j], jnp.concatenate(product, 0))
            for i in range(INNER):
                angle = angles(j)[i + 1]
                c, s = exact(math.cos(angle)), exact(-math.sin(angle))
                if c:
                    outs[i] = outs[i] + c * w[:rows]
                if s:
                    outs[i] = outs[i] + s * w[rows:]
        for i in range(INNER):
            conv[i * rows : (i + 1) * rows, :] = outs[i].astype(BF16)

    cols = lambda r: pl.BlockSpec((r, chunk), lambda i: (0, i))
    whole = lambda a: pl.BlockSpec(a.shape, lambda i: (0, 0, 0))
    return pl.pallas_call(
        kernel,
        grid=(cq // chunk,),
        out_shape=[shape((PAIRS, 2 * rows, cq), BF16), shape((INNER * rows, cq), BF16)],
        in_specs=[cols(rows)] * (INNER + 2)
        + [cols(taps)] * 2
        + [cols(1)]
        + [whole(const["into"]), whole(const["back"]), whole(const["taps"])]
        + [ANY] * len(deps),
        out_specs=[pl.BlockSpec((PAIRS, 2 * rows, chunk), lambda i: (0, 0, i)), cols(INNER * rows)],
        scratch_shapes=[pltpu.VMEM((INNER, rows, chunk), F32)],
        compiler_params=params(32),
        cost_estimate=cost(6),
        name="filtered",
    )(*pieces, before, after, own_taps, mirrored, gain, const["into"], const["back"], const["taps"], *deps)


def correlations(pieces, spectrum, const, scale, deps):
    rows, cq = pieces[0].shape
    taps = const["lags"].shape[1]
    chunk = chunk_of(cq)
    n = rows // 2
    chunks = cq // chunk

    def kernel(*refs):
        spec, into, lags, flip = refs[INNER : INNER + 4]
        forward, turned, ordered = refs[INNER + 4 + len(deps) :]
        q = group_index()
        for k in range(INNER):
            ordered[q ^ k] = refs[k][...].astype(F32)
        blocks = [ordered[i] for i in range(INNER)]
        even, odd = 0.0, 0.0
        for j in range(PAIRS):
            x = dot(into[j], combined(blocks, 1, j))
            g = spec[j].astype(F32)
            for i, ((xr, xi), (gr, gi)) in enumerate(zip(complex_rows(x, n), complex_rows(g, n))):
                z_re = ((gr * xr + gi * xi) * scale).astype(BF16)
                z_im = ((gi * xr - gr * xi) * scale).astype(BF16)
                even += dot(lags[j, :, 2 * i * n : (2 * i + 1) * n], z_re)
                odd += dot(lags[j, :, (2 * i + 1) * n : (2 * i + 2) * n], z_im)
        forward[...] = even - odd
        turned[...] = dot((even + odd).astype(BF16), flip[...]).astype(BF16)

    cols = lambda r: pl.BlockSpec((r, chunk), lambda i: (0, i))
    whole = lambda a: pl.BlockSpec(a.shape, lambda i: (0, 0, 0))
    return pl.pallas_call(
        kernel,
        grid=(chunks,),
        out_shape=[shape((taps, cq), F32), shape((taps, cq), BF16)],
        in_specs=[cols(rows)] * INNER
        + [pl.BlockSpec((PAIRS, 2 * rows, chunk), lambda i: (0, 0, i))]
        + [whole(const["into"]), whole(const["lags"]), pl.BlockSpec((chunk, chunk), lambda i: (0, 0))]
        + [ANY] * len(deps),
        out_specs=[cols(taps), pl.BlockSpec((taps, chunk), lambda i: (0, chunks - 1 - i))],
        scratch_shapes=[pltpu.VMEM((INNER, rows, chunk), F32)],
        compiler_params=params(32),
        cost_estimate=cost(5),
        name="correlations",
    )(*pieces, spectrum, const["into"], const["lags"], reversal(chunk), *deps)


def own_quarter(filter_taps, mirrored, gain):
    taps, width = filter_taps.shape
    cq = width // INNER

    def kernel(taps_ref, mirror_ref, gain_ref, flip, taps_out, mirror_out, gain_out):
        at = columns(group_index(), cq)
        taps_out[...] = taps_ref[:, at]
        gain_out[...] = gain_ref[:, at]
        mirror_out[...] = dot(mirror_ref[...], flip[...]).astype(BF16)

    return pl.pallas_call(
        kernel,
        out_shape=[shape((taps, cq), BF16), shape((taps, cq), BF16), shape((1, cq), F32)],
        in_specs=[VMEM] * 4,
        out_specs=[VMEM] * 3,
        compiler_params=params(16),
        cost_estimate=cost(1),
        name="own_quarter",
    )(filter_taps, mirrored, gain, reversal(cq))


def project(conv, choices, dtype, deps=()):
    span, cq = conv[0].shape
    o_rows, width = choices[0][1].shape
    tile = span // INNER

    def kernel(*refs):
        blocks = refs[INNER : INNER + len(choices)]
        out, rhs, sem = refs[INNER + len(choices) + len(deps) :]
        q = group_index()
        z = lax.div(lax.axis_index("seq"), INNER)
        early = lax.axis_index("ch") == lax.div(z, 2)
        at_end = (z == 0) | (z == 3)
        holds = {
            "early": early,
            "late": jnp.logical_not(early),
            "early_end": early & at_end,
            "early_mid": early & jnp.logical_not(at_end),
            "late_end": jnp.logical_not(early) & at_end,
            "late_mid": jnp.logical_not(early | at_end),
        }

        @pl.when(pl.program_id(0) == 0)
        def _():
            for (condition, _), block in zip(choices, blocks):
                @pl.when(holds[condition])
                def _():
                    copy = pltpu.make_async_copy(block, rhs, sem)
                    copy.start()
                    copy.wait()

        total = 0.0
        for k in range(INNER):
            total += dot_nt(refs[k][...], rhs[:, columns(q ^ k, cq)])
        out[...] = total.astype(dtype)

    rows = pl.BlockSpec((tile, cq), lambda i: (i, 0))
    return pl.pallas_call(
        kernel,
        grid=(INNER,),
        out_shape=shape((span, o_rows), dtype),
        in_specs=[rows] * INNER + [ANY] * (len(choices) + len(deps)),
        out_specs=pl.BlockSpec((tile, o_rows), lambda i: (i, 0)),
        scratch_shapes=[pltpu.VMEM((o_rows, width), BF16), pltpu.SemaphoreType.DMA],
        compiler_params=params(24),
        cost_estimate=cost(3),
        name="project",
    )(*conv, *[block for _, block in choices], *deps)


def summed_rows(kept, got, dtype):
    span, width = kept.shape
    rows = span // INNER

    def kernel(kept_ref, got_ref, *outs):
        q = group_index()
        for k in range(INNER):
            at = pl.ds(pl.multiple_of((q ^ k) * rows, rows), rows)
            outs[k][...] = (kept_ref[at, :] + got_ref[at, :].astype(F32)).astype(dtype)

    return pl.pallas_call(
        kernel,
        out_shape=[shape((rows, width), dtype)] * INNER,
        in_specs=[VMEM] * 2,
        out_specs=[VMEM] * INNER,
        compiler_params=params(16),
        cost_estimate=cost(1),
        name="summed_rows",
    )(kept, got)


def assembled(rounds, width):
    rows, o_rows = rounds[0][0].shape

    def kernel(*refs):
        q = group_index()
        z = lax.div(lax.axis_index("seq"), INNER)
        out = refs[-1]
        for r in range(2):
            for k in range(INNER):
                block = (lax.rem(z, 2) ^ r) * INNER + (q ^ k)
                out[:, columns(block, o_rows)] = refs[r * INNER + k][...]

    return pl.pallas_call(
        kernel,
        out_shape=shape((rows, width), BF16),
        in_specs=[VMEM] * (2 * INNER),
        out_specs=VMEM,
        compiler_params=params(16),
        cost_estimate=cost(1),
        name="assembled",
    )(*rounds[0], *rounds[1])


def halved(kept, got, bit):
    count = kept.shape[0] // 4 if kept.ndim == 2 else kept.shape[1]
    cq = kept.shape[-1]

    def kernel(kept_ref, got_ref, keep_out, send_out):
        own = lax.rem(lax.div(lax.div(lax.axis_index("seq"), INNER), 1 << bit), 2)
        for side, out in ((own, keep_out), (1 - own, send_out)):
            if bit == 0:
                for high in range(2):
                    at = pl.ds(pl.multiple_of((2 * high + side) * count, count), count)
                    out[high] = (kept_ref[at, :] + got_ref[at, :].astype(F32)).astype(out.dtype)
            else:
                out[...] = (kept_ref[side] + got_ref[side].astype(F32)).astype(out.dtype)

    dims = (2, count, cq) if bit == 0 else (count, cq)
    return pl.pallas_call(
        kernel,
        out_shape=[shape(dims, F32), shape(dims, BF16)],
        in_specs=[VMEM] * 2,
        out_specs=[VMEM] * 2,
        compiler_params=params(8),
        cost_estimate=cost(1),
        name="halved",
    )(kept, got)


def side_by_side(pieces):
    rows, cq = pieces[0].shape

    def kernel(*refs):
        q = group_index()
        for k in range(INNER):
            refs[-1][:, columns(q ^ k, cq)] = refs[k][...]

    return pl.pallas_call(
        kernel,
        out_shape=shape((rows, INNER * cq), pieces[0].dtype),
        in_specs=[VMEM] * INNER,
        out_specs=VMEM,
        compiler_params=params(8),
        cost_estimate=cost(1),
        name="side_by_side",
    )(*pieces)


def placed_by_source(pieces, q):
    result = jnp.zeros((INNER,) + pieces[0].shape, pieces[0].dtype)
    for k, piece in enumerate(pieces):
        result = lax.dynamic_update_index_in_dim(result, piece, q ^ k, 0)
    return result


def by_member(value, q):
    return [lax.dynamic_index_in_dim(value, q ^ k, 0, keepdims=False) for k in range(INNER)]


def pick_member(pieces, q, member):
    result = pieces[0]
    for k in range(1, INNER):
        result = jnp.where((q ^ k) == member, pieces[k], result)
    return result


def body(grad_out, saved_in, filter_taps, skip_gain, projection):
    rows, width = grad_out.shape
    taps = filter_taps.shape[0]
    n_seq, n_ch = lax.axis_size("seq"), lax.axis_size("ch")
    outer = n_seq // INNER
    cq = width // INNER
    span = INNER * rows
    window = span + 2 * rows
    seq = lax.axis_index("seq")
    q, z = seq % INNER, seq // INNER
    const = transforms(rows)
    special = outer == 4 and n_ch == 2

    if special:
        shift = lambda v, table: lax.ppermute(
            v, "seq", [(INNER * a + i, INNER * b + i) for a, b in table for i in range(INNER)]
        )
        near = shift(projection, [(0, 1), (1, 0), (2, 3), (3, 2)])
        mid = shift(projection, [(1, 2), (2, 1)])

    *pieces, mirror_piece = quarters(grad_out, (), filter_taps)
    grads = spread(pieces)
    mirrored = mirror_ch(mirror_piece)
    quarter = own_quarter(filter_taps, mirrored, skip_gain.reshape(1, width))

    before = lax.ppermute(
        pick_member(grads, q, INNER - 1), "seq", [(i, i + INNER) for i in range(n_seq - INNER)]
    )
    after = lax.ppermute(
        pick_member(grads, q, 0), "seq", [(i + INNER, i) for i in range(n_seq - INNER)]
    )
    input_own, input_near, input_far = halves_of_quarters(saved_in, (grads[2],))
    input_far = swap_seq(input_far, 2)
    inputs = [input_own, swap_seq(input_near, 1), input_far[0], swap_seq(input_far[1], 1)]
    spectrum, conv = filtered(grads, before, after, *quarter, const, (input_far,))
    if special:
        near = tie(near, before, after)
        mid = tie(mid, before, after)
        far_ends = shift(mid, [(1, 0), (2, 3)])
        far_mid = shift(near, [(2, 1), (1, 2)])

    conv2 = swap_seq(conv, 2)
    conv1 = swap_seq(conv, 1)
    scale = 2.0 / window / math.sqrt(rows * n_seq)
    forward, turned = correlations(inputs, spectrum, const, scale, ())
    if special:
        conv2 = tie(conv2, far_mid, far_ends, turned)
    conv3 = swap_seq(conv2, 1)
    conv_parts = [conv, conv1, conv2, conv3]

    mirrored = lax.ppermute(
        turned,
        ("seq", "ch"),
        [
            (s * n_ch + c, (s ^ (INNER - 1)) * n_ch + n_ch - 1 - c)
            for s in range(n_seq)
            for c in range(n_ch)
        ],
    )
    if special:
        last = shift(far_mid, [(1, 0), (2, 3)])
        x2 = [("end", far_ends), ("mid", far_mid)]
        x3 = [("end", last), ("mid", mid)]
        sent = lambda late, soon: [("early_" + w, block) for w, block in late] + [("late", soon)]
        kept = lambda late, soon: [("late_" + w, block) for w, block in late] + [("early", soon)]
        first = project(conv_parts, sent(x2, projection), BF16)
        got = mirror_ch(first)
        forward = tie(forward, first)
        lag_kept, lag_sent = halved(forward, mirrored, 0)
        second = project(conv_parts, sent(x3, near), BF16)
        got2 = mirror_ch(second)
        own = project(conv_parts, kept(x2, projection), F32)
        own2 = project(conv_parts, kept(x3, near), F32)
        lag_kept, lag_sent = halved(lag_kept, swap_seq(lag_sent, INNER), 1)
        lag_pieces = summed_rows(lag_kept, swap_seq(lag_sent, 2 * INNER), F32)
        rounds = [spread(summed_rows(own, got, BF16)), spread(summed_rows(own2, got2, BF16))]
        grad_in = assembled(rounds, width)
    else:
        groups = [[INNER * a + i for a in range(outer)] for i in range(INNER)]
        proj_all = lax.all_gather(
            projection, "seq", axis=0, tiled=True, axis_index_groups=groups
        )
        conv_all = placed_by_source(conv_parts, q)
        partial_value = lax.dot_general(
            conv_all.transpose(1, 0, 2).reshape(span, width),
            proj_all,
            (((1,), (1,)), ((), ())),
            preferred_element_type=F32,
        )
        total = lax.psum_scatter(
            partial_value.astype(BF16), "ch", scatter_dimension=1, tiled=True
        )
        o_rows = projection.shape[0]
        moved = spread(by_member(total.reshape(INNER, rows, -1), q))
        stacked = placed_by_source(moved, q).reshape(INNER, rows, -1, o_rows)
        grad_in = stacked.transpose(1, 2, 0, 3).reshape(rows, width)

        groups = [[INNER * a + i for a in range(outer)] for i in range(INNER)]
        summed = lax.psum_scatter(
            forward + mirrored.astype(F32), "seq", scatter_dimension=0, tiled=True, axis_index_groups=groups
        )
        lag_pieces = by_member(summed.reshape(INNER, -1, cq), q)
    filter_grad = side_by_side(spread(lag_pieces))
    return (grad_in, filter_grad)


def solution(mesh):
    placed = (P("seq", "ch"), P("seq", "ch"), P(None, "ch"), P("ch"), P("seq", "ch"))
    return jax.shard_map(
        body,
        mesh=mesh,
        in_specs=placed,
        out_specs=(P("seq", "ch"), P("seq", "ch")),
        check_vma=False,
    )
```

time: 826 us -> 149 us (0.18)
  waiting for transfers between devices: 408 us -> 60.3 us
  matrix products: 229 us -> 0 us
  local copies, waits for them, and re-layouts: 90.8 us -> 19.4 us
  starting transfers between devices: 67.2 us -> 34.6 us
  Pallas kernels: 0 us -> 32.4 us
  between operations: 13.9 us -> 1.07 us
  other arithmetic: 10.7 us -> 0.06 us
    ppermute x12 -> x31, waiting for transfers between devices: 367 us -> 60.3 us  [the longest x5 23.8 us: body(): lax.ppermute(v, 'seq', [(INNER * a + i, INNER * b + i) for a, b in table...]
    conv_general_dilated x4 -> x0, matrix products: 218 us -> none  [window(): lax.conv_general_dilated(signal[None], kernel[:, None, :], (1,), [(0, 0)]...]
    rev x5 -> x0, local copies, waits for them, and re-layouts: 78.7 us -> none  [the longest x1 17.6 us: body(): returned = mirror_result(conv_mirror[::-1, ::-1])]
    reduce_scatter x2 -> x0, waiting for transfers between devices: 41.2 us -> none  [the longest x1 32.2 us: body(): lax.psum_scatter(partial_value.astype(jnp.bfloat16), 'ch', scatter_dimens...]
    pallas_call x0 -> x20, Pallas kernels: none -> 32.4 us  [the longest x4 17.2 us: project(): pl.pallas_call(kernel, grid=(INNER,), out_shape=shape((span, o_rows), dty...]
    ppermute x12 -> x31, starting transfers between devices: 66.8 us -> 34.6 us  [the longest x20 14.6 us: swap_seq(): return lax.ppermute(value, 'seq', [(i, i ^ k) for i in range(count)])]
    dot_general x1 -> x0, matrix products: 11.2 us -> none  [body(): lax.dot_general(grad_conv, lax.all_gather(projection, 'seq', axis=0, tile...]
    unnamed x15 -> x78, local copies, waits for them, and re-layouts: 9.29 us -> 18.3 us
  transfers between devices with their start and end apart: 15 -> 31, of which waited for: 10 -> 14; matrix products, arithmetic and copies ran while one was open for 40% -> 1% of each run, Pallas kernels for 0% -> 21%
where the time goes in v1:
time: 149 us; the launch traced here: 148 us
  waiting for transfers between devices  60.3 us (40%)
  starting transfers between devices  34.6 us (23%)
  Pallas kernels  32.4 us (22%)
  local copies, waits for them, and re-layouts  19.4 us (13%)
    ppermute x5, waiting for transfers between devices, body(): lax.ppermute(v, 'seq', [(INNER * a + i, INNER * b + i) for a, b in table...  23.8 us
    ppermute x20, waiting for transfers between devices, swap_seq(): return lax.ppermute(value, 'seq', [(i, i ^ k) for i in range(count)])  23.1 us
    unnamed x78, local copies, waits for them, and re-layouts  18.3 us
    pallas_call x4, Pallas kernels, project(): pl.pallas_call(kernel, grid=(INNER,), out_shape=shape((span, o_rows), dty...  17.2 us
    ppermute x20, starting transfers between devices, swap_seq(): return lax.ppermute(value, 'seq', [(i, i ^ k) for i in range(count)])  14.6 us
    ppermute x1, waiting for transfers between devices, body(): lax.ppermute(pick_member(grads, q, INNER - 1), 'seq', [(i, i + INNER) for...  12.6 us
    ppermute x5, starting transfers between devices, body(): lax.ppermute(v, 'seq', [(INNER * a + i, INNER * b + i) for a, b in table...  7.29 us
    ppermute x3, starting transfers between devices, mirror_ch(): return lax.ppermute(value, 'ch', [(i, count - 1 - i) for i in range(count)])  6.28 us
  transfers between devices with their start and end apart: 31, of which 14 were waited for; matrix products, arithmetic and copies ran while one was open for 1% of the time, Pallas kernels for 21%

profile of v1, /device:TPU:0, one launch (start us, length us, event | category | flops | bytes accessed | tf_op | source)
XLA Modules:
  0.0 147.9 jit_solution(17172781528991835583)
XLA Ops:
  4.0 3.0 %collective-permute-start.1 = (bf16[256,512]{1,0:T(8,128)(2,1)}, bf16[256,512]{1,0:T(8,128)(2,1)S(1)}, u32[]{:S(2)}, u32[]{:S(2)}) collective-permute-start(bf16[256,512]{1,0:T(8,128)(2,1)} %get-tuple-element.35), channel_id=1, source_target_pairs={{0,4},{2,6},{4,0},{6,2},{8,12},{10,14},{12,8},{14,10},{16,20},{18,... | collective-permute-start | bytes 786440 | tf_op jit(solution)/shard_map/ppermute | solution.py:33
  7.1 2.1 %collective-permute-start.9 = (bf16[256,2048]{1,0:T(8,128)(2,1)}, bf16[256,2048]{1,0:T(8,128)(2,1)S(1)}, u32[]{:S(2)}, u32[]{:S(2)}) collective-permute-start(bf16[256,2048]{1,0:T(8,128)(2,1)} %refs_6_.4), channel_id=1, source_target_pairs={{0,8},{2,10},{4,12},{6,14},{8,0},{10,2},{12,4},{14,6},{16,24},{18,... | collective-permute-start | bytes 3145736 | tf_op jit(solution)/shard_map/ppermute | solution.py:480
  9.2 1.7 %collective-permute-start.11 = (bf16[256,2048]{1,0:T(8,128)(2,1)}, bf16[256,2048]{1,0:T(8,128)(2,1)}, u32[]{:S(2)}, u32[]{:S(2)}) collective-permute-start(bf16[256,2048]{1,0:T(8,128)(2,1)} %refs_6_.4), channel_id=1, source_target_pairs={{8,16},{10,18},{12,20},{14,22},{16,8},{18,10},{20,12},{22,14},{9,1... | collective-permute-start | bytes 3145736 | tf_op jit(solution)/shard_map/ppermute | solution.py:480
  10.8 3.5 %collective-permute-done.1.refs_1_.refs_2_ = bf16[256,512]{1,0:T(8,128)(2,1)S(1)} collective-permute-done((bf16[256,512]{1,0:T(8,128)(2,1)}, bf16[256,512]{1,0:T(8,128)(2,1)S(1)}, u32[]{:S(2)}, u32[]{:S(2)}) %collective-permute-start.1) | collective-permute-done | bytes 262176 | tf_op jit(solution)/shard_map/ppermute | solution.py:33
  14.3 2.0 %collective-permute-start.5 = (bf16[256,512]{1,0:T(8,128)(2,1)S(1)}, bf16[256,512]{1,0:T(8,128)(2,1)S(1)}, u32[]{:S(2)}, u32[]{:S(2)}) collective-permute-start(bf16[256,512]{1,0:T(8,128)(2,1)S(1)} %get-tuple-element.37), channel_id=1, source_target_pairs={{0,1},{1,0},{2,3},{3,2},{4,5},{5,4},{6,7},{7,6},{8,9},{9,8},{10,11... | collective-permute-start | bytes 786440 | tf_op jit(solution)/shard_map/ppermute | solution.py:38
  19.7 3.6 %collective-permute-start.3 = (bf16[256,512]{1,0:T(8,128)(2,1)S(1)}, bf16[256,512]{1,0:T(8,128)(2,1)S(1)}, u32[]{:S(2)}, u32[]{:S(2)}) collective-permute-start(bf16[256,512]{1,0:T(8,128)(2,1)S(1)} %get-tuple-element.65), channel_id=1, source_target_pairs={{0,8},{2,10},{4,12},{6,14},{8,16},{10,18},{12,20},{14,22},{16,24},... | collective-permute-start | bytes 786440 | tf_op jit(solution)/shard_map/ppermute | solution.py:491
  25.0 12.6 %collective-permute-done.3.refs_4_.refs_1_ = bf16[256,512]{1,0:T(8,128)(2,1)S(1)} collective-permute-done((bf16[256,512]{1,0:T(8,128)(2,1)S(1)}, bf16[256,512]{1,0:T(8,128)(2,1)S(1)}, u32[]{:S(2)}, u32[]{:S(2)}) %collective-permute-start.3) | collective-permute-done | bytes 262176 | tf_op jit(solution)/shard_map/ppermute | solution.py:491
  38.4 6.1 %filtered.1 = (bf16[3,512,512]{2,1,0:T(8,128)(2,1)S(1)}, bf16[1024,512]{1,0:T(8,128)(2,1)}) custom-call(bf16[256,512]{1,0:T(8,128)(2,1)S(1)} %get-tuple-element.33.refs_0_, bf16[256,512]{1,0:T(8,128)(2,1)S(1)} %collective-permute-done.refs_1_, bf16[256,512]{1,0:T(8,128)(2,1)S(1)} %collective-permute-done.1.refs_1_.refs_2_, ...), custom_call_target="tpu_custom_call" | custom-call | flops 6000000000 | bytes 6000000 | tf_op jit(solution)/shard_map/filtered/pallas_call | solution.py:228
  45.7 1.6 %collective-permute-start.8 = (bf16[1024,512]{1,0:T(8,128)(2,1)}, bf16[1024,512]{1,0:T(8,128)(2,1)S(1)}, u32[]{:S(2)}, u32[]{:S(2)}) collective-permute-start(bf16[1024,512]{1,0:T(8,128)(2,1)} %get-tuple-element.42.refs_0_), channel_id=1, source_target_pairs={{0,4},{2,6},{4,0},{6,2},{8,12},{10,14},{12,8},{14,10},{16,20},{18,... | collective-permute-start | bytes 3145736 | tf_op jit(solution)/shard_map/ppermute | solution.py:33
  58.3 3.8 %correlations.1 = (f32[256,512]{1,0:T(8,128)S(1)}, bf16[256,512]{1,0:T(8,128)(2,1)S(1)}) custom-call(bf16[256,512]{1,0:T(8,128)(2,1)S(1)} %copy-done.36, bf16[256,512]{1,0:T(8,128)(2,1)S(1)} %collective-permute-done.13.refs_1_, bf16[256,512]{1,0:T(8,128)(2,1)S(1)} %get-tuple-element.67.refs_2_, bf16[256,512]{1,0:T(8,128)(2,1)S(1)} %collective-permute-done.14.refs_3_, ...), custom_call_target="tpu_custom_call" | custom-call | flops 5000000000 | bytes 5000000 | tf_op jit(solution)/shard_map/correlations/pallas_call | solution.py:273
  63.6 7.0 %collective-permute-done.8.refs_0_ = bf16[1024,512]{1,0:T(8,128)(2,1)S(1)} collective-permute-done((bf16[1024,512]{1,0:T(8,128)(2,1)}, bf16[1024,512]{1,0:T(8,128)(2,1)S(1)}, u32[]{:S(2)}, u32[]{:S(2)}) %collective-permute-start.8) | collective-permute-done | bytes 1048608 | tf_op jit(solution)/shard_map/ppermute | solution.py:33
  70.6 9.2 %collective-permute-done.12.refs_2_.refs_4_ = bf16[256,2048]{1,0:T(8,128)(2,1)S(1)} collective-permute-done((bf16[256,2048]{1,0:T(8,128)(2,1)}, bf16[256,2048]{1,0:T(8,128)(2,1)S(1)}, u32[]{:S(2)}, u32[]{:S(2)}) %collective-permute-start.12) | collective-permute-done | bytes 1048608 | tf_op jit(solution)/shard_map/ppermute | solution.py:480
  87.4 3.8 %project.5.refs_1_ = bf16[1024,256]{1,0:T(8,128)(2,1)S(1)} custom-call(bf16[1024,512]{1,0:T(8,128)(2,1)} %get-tuple-element.42.refs_0_, bf16[1024,512]{1,0:T(8,128)(2,1)} %collective-permute-done.7.refs_1_, bf16[1024,512]{1,0:T(8,128)(2,1)S(1)} %copy-done.7, bf16[1024,512]{1,0:T(8,128)(2,1)S(1)} %collective-permute-done.15.refs_3_, ...), custom_call_target="tpu_custom_call" | custom-call | flops 3000000000 | bytes 3000000 | tf_op jit(solution)/shard_map/project/pallas_call | solution.py:346
  91.2 2.7 %collective-permute-start.16 = (bf16[1024,256]{1,0:T(8,128)(2,1)S(1)}, bf16[1024,256]{1,0:T(8,128)(2,1)}, u32[]{:S(2)}, u32[]{:S(2)}) collective-permute-start(bf16[1024,256]{1,0:T(8,128)(2,1)S(1)} %project.5.refs_1_), channel_id=1, source_target_pairs={{0,1},{1,0},{2,3},{3,2},{4,5},{5,4},{6,7},{7,6},{8,9},{9,8},{10,11... | collective-permute-start | bytes 1572872 | tf_op jit(solution)/shard_map/ppermute | solution.py:38
  93.8 14.6 %collective-permute-done.20.refs_4_ = bf16[256,2048]{1,0:T(8,128)(2,1)S(1)} collective-permute-done((bf16[256,2048]{1,0:T(8,128)(2,1)}, bf16[256,2048]{1,0:T(8,128)(2,1)S(1)}, u32[]{:S(2)}, u32[]{:S(2)}) %collective-permute-start.20) | collective-permute-done | bytes 1048608 | tf_op jit(solution)/shard_map/ppermute | solution.py:480
  108.5 4.8 %project.7 = bf16[1024,256]{1,0:T(8,128)(2,1)} custom-call(bf16[1024,512]{1,0:T(8,128)(2,1)} %get-tuple-element.42.refs_0_, bf16[1024,512]{1,0:T(8,128)(2,1)} %collective-permute-done.7.refs_1_, bf16[1024,512]{1,0:T(8,128)(2,1)S(1)} %copy-done.7, bf16[1024,512]{1,0:T(8,128)(2,1)S(1)} %collective-permute-done.15.refs_3_, ...), custom_call_target="tpu_custom_call" | custom-call | flops 3000000000 | bytes 3000000 | tf_op jit(solution)/shard_map/project/pallas_call | solution.py:346
  113.3 1.6 %collective-permute-start.21 = (bf16[1024,256]{1,0:T(8,128)(2,1)}, bf16[1024,256]{1,0:T(8,128)(2,1)S(1)}, u32[]{:S(2)}, u32[]{:S(2)}) collective-permute-start(bf16[1024,256]{1,0:T(8,128)(2,1)} %project.7), channel_id=1, source_target_pairs={{0,1},{1,0},{2,3},{3,2},{4,5},{5,4},{6,7},{7,6},{8,9},{9,8},{10,11... | collective-permute-start | bytes 1572872 | tf_op jit(solution)/shard_map/ppermute | solution.py:38
  117.2 4.9 %project.4.kept_ref = f32[1024,256]{1,0:T(8,128)S(1)} custom-call(bf16[1024,512]{1,0:T(8,128)(2,1)} %get-tuple-element.42.refs_0_, bf16[1024,512]{1,0:T(8,128)(2,1)} %collective-permute-done.7.refs_1_, bf16[1024,512]{1,0:T(8,128)(2,1)S(1)} %copy-done.8, bf16[1024,512]{1,0:T(8,128)(2,1)S(1)} %collective-permute-done.15.refs_3_, ...), custom_call_target="tpu_custom_call" | custom-call | flops 3000000000 | bytes 3000000 | tf_op jit(solution)/shard_map/project/pallas_call | solution.py:346
  122.1 3.7 %project.6.kept_ref = f32[1024,256]{1,0:T(8,128)S(1)} custom-call(bf16[1024,512]{1,0:T(8,128)(2,1)} %get-tuple-element.42.refs_0_, bf16[1024,512]{1,0:T(8,128)(2,1)} %collective-permute-done.7.refs_1_, bf16[1024,512]{1,0:T(8,128)(2,1)S(1)} %copy-done.8, bf16[1024,512]{1,0:T(8,128)(2,1)S(1)} %collective-permute-done.15.refs_3_, ...), custom_call_target="tpu_custom_call" | custom-call | flops 3000000000 | bytes 3000000 | tf_op jit(solution)/shard_map/project/pallas_call | solution.py:346
  125.9 2.0 %collective-permute-start.27 = (bf16[64,512]{1,0:T(8,128)(2,1)S(1)}, bf16[64,512]{1,0:T(8,128)(2,1)S(1)}, u32[]{:S(2)}, u32[]{:S(2)}) collective-permute-start(bf16[64,512]{1,0:T(8,128)(2,1)S(1)} %get-tuple-element.59), channel_id=1, source_target_pairs={{0,16},{2,18},{4,20},{6,22},{8,24},{10,26},{12,28},{14,30},{16,0},... | collective-permute-start | bytes 196616 | tf_op jit(solution)/shard_map/ppermute | solution.py:33
  129.1 2.1 %collective-permute-done.27.got_ref = bf16[64,512]{1,0:T(8,128)(2,1)S(1)} collective-permute-done((bf16[64,512]{1,0:T(8,128)(2,1)S(1)}, bf16[64,512]{1,0:T(8,128)(2,1)S(1)}, u32[]{:S(2)}, u32[]{:S(2)}) %collective-permute-start.27) | collective-permute-done | bytes 65568 | tf_op jit(solution)/shard_map/ppermute | solution.py:33
  139.5 1.7 %collective-permute-done.19.refs_3_ = bf16[256,256]{1,0:T(8,128)(2,1)S(1)} collective-permute-done((bf16[256,256]{1,0:T(8,128)(2,1)S(1)}, bf16[256,256]{1,0:T(8,128)(2,1)S(1)}, u32[]{:S(2)}, u32[]{:S(2)}) %collective-permute-start.19) | collective-permute-done | bytes 131104 | tf_op jit(solution)/shard_map/ppermute | solution.py:33
  141.1 3.9 %collective-permute-done.23.refs_6_ = bf16[256,256]{1,0:T(8,128)(2,1)S(1)} collective-permute-done((bf16[256,256]{1,0:T(8,128)(2,1)S(1)}, bf16[256,256]{1,0:T(8,128)(2,1)S(1)}, u32[]{:S(2)}, u32[]{:S(2)}) %collective-permute-start.23) | collective-permute-done | bytes 131104 | tf_op jit(solution)/shard_map/ppermute | solution.py:33
  145.1 1.7 %collective-permute-done.24.refs_7_ = bf16[256,256]{1,0:T(8,128)(2,1)S(1)} collective-permute-done((bf16[256,256]{1,0:T(8,128)(2,1)S(1)}, bf16[256,256]{1,0:T(8,128)(2,1)S(1)}, u32[]{:S(2)}, u32[]{:S(2)}) %collective-permute-start.24) | collective-permute-done | bytes 131104 | tf_op jit(solution)/shard_map/ppermute | solution.py:33
  (138 shorter events, 43.3 us)
Async XLA Ops:
  4.0 10.3 %collective-permute-start.1 = (bf16[256,512]{1,0:T(8,128)(2,1)}, bf16[256,512]{1,0:T(8,128)(2,1)S(1)}, u32[]{:S(2)}, u32[]{:S(2)}) collective-permute-start(bf16[256,512]{1,0:T(8,128)(2,1)} %get-tuple-element.35), channel_id=1, source_target_pairs={{0,4},{2,6},{4,0},{6,2},{8,12},{10,14},{12,8},{14,10},{16,20},{18,... | collective-permute-start | bytes 786440 | tf_op jit(solution)/shard_map/ppermute | solution.py:33
  7.0 10.9 %collective-permute-start = (bf16[256,512]{1,0:T(8,128)(2,1)}, bf16[256,512]{1,0:T(8,128)(2,1)S(1)}, u32[]{:S(2)}, u32[]{:S(2)}) collective-permute-start(bf16[256,512]{1,0:T(8,128)(2,1)} %get-tuple-element.34), channel_id=1, source_target_pairs={{0,2},{2,0},{4,6},{6,4},{8,10},{10,8},{12,14},{14,12},{16,18},{18,... | collective-permute-start | bytes 786440 | tf_op jit(solution)/shard_map/ppermute | solution.py:33
  7.0 12.6 %collective-permute-start.2 = (bf16[256,512]{1,0:T(8,128)(2,1)}, bf16[256,512]{1,0:T(8,128)(2,1)S(1)}, u32[]{:S(2)}, u32[]{:S(2)}) collective-permute-start(bf16[256,512]{1,0:T(8,128)(2,1)} %get-tuple-element.36), channel_id=1, source_target_pairs={{0,6},{2,4},{4,2},{6,0},{8,14},{10,12},{12,10},{14,8},{16,22},{18,... | collective-permute-start | bytes 786440 | tf_op jit(solution)/shard_map/ppermute | solution.py:33
  7.1 40.3 %collective-permute-start.9 = (bf16[256,2048]{1,0:T(8,128)(2,1)}, bf16[256,2048]{1,0:T(8,128)(2,1)S(1)}, u32[]{:S(2)}, u32[]{:S(2)}) collective-permute-start(bf16[256,2048]{1,0:T(8,128)(2,1)} %refs_6_.4), channel_id=1, source_target_pairs={{0,8},{2,10},{4,12},{6,14},{8,0},{10,2},{12,4},{14,6},{16,24},{18,... | collective-permute-start | bytes 3145736 | tf_op jit(solution)/shard_map/ppermute | solution.py:480
  9.2 40.0 %collective-permute-start.11 = (bf16[256,2048]{1,0:T(8,128)(2,1)}, bf16[256,2048]{1,0:T(8,128)(2,1)}, u32[]{:S(2)}, u32[]{:S(2)}) collective-permute-start(bf16[256,2048]{1,0:T(8,128)(2,1)} %refs_6_.4), channel_id=1, source_target_pairs={{8,16},{10,18},{12,20},{14,22},{16,8},{18,10},{20,12},{22,14},{9,1... | collective-permute-start | bytes 3145736 | tf_op jit(solution)/shard_map/ppermute | solution.py:480
  14.3 9.0 %collective-permute-start.5 = (bf16[256,512]{1,0:T(8,128)(2,1)S(1)}, bf16[256,512]{1,0:T(8,128)(2,1)S(1)}, u32[]{:S(2)}, u32[]{:S(2)}) collective-permute-start(bf16[256,512]{1,0:T(8,128)(2,1)S(1)} %get-tuple-element.37), channel_id=1, source_target_pairs={{0,1},{1,0},{2,3},{3,2},{4,5},{5,4},{6,7},{7,6},{8,9},{9,8},{10,11... | collective-permute-start | bytes 786440 | tf_op jit(solution)/shard_map/ppermute | solution.py:38
  17.8 20.6 %collective-permute-start.6 = (bf16[2,256,512]{2,1,0:T(8,128)(2,1)S(1)}, bf16[2,256,512]{2,1,0:T(8,128)(2,1)S(1)}, u32[]{:S(2)}, u32[]{:S(2)}) collective-permute-start(bf16[2,256,512]{2,1,0:T(8,128)(2,1)S(1)} %get-tuple-element.41), channel_id=1, source_target_pairs={{0,4},{2,6},{4,0},{6,2},{8,12},{10,14},{12,8},{14,10},{16,20},{18,... | collective-permute-start | bytes 1572872 | tf_op jit(solution)/shard_map/ppermute | solution.py:33
  19.7 17.9 %collective-permute-start.3 = (bf16[256,512]{1,0:T(8,128)(2,1)S(1)}, bf16[256,512]{1,0:T(8,128)(2,1)S(1)}, u32[]{:S(2)}, u32[]{:S(2)}) collective-permute-start(bf16[256,512]{1,0:T(8,128)(2,1)S(1)} %get-tuple-element.65), channel_id=1, source_target_pairs={{0,8},{2,10},{4,12},{6,14},{8,16},{10,18},{12,20},{14,22},{16,24},... | collective-permute-start | bytes 786440 | tf_op jit(solution)/shard_map/ppermute | solution.py:491
  23.3 15.1 %collective-permute-start.4 = (bf16[256,512]{1,0:T(8,128)(2,1)S(1)}, bf16[256,512]{1,0:T(8,128)(2,1)S(1)}, u32[]{:S(2)}, u32[]{:S(2)}) collective-permute-start(bf16[256,512]{1,0:T(8,128)(2,1)S(1)} %get-tuple-element.64), channel_id=1, source_target_pairs={{8,0},{10,2},{12,4},{14,6},{16,8},{18,10},{20,12},{22,14},{24,16},... | collective-permute-start | bytes 786440 | tf_op jit(solution)/shard_map/ppermute | solution.py:494
  45.7 24.8 %collective-permute-start.8 = (bf16[1024,512]{1,0:T(8,128)(2,1)}, bf16[1024,512]{1,0:T(8,128)(2,1)S(1)}, u32[]{:S(2)}, u32[]{:S(2)}) collective-permute-start(bf16[1024,512]{1,0:T(8,128)(2,1)} %get-tuple-element.42.refs_0_), channel_id=1, source_target_pairs={{0,4},{2,6},{4,0},{6,2},{8,12},{10,14},{12,8},{14,10},{16,20},{18,... | collective-permute-start | bytes 3145736 | tf_op jit(solution)/shard_map/ppermute | solution.py:33
  48.3 22.3 %collective-permute-start.10 = (bf16[256,2048]{1,0:T(8,128)(2,1)}, bf16[256,2048]{1,0:T(8,128)(2,1)S(1)}, u32[]{:S(2)}, u32[]{:S(2)}) collective-permute-start(bf16[256,2048]{1,0:T(8,128)(2,1)} %tie.4.refs_6_), channel_id=1, source_target_pairs={{16,8},{18,10},{20,12},{22,14},{8,16},{10,18},{12,20},{14,22},{17,... | collective-permute-start | bytes 3145736 | tf_op jit(solution)/shard_map/ppermute | solution.py:480
  49.2 30.6 %collective-permute-start.12 = (bf16[256,2048]{1,0:T(8,128)(2,1)}, bf16[256,2048]{1,0:T(8,128)(2,1)S(1)}, u32[]{:S(2)}, u32[]{:S(2)}) collective-permute-start(bf16[256,2048]{1,0:T(8,128)(2,1)} %tie.5.refs_5_), channel_id=1, source_target_pairs={{8,0},{10,2},{12,4},{14,6},{16,24},{18,26},{20,28},{22,30},{9,1},{... | collective-permute-start | bytes 3145736 | tf_op jit(solution)/shard_map/ppermute | solution.py:480
  52.2 31.5 %collective-permute-start.7 = (bf16[1024,512]{1,0:T(8,128)(2,1)}, bf16[1024,512]{1,0:T(8,128)(2,1)}, u32[]{:S(2)}, u32[]{:S(2)}) collective-permute-start(bf16[1024,512]{1,0:T(8,128)(2,1)} %get-tuple-element.42.refs_0_), channel_id=1, source_target_pairs={{0,2},{2,0},{4,6},{6,4},{8,10},{10,8},{12,14},{14,12},{16,18},{18,... | collective-permute-start | bytes 3145736 | tf_op jit(solution)/shard_map/ppermute | solution.py:33
  80.8 27.7 %collective-permute-start.20 = (bf16[256,2048]{1,0:T(8,128)(2,1)}, bf16[256,2048]{1,0:T(8,128)(2,1)S(1)}, u32[]{:S(2)}, u32[]{:S(2)}) collective-permute-start(bf16[256,2048]{1,0:T(8,128)(2,1)} %copy-done), channel_id=1, source_target_pairs={{8,0},{10,2},{12,4},{14,6},{16,24},{18,26},{20,28},{22,30},{9,1},{... | collective-permute-start | bytes 3145736 | tf_op jit(solution)/shard_map/ppermute | solution.py:480
  82.2 32.6 %collective-permute-start.25 = (bf16[256,512]{1,0:T(8,128)(2,1)S(1)}, bf16[256,512]{1,0:T(8,128)(2,1)}, u32[]{:S(2)}, u32[]{:S(2)}) collective-permute-start(bf16[256,512]{1,0:T(8,128)(2,1)S(1)} %copy-done.18), channel_id=1, source_target_pairs={{0,7},{1,6},{2,5},{3,4},{4,3},{5,2},{6,1},{7,0},{8,15},{9,14},{10,... | collective-permute-start | bytes 786440 | tf_op jit(solution)/shard_map/ppermute | solution.py:516
  91.2 36.7 %collective-permute-start.16 = (bf16[1024,256]{1,0:T(8,128)(2,1)S(1)}, bf16[1024,256]{1,0:T(8,128)(2,1)}, u32[]{:S(2)}, u32[]{:S(2)}) collective-permute-start(bf16[1024,256]{1,0:T(8,128)(2,1)S(1)} %project.5.refs_1_), channel_id=1, source_target_pairs={{0,1},{1,0},{2,3},{3,2},{4,5},{5,4},{6,7},{7,6},{8,9},{9,8},{10,11... | collective-permute-start | bytes 1572872 | tf_op jit(solution)/shard_map/ppermute | solution.py:38
  113.3 19.8 %collective-permute-start.21 = (bf16[1024,256]{1,0:T(8,128)(2,1)}, bf16[1024,256]{1,0:T(8,128)(2,1)S(1)}, u32[]{:S(2)}, u32[]{:S(2)}) collective-permute-start(bf16[1024,256]{1,0:T(8,128)(2,1)} %project.7), channel_id=1, source_target_pairs={{0,1},{1,0},{2,3},{3,2},{4,5},{5,4},{6,7},{7,6},{8,9},{9,8},{10,11... | collective-permute-start | bytes 1572872 | tf_op jit(solution)/shard_map/ppermute | solution.py:38
  117.1 8.7 %collective-permute-start.26 = (bf16[2,64,512]{2,1,0:T(8,128)(2,1)S(1)}, bf16[2,64,512]{2,1,0:T(8,128)(2,1)S(1)}, u32[]{:S(2)}, u32[]{:S(2)}) collective-permute-start(bf16[2,64,512]{2,1,0:T(8,128)(2,1)S(1)} %get-tuple-element.57), channel_id=1, source_target_pairs={{0,8},{2,10},{4,12},{6,14},{8,0},{10,2},{12,4},{14,6},{16,24},{18,... | collective-permute-start | bytes 393224 | tf_op jit(solution)/shard_map/ppermute | solution.py:33
  129.0 7.7 %collective-permute-start.17 = (bf16[256,256]{1,0:T(8,128)(2,1)S(1)}, bf16[256,256]{1,0:T(8,128)(2,1)S(1)}, u32[]{:S(2)}, u32[]{:S(2)}) collective-permute-start(bf16[256,256]{1,0:T(8,128)(2,1)S(1)} %get-tuple-element.48), channel_id=1, source_target_pairs={{0,2},{2,0},{4,6},{6,4},{8,10},{10,8},{12,14},{14,12},{16,18},{18,... | collective-permute-start | bytes 393224 | tf_op jit(solution)/shard_map/ppermute | solution.py:33
  133.2 6.3 %collective-permute-start.18 = (bf16[256,256]{1,0:T(8,128)(2,1)S(1)}, bf16[256,256]{1,0:T(8,128)(2,1)S(1)}, u32[]{:S(2)}, u32[]{:S(2)}) collective-permute-start(bf16[256,256]{1,0:T(8,128)(2,1)S(1)} %get-tuple-element.49), channel_id=1, source_target_pairs={{0,4},{2,6},{4,0},{6,2},{8,12},{10,14},{12,8},{14,10},{16,20},{18,... | collective-permute-start | bytes 393224 | tf_op jit(solution)/shard_map/ppermute | solution.py:33
  133.8 7.4 %collective-permute-start.19 = (bf16[256,256]{1,0:T(8,128)(2,1)S(1)}, bf16[256,256]{1,0:T(8,128)(2,1)S(1)}, u32[]{:S(2)}, u32[]{:S(2)}) collective-permute-start(bf16[256,256]{1,0:T(8,128)(2,1)S(1)} %get-tuple-element.50), channel_id=1, source_target_pairs={{0,6},{2,4},{4,2},{6,0},{8,14},{10,12},{12,10},{14,8},{16,22},{18,... | collective-permute-start | bytes 393224 | tf_op jit(solution)/shard_map/ppermute | solution.py:33
  135.6 5.6 %collective-permute-start.22 = (bf16[256,256]{1,0:T(8,128)(2,1)S(1)}, bf16[256,256]{1,0:T(8,128)(2,1)S(1)}, u32[]{:S(2)}, u32[]{:S(2)}) collective-permute-start(bf16[256,256]{1,0:T(8,128)(2,1)S(1)} %get-tuple-element.52), channel_id=1, source_target_pairs={{0,2},{2,0},{4,6},{6,4},{8,10},{10,8},{12,14},{14,12},{16,18},{18,... | collective-permute-start | bytes 393224 | tf_op jit(solution)/shard_map/ppermute | solution.py:33
  135.6 9.5 %collective-permute-start.23 = (bf16[256,256]{1,0:T(8,128)(2,1)S(1)}, bf16[256,256]{1,0:T(8,128)(2,1)S(1)}, u32[]{:S(2)}, u32[]{:S(2)}) collective-permute-start(bf16[256,256]{1,0:T(8,128)(2,1)S(1)} %get-tuple-element.53), channel_id=1, source_target_pairs={{0,4},{2,6},{4,0},{6,2},{8,12},{10,14},{12,8},{14,10},{16,20},{18,... | collective-permute-start | bytes 393224 | tf_op jit(solution)/shard_map/ppermute | solution.py:33
  136.7 10.0 %collective-permute-start.24 = (bf16[256,256]{1,0:T(8,128)(2,1)S(1)}, bf16[256,256]{1,0:T(8,128)(2,1)S(1)}, u32[]{:S(2)}, u32[]{:S(2)}) collective-permute-start(bf16[256,256]{1,0:T(8,128)(2,1)S(1)} %get-tuple-element.54), channel_id=1, source_target_pairs={{0,6},{2,4},{4,2},{6,0},{8,14},{10,12},{12,10},{14,8},{16,22},{18,... | collective-permute-start | bytes 393224 | tf_op jit(solution)/shard_map/ppermute | solution.py:33
  (46 other events, 228.4 us)

commit v2 on v1

--- a/solution.py
+++ b/solution.py
@@ -12,6 +12,8 @@
 F32, BF16 = jnp.float32, jnp.bfloat16
 VMEM = pl.BlockSpec(memory_space=pltpu.VMEM)
 ANY = pl.BlockSpec(memory_space=pl.ANY)
+HBM = pl.BlockSpec(memory_space=pltpu.HBM)
+TOKEN = (8, 128)
 MIB = 1 << 20
 SMALL = pl.CostEstimate(flops=1000, bytes_accessed=1000, transcendentals=0)
 
@@ -95,70 +97,51 @@
 
 
 def tie(value, *deps):
-    def kernel(*refs):
-        pass
+    def kernel(value_ref, *rest):
+        rest[-1][...] = value_ref[...]
 
     return pl.pallas_call(
         kernel,
         out_shape=shape(value.shape, value.dtype),
-        in_specs=[ANY] * (1 + len(deps)),
-        out_specs=ANY,
-        input_output_aliases={0: 0},
-        cost_estimate=SMALL,
+        in_specs=[VMEM] + [ANY] * len(deps),
+        out_specs=VMEM,
+        compiler_params=params(8),
+        cost_estimate=cost(1),
         name="tie",
     )(value, *deps)
 
 
-def quarters(value, deps=(), mirror=None):
+def quarters(value, outputs, deps=(), reverse=False):
     rows, width = value.shape
     cq = width // INNER
-    n_in = 1 + (mirror is not None)
+    total = sum(len(members) for members in outputs)
 
     def kernel(*refs):
         q = group_index()
-        outs = refs[n_in + len(deps) :]
-        for k in range(INNER):
-            outs[k][...] = refs[0][:, columns(q ^ k, cq)]
-        if mirror is not None:
-            outs[INNER][...] = refs[1][:, columns(INNER - 1 - q, cq)]
-
-    out_shape = [shape((rows, cq), value.dtype)] * INNER
-    inputs = [value]
-    if mirror is not None:
-        inputs.append(mirror)
-        out_shape.append(shape((mirror.shape[0], cq), mirror.dtype))
-    return pl.pallas_call(
-        kernel,
-        out_shape=out_shape,
-        in_specs=[VMEM] * n_in + [ANY] * len(deps),
-        out_specs=[VMEM] * len(out_shape),
-        compiler_params=params(16),
+        if reverse:
+            q = INNER - 1 - q
+        outs, sems = refs[1 + len(deps) : -1], refs[-1]
+        copies = []
+        for members, out in zip(outputs, outs):
+            for i, k in enumerate(members):
+                source = refs[0].at[:, columns(q ^ k, cq)]
+                target = out if len(members) == 1 else out.at[i]
+                copies.append(pltpu.make_async_copy(source, target, sems.at[len(copies)]))
+        for copy in copies:
+            copy.start()
+        for copy in copies:
+            copy.wait()
+
+    dims = [(rows, cq) if len(m) == 1 else (len(m), rows, cq) for m in outputs]
+    return pl.pallas_call(
+        kernel,
+        out_shape=[shape(d, value.dtype) for d in dims],
+        in_specs=[HBM] + [ANY] * len(deps),
+        out_specs=[ANY] * len(outputs),
+        scratch_shapes=[pltpu.SemaphoreType.DMA((total,))],
+        compiler_params=params(8),
         cost_estimate=cost(1),
         name="quarters",
-    )(*inputs, *deps)
-
-
-def halves_of_quarters(value, deps):
-    rows, width = value.shape
-    cq = width // INNER
-
-    def kernel(*refs):
-        q = group_index()
-        own, near, far = refs[1 + len(deps) :]
-        own[...] = refs[0][:, columns(q, cq)]
-        near[...] = refs[0][:, columns(q ^ 1, cq)]
-        far[0] = refs[0][:, columns(q ^ 2, cq)]
-        far[1] = refs[0][:, columns(q ^ 3, cq)]
-
-    dims = [(rows, cq), (rows, cq), (2, rows, cq)]
-    return pl.pallas_call(
-        kernel,
-        out_shape=[shape(d, value.dtype) for d in dims],
-        in_specs=[VMEM] + [ANY] * len(deps),
-        out_specs=[VMEM] * 3,
-        compiler_params=params(16),
-        cost_estimate=cost(1),
-        name="halves_of_quarters",
     )(value, *deps)
 
 
@@ -186,7 +169,7 @@
     return min(256, cq)
 
 
-def filtered(pieces, before, after, own_taps, mirrored, gain, const, deps):
+def filtered(pieces, before, after, own_taps, mirrored, gain, const, deps, large):
     rows, cq = pieces[0].shape
     taps = own_taps.shape[0]
     chunk = chunk_of(cq)
@@ -195,7 +178,7 @@
 
     def kernel(*refs):
         before_ref, after_ref, taps_ref, mirror_ref, gain_ref, into, back, at_taps = refs[INNER : INNER + 8]
-        spectrum, conv, ordered = refs[INNER + 8 + len(deps) :]
+        spectrum, conv, ordered = refs[INNER + 8 + len(deps) + len(large) :]
         q = group_index()
         for k in range(INNER):
             ordered[q ^ k] = refs[k][...].astype(F32)
@@ -233,13 +216,14 @@
         + [cols(taps)] * 2
         + [cols(1)]
         + [whole(const["into"]), whole(const["back"]), whole(const["taps"])]
-        + [ANY] * len(deps),
+        + [ANY] * len(deps)
+        + [HBM] * len(large),
         out_specs=[pl.BlockSpec((PAIRS, 2 * rows, chunk), lambda i: (0, 0, i)), cols(INNER * rows)],
         scratch_shapes=[pltpu.VMEM((INNER, rows, chunk), F32)],
         compiler_params=params(32),
         cost_estimate=cost(6),
         name="filtered",
-    )(*pieces, before, after, own_taps, mirrored, gain, const["into"], const["back"], const["taps"], *deps)
+    )(*pieces, before, after, own_taps, mirrored, gain, const["into"], const["back"], const["taps"], *deps, *large)
 
 
 def correlations(pieces, spectrum, const, scale, deps):
@@ -251,7 +235,8 @@
 
     def kernel(*refs):
         spec, into, lags, flip = refs[INNER : INNER + 4]
-        forward, turned, ordered = refs[INNER + 4 + len(deps) :]
+        forward, turned, token, ordered = refs[INNER + 4 + len(deps) :]
+        token[...] = jnp.zeros(TOKEN, F32)
         q = group_index()
         for k in range(INNER):
             ordered[q ^ k] = refs[k][...].astype(F32)
@@ -273,12 +258,16 @@
     return pl.pallas_call(
         kernel,
         grid=(chunks,),
-        out_shape=[shape((taps, cq), F32), shape((taps, cq), BF16)],
+        out_shape=[shape((taps, cq), F32), shape((taps, cq), BF16), shape(TOKEN, F32)],
         in_specs=[cols(rows)] * INNER
         + [pl.BlockSpec((PAIRS, 2 * rows, chunk), lambda i: (0, 0, i))]
         + [whole(const["into"]), whole(const["lags"]), pl.BlockSpec((chunk, chunk), lambda i: (0, 0))]
-        + [ANY] * len(deps),
-        out_specs=[cols(taps), pl.BlockSpec((taps, chunk), lambda i: (0, chunks - 1 - i))],
+        + [HBM] * len(deps),
+        out_specs=[
+            cols(taps),
+            pl.BlockSpec((taps, chunk), lambda i: (0, chunks - 1 - i)),
+            pl.BlockSpec(TOKEN, lambda i: (0, 0)),
+        ],
         scratch_shapes=[pltpu.VMEM((INNER, rows, chunk), F32)],
         compiler_params=params(32),
         cost_estimate=cost(5),
@@ -314,80 +303,82 @@
 
     def kernel(*refs):
         blocks = refs[INNER : INNER + len(choices)]
-        out, rhs, sem = refs[INNER + len(choices) + len(deps) :]
+        out, token, rhs, sem = refs[INNER + len(choices) + len(deps) :]
         q = group_index()
         z = lax.div(lax.axis_index("seq"), INNER)
         early = lax.axis_index("ch") == lax.div(z, 2)
-        at_end = (z == 0) | (z == 3)
+        end = (z == 0) | (z == 3)
+        late, inside = jnp.logical_not(early), jnp.logical_not(end)
         holds = {
             "early": early,
-            "late": jnp.logical_not(early),
-            "early_end": early & at_end,
-            "early_mid": early & jnp.logical_not(at_end),
-            "late_end": jnp.logical_not(early) & at_end,
-            "late_mid": jnp.logical_not(early | at_end),
+            "late": late,
+            "early_end": early & end,
+            "early_mid": early & inside,
+            "late_end": late & end,
+            "late_mid": late & inside,
         }
-
-        @pl.when(pl.program_id(0) == 0)
-        def _():
-            for (condition, _), block in zip(choices, blocks):
-                @pl.when(holds[condition])
-                def _():
-                    copy = pltpu.make_async_copy(block, rhs, sem)
-                    copy.start()
-                    copy.wait()
-
-        total = 0.0
-        for k in range(INNER):
-            total += dot_nt(refs[k][...], rhs[:, columns(q ^ k, cq)])
-        out[...] = total.astype(dtype)
-
-    rows = pl.BlockSpec((tile, cq), lambda i: (i, 0))
-    return pl.pallas_call(
-        kernel,
-        grid=(INNER,),
-        out_shape=shape((span, o_rows), dtype),
-        in_specs=[rows] * INNER + [ANY] * (len(choices) + len(deps)),
-        out_specs=pl.BlockSpec((tile, o_rows), lambda i: (i, 0)),
+        for (condition, _), block in zip(choices, blocks):
+            @pl.when(holds[condition])
+            def _():
+                copy = pltpu.make_async_copy(block, rhs, sem)
+                copy.start()
+                copy.wait()
+
+        token[...] = jnp.zeros(TOKEN, F32)
+        for t in range(INNER):
+            at = slice(t * tile, (t + 1) * tile)
+            total = 0.0
+            for k in range(INNER):
+                total += dot_nt(refs[k][at, :], rhs[:, columns(q ^ k, cq)])
+            out[at, :] = total.astype(dtype)
+
+    return pl.pallas_call(
+        kernel,
+        out_shape=[shape((span, o_rows), dtype), shape(TOKEN, F32)],
+        in_specs=[VMEM] * INNER + [HBM] * len(choices) + [ANY] * len(deps),
+        out_specs=[VMEM] * 2,
         scratch_shapes=[pltpu.VMEM((o_rows, width), BF16), pltpu.SemaphoreType.DMA],
-        compiler_params=params(24),
+        compiler_params=params(16),
         cost_estimate=cost(3),
         name="project",
     )(*conv, *[block for _, block in choices], *deps)
 
 
-def summed_rows(kept, got, dtype):
+def summed_rows(kept, received, dtype, deps=()):
+    n = len(received)
     span, width = kept.shape
     rows = span // INNER
 
-    def kernel(kept_ref, got_ref, *outs):
-        q = group_index()
+    def kernel(kept_ref, *rest):
+        q, outs = group_index(), rest[n + len(deps) :]
         for k in range(INNER):
             at = pl.ds(pl.multiple_of((q ^ k) * rows, rows), rows)
-            outs[k][...] = (kept_ref[at, :] + got_ref[at, :].astype(F32)).astype(dtype)
+            total = kept_ref[at, :]
+            for got_ref in rest[:n]:
+                total += got_ref[at, :].astype(F32)
+            outs[k][...] = total.astype(dtype)
 
     return pl.pallas_call(
         kernel,
         out_shape=[shape((rows, width), dtype)] * INNER,
-        in_specs=[VMEM] * 2,
+        in_specs=[VMEM] * (1 + n) + [ANY] * len(deps),
         out_specs=[VMEM] * INNER,
         compiler_params=params(16),
         cost_estimate=cost(1),
         name="summed_rows",
-    )(kept, got)
-
-
-def assembled(rounds, width):
-    rows, o_rows = rounds[0][0].shape
+    )(kept, *received, *deps)
+
+
+def assembled(first, second, width):
+    rows, o_rows = first[0].shape
 
     def kernel(*refs):
         q = group_index()
         z = lax.div(lax.axis_index("seq"), INNER)
-        out = refs[-1]
         for r in range(2):
             for k in range(INNER):
                 block = (lax.rem(z, 2) ^ r) * INNER + (q ^ k)
-                out[:, columns(block, o_rows)] = refs[r * INNER + k][...]
+                refs[-1][:, columns(block, o_rows)] = refs[r * INNER + k][...]
 
     return pl.pallas_call(
         kernel,
@@ -397,33 +388,28 @@
         compiler_params=params(16),
         cost_estimate=cost(1),
         name="assembled",
-    )(*rounds[0], *rounds[1])
-
-
-def halved(kept, got, bit):
-    count = kept.shape[0] // 4 if kept.ndim == 2 else kept.shape[1]
-    cq = kept.shape[-1]
-
-    def kernel(kept_ref, got_ref, keep_out, send_out):
-        own = lax.rem(lax.div(lax.div(lax.axis_index("seq"), INNER), 1 << bit), 2)
-        for side, out in ((own, keep_out), (1 - own, send_out)):
-            if bit == 0:
-                for high in range(2):
-                    at = pl.ds(pl.multiple_of((2 * high + side) * count, count), count)
-                    out[high] = (kept_ref[at, :] + got_ref[at, :].astype(F32)).astype(out.dtype)
-            else:
-                out[...] = (kept_ref[side] + got_ref[side].astype(F32)).astype(out.dtype)
-
-    dims = (2, count, cq) if bit == 0 else (count, cq)
-    return pl.pallas_call(
-        kernel,
-        out_shape=[shape(dims, F32), shape(dims, BF16)],
-        in_specs=[VMEM] * 2,
-        out_specs=[VMEM] * 2,
+    )(*first, *second)
+
+
+def lag_blocks(forward, mirrored, count, deps):
+    taps, cq = forward.shape
+    lags = taps // count
+
+    def kernel(forward_ref, mirrored_ref, *rest):
+        z = lax.div(lax.axis_index("seq"), INNER)
+        for k, out in enumerate(rest[len(deps) :]):
+            at = pl.ds(pl.multiple_of((z ^ k) * lags, lags), lags)
+            out[...] = (forward_ref[at, :] + mirrored_ref[at, :].astype(F32)).astype(out.dtype)
+
+    return pl.pallas_call(
+        kernel,
+        out_shape=[shape((lags, cq), F32)] + [shape((lags, cq), BF16)] * (count - 1),
+        in_specs=[VMEM] * 2 + [ANY] * len(deps),
+        out_specs=[VMEM] * count,
         compiler_params=params(8),
         cost_estimate=cost(1),
-        name="halved",
-    )(kept, got)
+        name="lag_blocks",
+    )(forward, mirrored, *deps)
 
 
 def side_by_side(pieces):
@@ -432,13 +418,14 @@
     def kernel(*refs):
         q = group_index()
         for k in range(INNER):
-            refs[-1][:, columns(q ^ k, cq)] = refs[k][...]
-
-    return pl.pallas_call(
-        kernel,
-        out_shape=shape((rows, INNER * cq), pieces[0].dtype),
+            refs[INNER][:, columns(q ^ k, cq)] = refs[k][...]
+        refs[-1][...] = jnp.zeros(TOKEN, F32)
+
+    return pl.pallas_call(
+        kernel,
+        out_shape=[shape((rows, INNER * cq), pieces[0].dtype), shape(TOKEN, F32)],
         in_specs=[VMEM] * INNER,
-        out_specs=VMEM,
+        out_specs=[VMEM] * 2,
         compiler_params=params(8),
         cost_estimate=cost(1),
         name="side_by_side",
@@ -483,34 +470,30 @@
         near = shift(projection, [(0, 1), (1, 0), (2, 3), (3, 2)])
         mid = shift(projection, [(1, 2), (2, 1)])
 
-    *pieces, mirror_piece = quarters(grad_out, (), filter_taps)
-    grads = spread(pieces)
-    mirrored = mirror_ch(mirror_piece)
+    singles = [(k,) for k in range(INNER)]
+    grads = spread(quarters(grad_out, singles))
+    mirrored = mirror_ch(quarters(filter_taps, [(0,)], reverse=True)[0])
     quarter = own_quarter(filter_taps, mirrored, skip_gain.reshape(1, width))
 
-    before = lax.ppermute(
-        pick_member(grads, q, INNER - 1), "seq", [(i, i + INNER) for i in range(n_seq - INNER)]
-    )
-    after = lax.ppermute(
-        pick_member(grads, q, 0), "seq", [(i + INNER, i) for i in range(n_seq - INNER)]
-    )
-    input_own, input_near, input_far = halves_of_quarters(saved_in, (grads[2],))
+    final, initial = pick_member(grads, q, INNER - 1), pick_member(grads, q, 0)
+    before = lax.ppermute(final, "seq", [(i, i + INNER) for i in range(n_seq - INNER)])
+    after = lax.ppermute(initial, "seq", [(i + INNER, i) for i in range(n_seq - INNER)])
+    near_ones = ()
+    if special:
+        near_ones = (near, mid)
+        far_ends = shift(mid, [(1, 0), (2, 3)])
+        far_mid = shift(near, [(2, 1), (1, 2)])
+        last = shift(far_mid, [(1, 0), (2, 3)])
+    input_own, input_near, input_far = quarters(saved_in, [(0,), (1,), (2, 3)], (grads[2],))
     input_far = swap_seq(input_far, 2)
     inputs = [input_own, swap_seq(input_near, 1), input_far[0], swap_seq(input_far[1], 1)]
-    spectrum, conv = filtered(grads, before, after, *quarter, const, (input_far,))
-    if special:
-        near = tie(near, before, after)
-        mid = tie(mid, before, after)
-        far_ends = shift(mid, [(1, 0), (2, 3)])
-        far_mid = shift(near, [(2, 1), (1, 2)])
+    spectrum, conv = filtered(grads, before, after, *quarter, const, (input_far,), near_ones)
 
     conv2 = swap_seq(conv, 2)
     conv1 = swap_seq(conv, 1)
     scale = 2.0 / window / math.sqrt(rows * n_seq)
-    forward, turned = correlations(inputs, spectrum, const, scale, ())
-    if special:
-        conv2 = tie(conv2, far_mid, far_ends, turned)
-    conv3 = swap_seq(conv2, 1)
+    forward, turned, token = correlations(inputs, spectrum, const, scale, ())
+    conv3 = swap_seq(tie(conv2, token), 1)
     conv_parts = [conv, conv1, conv2, conv3]
 
     mirrored = lax.ppermute(
@@ -523,32 +506,30 @@
         ],
     )
     if special:
-        last = shift(far_mid, [(1, 0), (2, 3)])
         x2 = [("end", far_ends), ("mid", far_mid)]
         x3 = [("end", last), ("mid", mid)]
         sent = lambda late, soon: [("early_" + w, block) for w, block in late] + [("late", soon)]
         kept = lambda late, soon: [("late_" + w, block) for w, block in late] + [("early", soon)]
-        first = project(conv_parts, sent(x2, projection), BF16)
+        first, token = project(conv_parts, sent(x2, projection), BF16, (token,))
         got = mirror_ch(first)
-        forward = tie(forward, first)
-        lag_kept, lag_sent = halved(forward, mirrored, 0)
-        second = project(conv_parts, sent(x3, near), BF16)
+        own, token = project(conv_parts, kept(x2, projection), F32, (token,))
+        second, token = project(conv_parts, sent(x3, near), BF16, (token,))
         got2 = mirror_ch(second)
-        own = project(conv_parts, kept(x2, projection), F32)
-        own2 = project(conv_parts, kept(x3, near), F32)
-        lag_kept, lag_sent = halved(lag_kept, swap_seq(lag_sent, INNER), 1)
-        lag_pieces = summed_rows(lag_kept, swap_seq(lag_sent, 2 * INNER), F32)
-        rounds = [spread(summed_rows(own, got, BF16)), spread(summed_rows(own2, got2, BF16))]
-        grad_in = assembled(rounds, width)
+        lag_own, *lag_sent = lag_blocks(forward, mirrored, outer, (token,))
+        lag_got = [swap_seq(block, INNER * (k + 1)) for k, block in enumerate(lag_sent)]
+        moved = spread(summed_rows(own, [got], BF16, (token,)))
+        own2, token = project(conv_parts, kept(x3, near), F32, (token,))
+        lag_pieces = summed_rows(lag_own, lag_got, F32)
+        filter_grad, filter_token = side_by_side(spread(lag_pieces))
+        moved2 = spread(summed_rows(own2, [got2], BF16, tuple(moved)))
+        grad_in = assembled(moved, moved2, width)
     else:
         groups = [[INNER * a + i for a in range(outer)] for i in range(INNER)]
-        proj_all = lax.all_gather(
-            projection, "seq", axis=0, tiled=True, axis_index_groups=groups
-        )
+        proj_all = lax.all_gather(projection, "seq", axis=0, axis_index_groups=groups)
         conv_all = placed_by_source(conv_parts, q)
         partial_value = lax.dot_general(
             conv_all.transpose(1, 0, 2).reshape(span, width),
-            proj_all,
+            proj_all.reshape(-1, width),
             (((1,), (1,)), ((), ())),
             preferred_element_type=F32,
         )
@@ -560,12 +541,11 @@
         stacked = placed_by_source(moved, q).reshape(INNER, rows, -1, o_rows)
         grad_in = stacked.transpose(1, 2, 0, 3).reshape(rows, width)
 
-        groups = [[INNER * a + i for a in range(outer)] for i in range(INNER)]
         summed = lax.psum_scatter(
             forward + mirrored.astype(F32), "seq", scatter_dimension=0, tiled=True, axis_index_groups=groups
         )
         lag_pieces = by_member(summed.reshape(INNER, -1, cq), q)
-    filter_grad = side_by_side(spread(lag_pieces))
+        filter_grad, _ = side_by_side(spread(lag_pieces))
     return (grad_in, filter_grad)
 
 

time: 149 us -> 128 us (0.86)
  local copies, waits for them, and re-layouts: 19.4 us -> 1.31 us
  Pallas kernels: 32.4 us -> 18.8 us
  waiting for transfers between devices: 60.3 us -> 68.5 us
  starting transfers between devices: 34.6 us -> 37.9 us
    unnamed x78 -> x22, local copies, waits for them, and re-layouts: 18.3 us -> 1.28 us
    ppermute x20 -> x21, waiting for transfers between devices: 23.1 us -> 35.4 us  [swap_seq(): return lax.ppermute(value, 'seq', [(i, i ^ k) for i in range(count)])]
    pallas_call x9, Pallas kernels: 19.9 us -> 7.69 us  [the longest x4 5.94 us: project(): pl.pallas_call(kernel, out_shape=[shape((span, o_rows), dtype), shape(TOK...]
    ppermute x2, waiting for transfers between devices: 13.4 us -> 9.34 us  [the longest x1 4.78 us: body(): lax.ppermute(final, 'seq', [(i, i + INNER) for i in range(n_seq - INNER)])]
    ppermute x20 -> x21, starting transfers between devices: 14.6 us -> 17.1 us  [swap_seq(): return lax.ppermute(value, 'seq', [(i, i ^ k) for i in range(count)])]
    ppermute x2, starting transfers between devices: 4.92 us -> 6.73 us  [the longest x1 5.44 us: body(): lax.ppermute(final, 'seq', [(i, i + INNER) for i in range(n_seq - INNER)])]
    ppermute x3, starting transfers between devices: 6.28 us -> 4.6 us  [mirror_ch(): return lax.ppermute(value, 'ch', [(i, count - 1 - i) for i in range(count)])]
  transfers between devices with their start and end apart: 31 -> 32, of which waited for: 14 -> 12; matrix products, arithmetic and copies ran while one was open for 1% -> 0% of each run, Pallas kernels for 21% -> 10%
where the time goes in v2:
time: 128 us
  waiting for transfers between devices  68.5 us (54%)
  starting transfers between devices  37.9 us (30%)
  Pallas kernels  18.8 us (15%)
  local copies, waits for them, and re-layouts  1.31 us (1%)
    ppermute x21, waiting for transfers between devices, swap_seq(): return lax.ppermute(value, 'seq', [(i, i ^ k) for i in range(count)])  35.4 us
    ppermute x5, waiting for transfers between devices, body(): lax.ppermute(v, 'seq', [(INNER * a + i, INNER * b + i) for a, b in table...  23.5 us
    ppermute x21, starting transfers between devices, swap_seq(): return lax.ppermute(value, 'seq', [(i, i ^ k) for i in range(count)])  17.1 us
    ppermute x5, starting transfers between devices, body(): lax.ppermute(v, 'seq', [(INNER * a + i, INNER * b + i) for a, b in table...  8.21 us
    pallas_call x4, Pallas kernels, project(): pl.pallas_call(kernel, out_shape=[shape((span, o_rows), dtype), shape(TOK...  5.94 us
    pallas_call x1, Pallas kernels, filtered(): pl.pallas_call(kernel, grid=(cq // chunk,), out_shape=[shape((PAIRS, 2 *...  5.5 us
    ppermute x1, starting transfers between devices, body(): lax.ppermute(final, 'seq', [(i, i + INNER) for i in range(n_seq - INNER)])  5.44 us
    ppermute x1, waiting for transfers between devices, body(): lax.ppermute(final, 'seq', [(i, i + INNER) for i in range(n_seq - INNER)])  4.78 us
  transfers between devices with their start and end apart: 32, of which 12 were waited for; matrix products, arithmetic and copies ran while one was open for 0% of the time, Pallas kernels for 10%

profile of v2, /device:TPU:0, one launch (start us, length us, event | category | flops | bytes accessed | tf_op | source)
XLA Modules:
  0.0 127.6 jit_solution(10723156032800395264)
XLA Ops:
  0.6 3.1 %collective-permute-start.7 = (bf16[256,2048]{1,0:T(8,128)(2,1)}, bf16[256,2048]{1,0:T(8,128)(2,1)S(1)}, u32[]{:S(2)}, u32[]{:S(2)}) collective-permute-start(bf16[256,2048]{1,0:T(8,128)(2,1)} %refs_6_.4), channel_id=1, source_target_pairs={{0,8},{2,10},{4,12},{6,14},{8,0},{10,2},{12,4},{14,6},{16,24},{18,... | collective-permute-start | bytes 3145736 | tf_op jit(solution)/shard_map/ppermute | solution.py:467
  3.7 1.7 %collective-permute-start.8 = (bf16[256,2048]{1,0:T(8,128)(2,1)}, bf16[256,2048]{1,0:T(8,128)(2,1)}, u32[]{:S(2)}, u32[]{:S(2)}) collective-permute-start(bf16[256,2048]{1,0:T(8,128)(2,1)} %refs_6_.4), channel_id=1, source_target_pairs={{8,16},{10,18},{12,20},{14,22},{16,8},{18,10},{20,12},{22,14},{9,1... | collective-permute-start | bytes 3145736 | tf_op jit(solution)/shard_map/ppermute | solution.py:467
  7.5 1.6 %collective-permute-start.1 = (bf16[256,512]{1,0:T(8,128)(2,1)}, bf16[256,512]{1,0:T(8,128)(2,1)S(1)}, u32[]{:S(2)}, u32[]{:S(2)}) collective-permute-start(bf16[256,512]{1,0:T(8,128)(2,1)} %get-tuple-element.43), channel_id=1, source_target_pairs={{0,4},{2,6},{4,0},{6,2},{8,12},{10,14},{12,8},{14,10},{16,20},{18,... | collective-permute-start | bytes 786440 | tf_op jit(solution)/shard_map/ppermute | solution.py:35
  9.8 7.3 %collective-permute-done.1.refs_1_.refs_2_ = bf16[256,512]{1,0:T(8,128)(2,1)S(1)} collective-permute-done((bf16[256,512]{1,0:T(8,128)(2,1)}, bf16[256,512]{1,0:T(8,128)(2,1)S(1)}, u32[]{:S(2)}, u32[]{:S(2)}) %collective-permute-start.1) | collective-permute-done | bytes 262176 | tf_op jit(solution)/shard_map/ppermute | solution.py:35
  17.0 1.5 %collective-permute-start.5 = (bf16[256,512]{1,0:T(8,128)(2,1)S(1)}, bf16[256,512]{1,0:T(8,128)(2,1)S(1)}, u32[]{:S(2)}, u32[]{:S(2)}) collective-permute-start(bf16[256,512]{1,0:T(8,128)(2,1)S(1)} %quarters.4), channel_id=1, source_target_pairs={{0,1},{1,0},{2,3},{3,2},{4,5},{5,4},{6,7},{7,6},{8,9},{9,8},{10,11... | collective-permute-start | bytes 786440 | tf_op jit(solution)/shard_map/ppermute | solution.py:40
  18.7 1.6 %collective-permute-start.6 = (bf16[2,256,512]{2,1,0:T(8,128)(2,1)S(1)}, bf16[2,256,512]{2,1,0:T(8,128)(2,1)S(1)}, u32[]{:S(2)}, u32[]{:S(2)}) collective-permute-start(bf16[2,256,512]{2,1,0:T(8,128)(2,1)S(1)} %get-tuple-element.48), channel_id=1, source_target_pairs={{0,4},{2,6},{4,0},{6,2},{8,12},{10,14},{12,8},{14,10},{16,20},{18,... | collective-permute-start | bytes 1572872 | tf_op jit(solution)/shard_map/ppermute | solution.py:35
  21.7 5.4 %collective-permute-start.3 = (bf16[256,512]{1,0:T(8,128)(2,1)S(1)}, bf16[256,512]{1,0:T(8,128)(2,1)S(1)}, u32[]{:S(2)}, u32[]{:S(2)}) collective-permute-start(bf16[256,512]{1,0:T(8,128)(2,1)S(1)} %get-tuple-element.81), channel_id=1, source_target_pairs={{0,8},{2,10},{4,12},{6,14},{8,16},{10,18},{12,20},{14,22},{16,24},... | collective-permute-start | bytes 786440 | tf_op jit(solution)/shard_map/ppermute | solution.py:479
  28.9 4.8 %collective-permute-done.3.refs_4_ = bf16[256,512]{1,0:T(8,128)(2,1)S(1)} collective-permute-done((bf16[256,512]{1,0:T(8,128)(2,1)S(1)}, bf16[256,512]{1,0:T(8,128)(2,1)S(1)}, u32[]{:S(2)}, u32[]{:S(2)}) %collective-permute-start.3) | collective-permute-done | bytes 262176 | tf_op jit(solution)/shard_map/ppermute | solution.py:479
  33.6 4.6 %collective-permute-done.4.refs_5_ = bf16[256,512]{1,0:T(8,128)(2,1)S(1)} collective-permute-done((bf16[256,512]{1,0:T(8,128)(2,1)S(1)}, bf16[256,512]{1,0:T(8,128)(2,1)S(1)}, u32[]{:S(2)}, u32[]{:S(2)}) %collective-permute-start.4) | collective-permute-done | bytes 262176 | tf_op jit(solution)/shard_map/ppermute | solution.py:480
  38.3 5.5 %filtered.1 = (bf16[3,512,512]{2,1,0:T(8,128)(2,1)S(1)}, bf16[1024,512]{1,0:T(8,128)(2,1)S(1)}) custom-call(bf16[256,512]{1,0:T(8,128)(2,1)S(1)} %get-tuple-element.41.refs_0_, bf16[256,512]{1,0:T(8,128)(2,1)S(1)} %collective-permute-done.refs_1_, bf16[256,512]{1,0:T(8,128)(2,1)S(1)} %collective-permute-done.1.refs_1_.refs_2_, ...), custom_call_target="tpu_custom_call" | custom-call | flops 6000000000 | bytes 6000000 | tf_op jit(solution)/shard_map/filtered/pallas_call | solution.py:211
  46.7 3.9 %correlations.1 = (f32[256,512]{1,0:T(8,128)S(1)}, bf16[256,512]{1,0:T(8,128)(2,1)S(1)}, f32[8,128]{1,0:T(8,128)S(1)}) custom-call(bf16[256,512]{1,0:T(8,128)(2,1)S(1)} %get-tuple-element.50.refs_0_, bf16[256,512]{1,0:T(8,128)(2,1)S(1)} %collective-permute-done.11.refs_1_, bf16[256,512]{1,0:T(8,128)(2,1)S(1)} %get-tuple-element.83.refs_2_, ...), custom_call_target="tpu_custom_call" | custom-call | flops 5000000000 | bytes 5000000 | tf_op jit(solution)/shard_map/correlations/pallas_call | solution.py:258
  50.6 18.4 %collective-permute-done.10.value_ref.refs_2_ = bf16[1024,512]{1,0:T(8,128)(2,1)S(1)} collective-permute-done((bf16[1024,512]{1,0:T(8,128)(2,1)S(1)}, bf16[1024,512]{1,0:T(8,128)(2,1)S(1)}, u32[]{:S(2)}, u32[]{:S(2)}) %collective-permute-start.10) | collective-permute-done | bytes 1048608 | tf_op jit(solution)/shard_map/ppermute | solution.py:35
  73.6 1.6 %collective-permute-start.16 = (bf16[1024,256]{1,0:T(8,128)(2,1)S(1)}, bf16[1024,256]{1,0:T(8,128)(2,1)S(1)}, u32[]{:S(2)}, u32[]{:S(2)}) collective-permute-start(bf16[1024,256]{1,0:T(8,128)(2,1)S(1)} %get-tuple-element.56), channel_id=1, source_target_pairs={{0,1},{1,0},{2,3},{3,2},{4,5},{5,4},{6,7},{7,6},{8,9},{9,8},{10,11... | collective-permute-start | bytes 1572872 | tf_op jit(solution)/shard_map/ppermute | solution.py:40
  76.6 23.1 %collective-permute-done.17.refs_4_ = bf16[256,2048]{1,0:T(8,128)(2,1)S(1)} collective-permute-done((bf16[256,2048]{1,0:T(8,128)(2,1)S(1)}, bf16[256,2048]{1,0:T(8,128)(2,1)S(1)}, u32[]{:S(2)}, u32[]{:S(2)}) %collective-permute-start.17) | collective-permute-done | bytes 1048608 | tf_op jit(solution)/shard_map/ppermute | solution.py:467
  101.1 1.6 %collective-permute-start.21 = (bf16[1024,256]{1,0:T(8,128)(2,1)S(1)}, bf16[1024,256]{1,0:T(8,128)(2,1)S(1)}, u32[]{:S(2)}, u32[]{:S(2)}) collective-permute-start(bf16[1024,256]{1,0:T(8,128)(2,1)S(1)} %get-tuple-element.64), channel_id=1, source_target_pairs={{0,1},{1,0},{2,3},{3,2},{4,5},{5,4},{6,7},{7,6},{8,9},{9,8},{10,11... | collective-permute-start | bytes 1572872 | tf_op jit(solution)/shard_map/ppermute | solution.py:40
  102.7 2.1 %collective-permute-start.27 = (bf16[64,512]{1,0:T(8,128)(2,1)S(1)}, bf16[64,512]{1,0:T(8,128)(2,1)S(1)}, u32[]{:S(2)}, u32[]{:S(2)}) collective-permute-start(bf16[64,512]{1,0:T(8,128)(2,1)S(1)} %get-tuple-element.73), channel_id=1, source_target_pairs={{0,16},{2,18},{4,20},{6,22},{8,24},{10,26},{12,28},{14,30},{16,0},... | collective-permute-start | bytes 196616 | tf_op jit(solution)/shard_map/ppermute | solution.py:35
  104.8 2.3 %collective-permute-start.28 = (bf16[64,512]{1,0:T(8,128)(2,1)S(1)}, bf16[64,512]{1,0:T(8,128)(2,1)S(1)}, u32[]{:S(2)}, u32[]{:S(2)}) collective-permute-start(bf16[64,512]{1,0:T(8,128)(2,1)S(1)} %get-tuple-element.74), channel_id=1, source_target_pairs={{0,24},{2,26},{4,28},{6,30},{8,16},{10,18},{12,20},{14,22},{16,8},... | collective-permute-start | bytes 196616 | tf_op jit(solution)/shard_map/ppermute | solution.py:35
  107.3 2.0 %collective-permute-start.19 = (bf16[256,256]{1,0:T(8,128)(2,1)S(1)}, bf16[256,256]{1,0:T(8,128)(2,1)S(1)}, u32[]{:S(2)}, u32[]{:S(2)}) collective-permute-start(bf16[256,256]{1,0:T(8,128)(2,1)S(1)} %get-tuple-element.61), channel_id=1, source_target_pairs={{0,4},{2,6},{4,0},{6,2},{8,12},{10,14},{12,8},{14,10},{16,20},{18,... | collective-permute-start | bytes 393224 | tf_op jit(solution)/shard_map/ppermute | solution.py:35
  109.4 1.8 %project.7 = (f32[1024,256]{1,0:T(8,128)S(1)}, f32[8,128]{1,0:T(8,128)}) custom-call(bf16[1024,512]{1,0:T(8,128)(2,1)S(1)} %get-tuple-element.49.refs_0_, bf16[1024,512]{1,0:T(8,128)(2,1)S(1)} %collective-permute-done.9.refs_1_, bf16[1024,512]{1,0:T(8,128)(2,1)S(1)} %collective-permute-done.10.value_ref.refs_2_, ...), custom_call_target="tpu_custom_call" | custom-call | flops 3000000000 | bytes 3000000 | tf_op jit(solution)/shard_map/project/pallas_call | solution.py:335
  111.3 2.1 %collective-permute-start.29 = (f32[16,512]{1,0:T(8,128)S(1)}, f32[16,512]{1,0:T(8,128)S(1)}, u32[]{:S(2)}, u32[]{:S(2)}) collective-permute-start(f32[16,512]{1,0:T(8,128)S(1)} %get-tuple-element.76), channel_id=1, source_target_pairs={{0,2},{2,0},{4,6},{6,4},{8,10},{10,8},{12,14},{14,12},{16,18},{18,... | collective-permute-start | bytes 98312 | tf_op jit(solution)/shard_map/ppermute | solution.py:35
  113.7 2.1 %collective-permute-done.20.rest_4_.refs_3_ = bf16[256,256]{1,0:T(8,128)(2,1)S(1)} collective-permute-done((bf16[256,256]{1,0:T(8,128)(2,1)S(1)}, bf16[256,256]{1,0:T(8,128)(2,1)S(1)}, u32[]{:S(2)}, u32[]{:S(2)}) %collective-permute-start.20) | collective-permute-done | bytes 131104 | tf_op jit(solution)/shard_map/ppermute | solution.py:35
  116.2 1.8 %collective-permute-start.23 = (bf16[256,256]{1,0:T(8,128)(2,1)S(1)}, bf16[256,256]{1,0:T(8,128)(2,1)S(1)}, u32[]{:S(2)}, u32[]{:S(2)}) collective-permute-start(bf16[256,256]{1,0:T(8,128)(2,1)S(1)} %get-tuple-element.67), channel_id=1, source_target_pairs={{0,4},{2,6},{4,0},{6,2},{8,12},{10,14},{12,8},{14,10},{16,20},{18,... | collective-permute-start | bytes 393224 | tf_op jit(solution)/shard_map/ppermute | solution.py:35
  118.0 1.6 %collective-permute-start.30 = (f32[16,512]{1,0:T(8,128)S(1)}, f32[16,512]{1,0:T(8,128)S(1)}, u32[]{:S(2)}, u32[]{:S(2)}) collective-permute-start(f32[16,512]{1,0:T(8,128)S(1)} %get-tuple-element.77), channel_id=1, source_target_pairs={{0,4},{2,6},{4,0},{6,2},{8,12},{10,14},{12,8},{14,10},{16,20},{18,... | collective-permute-start | bytes 98312 | tf_op jit(solution)/shard_map/ppermute | solution.py:35
  119.8 6.0 %collective-permute-done.30.refs_2_ = f32[16,512]{1,0:T(8,128)S(1)} collective-permute-done((f32[16,512]{1,0:T(8,128)S(1)}, f32[16,512]{1,0:T(8,128)S(1)}, u32[]{:S(2)}, u32[]{:S(2)}) %collective-permute-start.30) | collective-permute-done | bytes 32800 | tf_op jit(solution)/shard_map/ppermute | solution.py:35
  (81 shorter events, 19.4 us)
Async XLA Ops:
  0.6 37.6 %collective-permute-start.7 = (bf16[256,2048]{1,0:T(8,128)(2,1)}, bf16[256,2048]{1,0:T(8,128)(2,1)S(1)}, u32[]{:S(2)}, u32[]{:S(2)}) collective-permute-start(bf16[256,2048]{1,0:T(8,128)(2,1)} %refs_6_.4), channel_id=1, source_target_pairs={{0,8},{2,10},{4,12},{6,14},{8,0},{10,2},{12,4},{14,6},{16,24},{18,... | collective-permute-start | bytes 3145736 | tf_op jit(solution)/shard_map/ppermute | solution.py:467
  3.7 34.5 %collective-permute-start.8 = (bf16[256,2048]{1,0:T(8,128)(2,1)}, bf16[256,2048]{1,0:T(8,128)(2,1)}, u32[]{:S(2)}, u32[]{:S(2)}) collective-permute-start(bf16[256,2048]{1,0:T(8,128)(2,1)} %refs_6_.4), channel_id=1, source_target_pairs={{8,16},{10,18},{12,20},{14,22},{16,8},{18,10},{20,12},{22,14},{9,1... | collective-permute-start | bytes 3145736 | tf_op jit(solution)/shard_map/ppermute | solution.py:467
  7.5 9.5 %collective-permute-start.1 = (bf16[256,512]{1,0:T(8,128)(2,1)}, bf16[256,512]{1,0:T(8,128)(2,1)S(1)}, u32[]{:S(2)}, u32[]{:S(2)}) collective-permute-start(bf16[256,512]{1,0:T(8,128)(2,1)} %get-tuple-element.43), channel_id=1, source_target_pairs={{0,4},{2,6},{4,0},{6,2},{8,12},{10,14},{12,8},{14,10},{16,20},{18,... | collective-permute-start | bytes 786440 | tf_op jit(solution)/shard_map/ppermute | solution.py:35
  9.1 9.6 %collective-permute-start = (bf16[256,512]{1,0:T(8,128)(2,1)}, bf16[256,512]{1,0:T(8,128)(2,1)S(1)}, u32[]{:S(2)}, u32[]{:S(2)}) collective-permute-start(bf16[256,512]{1,0:T(8,128)(2,1)} %get-tuple-element.42), channel_id=1, source_target_pairs={{0,2},{2,0},{4,6},{6,4},{8,10},{10,8},{12,14},{14,12},{16,18},{18,... | collective-permute-start | bytes 786440 | tf_op jit(solution)/shard_map/ppermute | solution.py:35
  9.1 12.6 %collective-permute-start.2 = (bf16[256,512]{1,0:T(8,128)(2,1)S(1)}, bf16[256,512]{1,0:T(8,128)(2,1)S(1)}, u32[]{:S(2)}, u32[]{:S(2)}) collective-permute-start(bf16[256,512]{1,0:T(8,128)(2,1)S(1)} %get-tuple-element.44), channel_id=1, source_target_pairs={{0,6},{2,4},{4,2},{6,0},{8,14},{10,12},{12,10},{14,8},{16,22},{18,... | collective-permute-start | bytes 786440 | tf_op jit(solution)/shard_map/ppermute | solution.py:35
  17.0 10.2 %collective-permute-start.5 = (bf16[256,512]{1,0:T(8,128)(2,1)S(1)}, bf16[256,512]{1,0:T(8,128)(2,1)S(1)}, u32[]{:S(2)}, u32[]{:S(2)}) collective-permute-start(bf16[256,512]{1,0:T(8,128)(2,1)S(1)} %quarters.4), channel_id=1, source_target_pairs={{0,1},{1,0},{2,3},{3,2},{4,5},{5,4},{6,7},{7,6},{8,9},{9,8},{10,11... | collective-permute-start | bytes 786440 | tf_op jit(solution)/shard_map/ppermute | solution.py:40
  18.7 19.5 %collective-permute-start.6 = (bf16[2,256,512]{2,1,0:T(8,128)(2,1)S(1)}, bf16[2,256,512]{2,1,0:T(8,128)(2,1)S(1)}, u32[]{:S(2)}, u32[]{:S(2)}) collective-permute-start(bf16[2,256,512]{2,1,0:T(8,128)(2,1)S(1)} %get-tuple-element.48), channel_id=1, source_target_pairs={{0,4},{2,6},{4,0},{6,2},{8,12},{10,14},{12,8},{14,10},{16,20},{18,... | collective-permute-start | bytes 1572872 | tf_op jit(solution)/shard_map/ppermute | solution.py:35
  21.7 11.9 %collective-permute-start.3 = (bf16[256,512]{1,0:T(8,128)(2,1)S(1)}, bf16[256,512]{1,0:T(8,128)(2,1)S(1)}, u32[]{:S(2)}, u32[]{:S(2)}) collective-permute-start(bf16[256,512]{1,0:T(8,128)(2,1)S(1)} %get-tuple-element.81), channel_id=1, source_target_pairs={{0,8},{2,10},{4,12},{6,14},{8,16},{10,18},{12,20},{14,22},{16,24},... | collective-permute-start | bytes 786440 | tf_op jit(solution)/shard_map/ppermute | solution.py:479
  27.2 11.0 %collective-permute-start.4 = (bf16[256,512]{1,0:T(8,128)(2,1)S(1)}, bf16[256,512]{1,0:T(8,128)(2,1)S(1)}, u32[]{:S(2)}, u32[]{:S(2)}) collective-permute-start(bf16[256,512]{1,0:T(8,128)(2,1)S(1)} %get-tuple-element.80), channel_id=1, source_target_pairs={{8,0},{10,2},{12,4},{14,6},{16,8},{18,10},{20,12},{22,14},{24,16},... | collective-permute-start | bytes 786440 | tf_op jit(solution)/shard_map/ppermute | solution.py:480
  43.8 25.2 %collective-permute-start.10 = (bf16[1024,512]{1,0:T(8,128)(2,1)S(1)}, bf16[1024,512]{1,0:T(8,128)(2,1)S(1)}, u32[]{:S(2)}, u32[]{:S(2)}) collective-permute-start(bf16[1024,512]{1,0:T(8,128)(2,1)S(1)} %get-tuple-element.49.refs_0_), channel_id=1, source_target_pairs={{0,4},{2,6},{4,0},{6,2},{8,12},{10,14},{12,8},{14,10},{16,20},{18,... | collective-permute-start | bytes 3145736 | tf_op jit(solution)/shard_map/ppermute | solution.py:35
  44.5 27.3 %collective-permute-start.9 = (bf16[1024,512]{1,0:T(8,128)(2,1)S(1)}, bf16[1024,512]{1,0:T(8,128)(2,1)S(1)}, u32[]{:S(2)}, u32[]{:S(2)}) collective-permute-start(bf16[1024,512]{1,0:T(8,128)(2,1)S(1)} %get-tuple-element.49.refs_0_), channel_id=1, source_target_pairs={{0,2},{2,0},{4,6},{6,4},{8,10},{10,8},{12,14},{14,12},{16,18},{18,... | collective-permute-start | bytes 3145736 | tf_op jit(solution)/shard_map/ppermute | solution.py:35
  44.6 27.6 %collective-permute-start.14 = (bf16[256,2048]{1,0:T(8,128)(2,1)}, bf16[256,2048]{1,0:T(8,128)(2,1)S(1)}, u32[]{:S(2)}, u32[]{:S(2)}) collective-permute-start(bf16[256,2048]{1,0:T(8,128)(2,1)} %collective-permute-done.8.refs_14_.refs_5_), channel_id=1, source_target_pairs={{8,0},{10,2},{12,4},{14,6},{16,24},{18,26},{20,28},{22,30},{9,1},{... | collective-permute-start | bytes 3145736 | tf_op jit(solution)/shard_map/ppermute | solution.py:467
  45.9 23.2 %collective-permute-start.15 = (bf16[256,2048]{1,0:T(8,128)(2,1)S(1)}, bf16[256,2048]{1,0:T(8,128)(2,1)S(1)}, u32[]{:S(2)}, u32[]{:S(2)}) collective-permute-start(bf16[256,2048]{1,0:T(8,128)(2,1)S(1)} %collective-permute-done.7.refs_13_.refs_6_), channel_id=1, source_target_pairs={{16,8},{18,10},{20,12},{22,14},{8,16},{10,18},{12,20},{14,22},{17,... | collective-permute-start | bytes 3145736 | tf_op jit(solution)/shard_map/ppermute | solution.py:467
  69.1 30.6 %collective-permute-start.17 = (bf16[256,2048]{1,0:T(8,128)(2,1)S(1)}, bf16[256,2048]{1,0:T(8,128)(2,1)S(1)}, u32[]{:S(2)}, u32[]{:S(2)}) collective-permute-start(bf16[256,2048]{1,0:T(8,128)(2,1)S(1)} %collective-permute-done.15.refs_5_), channel_id=1, source_target_pairs={{8,0},{10,2},{12,4},{14,6},{16,24},{18,26},{20,28},{22,30},{9,1},{... | collective-permute-start | bytes 3145736 | tf_op jit(solution)/shard_map/ppermute | solution.py:467
  70.5 32.1 %collective-permute-start.25 = (bf16[256,512]{1,0:T(8,128)(2,1)S(1)}, bf16[256,512]{1,0:T(8,128)(2,1)S(1)}, u32[]{:S(2)}, u32[]{:S(2)}) collective-permute-start(bf16[256,512]{1,0:T(8,128)(2,1)S(1)} %get-tuple-element.70), channel_id=1, source_target_pairs={{0,7},{1,6},{2,5},{3,4},{4,3},{5,2},{6,1},{7,0},{8,15},{9,14},{10,... | collective-permute-start | bytes 786440 | tf_op jit(solution)/shard_map/ppermute | solution.py:499
  73.6 33.5 %collective-permute-start.16 = (bf16[1024,256]{1,0:T(8,128)(2,1)S(1)}, bf16[1024,256]{1,0:T(8,128)(2,1)S(1)}, u32[]{:S(2)}, u32[]{:S(2)}) collective-permute-start(bf16[1024,256]{1,0:T(8,128)(2,1)S(1)} %get-tuple-element.56), channel_id=1, source_target_pairs={{0,1},{1,0},{2,3},{3,2},{4,5},{5,4},{6,7},{7,6},{8,9},{9,8},{10,11... | collective-permute-start | bytes 1572872 | tf_op jit(solution)/shard_map/ppermute | solution.py:40
  101.1 12.6 %collective-permute-start.21 = (bf16[1024,256]{1,0:T(8,128)(2,1)S(1)}, bf16[1024,256]{1,0:T(8,128)(2,1)S(1)}, u32[]{:S(2)}, u32[]{:S(2)}) collective-permute-start(bf16[1024,256]{1,0:T(8,128)(2,1)S(1)} %get-tuple-element.64), channel_id=1, source_target_pairs={{0,1},{1,0},{2,3},{3,2},{4,5},{5,4},{6,7},{7,6},{8,9},{9,8},{10,11... | collective-permute-start | bytes 1572872 | tf_op jit(solution)/shard_map/ppermute | solution.py:40
  102.7 6.6 %collective-permute-start.27 = (bf16[64,512]{1,0:T(8,128)(2,1)S(1)}, bf16[64,512]{1,0:T(8,128)(2,1)S(1)}, u32[]{:S(2)}, u32[]{:S(2)}) collective-permute-start(bf16[64,512]{1,0:T(8,128)(2,1)S(1)} %get-tuple-element.73), channel_id=1, source_target_pairs={{0,16},{2,18},{4,20},{6,22},{8,24},{10,26},{12,28},{14,30},{16,0},... | collective-permute-start | bytes 196616 | tf_op jit(solution)/shard_map/ppermute | solution.py:35
  109.4 6.5 %collective-permute-start.20 = (bf16[256,256]{1,0:T(8,128)(2,1)S(1)}, bf16[256,256]{1,0:T(8,128)(2,1)S(1)}, u32[]{:S(2)}, u32[]{:S(2)}) collective-permute-start(bf16[256,256]{1,0:T(8,128)(2,1)S(1)} %get-tuple-element.62), channel_id=1, source_target_pairs={{0,6},{2,4},{4,2},{6,0},{8,14},{10,12},{12,10},{14,8},{16,22},{18,... | collective-permute-start | bytes 393224 | tf_op jit(solution)/shard_map/ppermute | solution.py:35
  111.3 8.3 %collective-permute-start.29 = (f32[16,512]{1,0:T(8,128)S(1)}, f32[16,512]{1,0:T(8,128)S(1)}, u32[]{:S(2)}, u32[]{:S(2)}) collective-permute-start(f32[16,512]{1,0:T(8,128)S(1)} %get-tuple-element.76), channel_id=1, source_target_pairs={{0,2},{2,0},{4,6},{6,4},{8,10},{10,8},{12,14},{14,12},{16,18},{18,... | collective-permute-start | bytes 98312 | tf_op jit(solution)/shard_map/ppermute | solution.py:35
  116.0 10.5 %collective-permute-start.22 = (bf16[256,256]{1,0:T(8,128)(2,1)S(1)}, bf16[256,256]{1,0:T(8,128)(2,1)S(1)}, u32[]{:S(2)}, u32[]{:S(2)}) collective-permute-start(bf16[256,256]{1,0:T(8,128)(2,1)S(1)} %get-tuple-element.66), channel_id=1, source_target_pairs={{0,2},{2,0},{4,6},{6,4},{8,10},{10,8},{12,14},{14,12},{16,18},{18,... | collective-permute-start | bytes 393224 | tf_op jit(solution)/shard_map/ppermute | solution.py:35
  116.2 10.3 %collective-permute-start.23 = (bf16[256,256]{1,0:T(8,128)(2,1)S(1)}, bf16[256,256]{1,0:T(8,128)(2,1)S(1)}, u32[]{:S(2)}, u32[]{:S(2)}) collective-permute-start(bf16[256,256]{1,0:T(8,128)(2,1)S(1)} %get-tuple-element.67), channel_id=1, source_target_pairs={{0,4},{2,6},{4,0},{6,2},{8,12},{10,14},{12,8},{14,10},{16,20},{18,... | collective-permute-start | bytes 393224 | tf_op jit(solution)/shard_map/ppermute | solution.py:35
  118.0 8.5 %collective-permute-start.24 = (bf16[256,256]{1,0:T(8,128)(2,1)S(1)}, bf16[256,256]{1,0:T(8,128)(2,1)S(1)}, u32[]{:S(2)}, u32[]{:S(2)}) collective-permute-start(bf16[256,256]{1,0:T(8,128)(2,1)S(1)} %get-tuple-element.68), channel_id=1, source_target_pairs={{0,6},{2,4},{4,2},{6,0},{8,14},{10,12},{12,10},{14,8},{16,22},{18,... | collective-permute-start | bytes 393224 | tf_op jit(solution)/shard_map/ppermute | solution.py:35
  118.0 7.8 %collective-permute-start.30 = (f32[16,512]{1,0:T(8,128)S(1)}, f32[16,512]{1,0:T(8,128)S(1)}, u32[]{:S(2)}, u32[]{:S(2)}) collective-permute-start(f32[16,512]{1,0:T(8,128)S(1)} %get-tuple-element.77), channel_id=1, source_target_pairs={{0,4},{2,6},{4,0},{6,2},{8,12},{10,14},{12,8},{14,10},{16,20},{18,... | collective-permute-start | bytes 98312 | tf_op jit(solution)/shard_map/ppermute | solution.py:35
  (19 other events, 127.0 us)

commit v3 on v2

--- a/solution.py
+++ b/solution.py
@@ -96,18 +96,21 @@
     return np.eye(count, dtype=np.float32)[::-1].astype(BF16)
 
 
-def tie(value, *deps):
+def halves_after(value, *deps):
+    half = value.shape[0] // 2
+
     def kernel(value_ref, *rest):
-        rest[-1][...] = value_ref[...]
-
-    return pl.pallas_call(
-        kernel,
-        out_shape=shape(value.shape, value.dtype),
+        rest[-2][...] = value_ref[:half]
+        rest[-1][...] = value_ref[half:]
+
+    return pl.pallas_call(
+        kernel,
+        out_shape=[shape((half, value.shape[1]), value.dtype)] * 2,
         in_specs=[VMEM] + [ANY] * len(deps),
-        out_specs=VMEM,
+        out_specs=[VMEM] * 2,
         compiler_params=params(8),
-        cost_estimate=cost(1),
-        name="tie",
+        cost_estimate=SMALL,
+        name="halves_after",
     )(value, *deps)
 
 
@@ -270,7 +273,7 @@
         ],
         scratch_shapes=[pltpu.VMEM((INNER, rows, chunk), F32)],
         compiler_params=params(32),
-        cost_estimate=cost(5),
+        cost_estimate=cost(0.1),
         name="correlations",
     )(*pieces, spectrum, const["into"], const["lags"], reversal(chunk), *deps)
 
@@ -302,8 +305,8 @@
     tile = span // INNER
 
     def kernel(*refs):
-        blocks = refs[INNER : INNER + len(choices)]
-        out, token, rhs, sem = refs[INNER + len(choices) + len(deps) :]
+        blocks = refs[INNER + 1 : INNER + 1 + len(choices)]
+        out, token, rhs, sem = refs[INNER + 1 + len(choices) + len(deps) :]
         q = group_index()
         z = lax.div(lax.axis_index("seq"), INNER)
         early = lax.axis_index("ch") == lax.div(z, 2)
@@ -328,63 +331,80 @@
         for t in range(INNER):
             at = slice(t * tile, (t + 1) * tile)
             total = 0.0
-            for k in range(INNER):
+            for k in range(INNER - 1):
                 total += dot_nt(refs[k][at, :], rhs[:, columns(q ^ k, cq)])
+            within = slice(t % 2 * tile, (t % 2 + 1) * tile)
+            total += dot_nt(refs[INNER - 1 + t // 2][within, :], rhs[:, columns(q ^ (INNER - 1), cq)])
             out[at, :] = total.astype(dtype)
 
     return pl.pallas_call(
         kernel,
         out_shape=[shape((span, o_rows), dtype), shape(TOKEN, F32)],
-        in_specs=[VMEM] * INNER + [HBM] * len(choices) + [ANY] * len(deps),
+        in_specs=[VMEM] * (INNER + 1) + [HBM] * len(choices) + [ANY] * len(deps),
         out_specs=[VMEM] * 2,
         scratch_shapes=[pltpu.VMEM((o_rows, width), BF16), pltpu.SemaphoreType.DMA],
         compiler_params=params(16),
-        cost_estimate=cost(3),
+        cost_estimate=SMALL,
         name="project",
     )(*conv, *[block for _, block in choices], *deps)
 
 
-def summed_rows(kept, received, dtype, deps=()):
-    n = len(received)
+def summed_rows(kept, got, lags, deps=()):
     span, width = kept.shape
     rows = span // INNER
-
-    def kernel(kept_ref, *rest):
-        q, outs = group_index(), rest[n + len(deps) :]
-        for k in range(INNER):
+    count = len(lags)
+    lag_rows = lags[0].shape[0] // INNER if lags else 0
+    folds = lags[0].shape[1] // width if lags else 0
+
+    def kernel(kept_ref, got_ref, *rest):
+        q = group_index()
+        for k, out in enumerate(rest[count + len(deps) :]):
             at = pl.ds(pl.multiple_of((q ^ k) * rows, rows), rows)
-            total = kept_ref[at, :]
-            for got_ref in rest[:n]:
-                total += got_ref[at, :].astype(F32)
-            outs[k][...] = total.astype(dtype)
-
-    return pl.pallas_call(
-        kernel,
-        out_shape=[shape((rows, width), dtype)] * INNER,
-        in_specs=[VMEM] * (1 + n) + [ANY] * len(deps),
+            out[:rows, :] = (kept_ref[at, :] + got_ref[at, :].astype(F32)).astype(BF16)
+            if lags:
+                at = pl.ds(pl.multiple_of((q ^ k) * lag_rows, lag_rows), lag_rows)
+                total = 0.0
+                for lag_ref in rest[:count]:
+                    total += lag_ref[at, :].astype(F32)
+                for fold in range(folds):
+                    to = rows + fold * lag_rows
+                    out[to : to + lag_rows, :] = total[:, fold * width : (fold + 1) * width].astype(BF16)
+
+    return pl.pallas_call(
+        kernel,
+        out_shape=[shape((rows + folds * lag_rows, width), BF16)] * INNER,
+        in_specs=[VMEM] * (2 + count) + [ANY] * len(deps),
         out_specs=[VMEM] * INNER,
         compiler_params=params(16),
         cost_estimate=cost(1),
         name="summed_rows",
-    )(kept, *received, *deps)
+    )(kept, got, *lags, *deps)
 
 
 def assembled(first, second, width):
     rows, o_rows = first[0].shape
+    folds = width // INNER // o_rows
+    lag_rows = (second[0].shape[0] - rows) // folds
 
     def kernel(*refs):
         q = group_index()
         z = lax.div(lax.axis_index("seq"), INNER)
+        out, filter_out = refs[-2:]
         for r in range(2):
             for k in range(INNER):
                 block = (lax.rem(z, 2) ^ r) * INNER + (q ^ k)
-                refs[-1][:, columns(block, o_rows)] = refs[r * INNER + k][...]
-
-    return pl.pallas_call(
-        kernel,
-        out_shape=shape((rows, width), BF16),
+                out[:, columns(block, o_rows)] = refs[r * INNER + k][:rows, :]
+        for k in range(INNER):
+            for fold in range(folds):
+                at = rows + fold * lag_rows
+                lag = refs[INNER + k][at : at + lag_rows, :]
+                filter_out[:, columns((q ^ k) * folds + fold, o_rows)] = lag.astype(F32)
+
+    return pl.pallas_call(
+        kernel,
+        out_shape=[shape((rows, width), BF16), shape((lag_rows, width), F32)],
         in_specs=[VMEM] * (2 * INNER),
-        out_specs=VMEM,
+        out_specs=[VMEM] * 2,
         compiler_params=params(16),
         cost_estimate=cost(1),
         name="assembled",
@@ -478,11 +498,12 @@
     final, initial = pick_member(grads, q, INNER - 1), pick_member(grads, q, 0)
     before = lax.ppermute(final, "seq", [(i, i + INNER) for i in range(n_seq - INNER)])
     after = lax.ppermute(initial, "seq", [(i + INNER, i) for i in range(n_seq - INNER)])
-    near_ones = ()
+    near_ones, far = (), ()
     if special:
         near_ones = (near, mid)
         far_ends = shift(mid, [(1, 0), (2, 3)])
         far_mid = shift(near, [(2, 1), (1, 2)])
+        far = (far_mid, far_ends)
         last = shift(far_mid, [(1, 0), (2, 3)])
     input_own, input_near, input_far = quarters(saved_in, [(0,), (1,), (2, 3)], (grads[2],))
     input_far = swap_seq(input_far, 2)
@@ -492,9 +513,9 @@
     conv2 = swap_seq(conv, 2)
     conv1 = swap_seq(conv, 1)
     scale = 2.0 / window / math.sqrt(rows * n_seq)
-    forward, turned, token = correlations(inputs, spectrum, const, scale, ())
-    conv3 = swap_seq(tie(conv2, token), 1)
-    conv_parts = [conv, conv1, conv2, conv3]
+    forward, turned, token = correlations(inputs, spectrum, const, scale, far)
+    conv3 = [swap_seq(half, 1) for half in halves_after(conv2, token)]
+    conv_parts = [conv, conv1, conv2, *conv3]
 
     mirrored = lax.ppermute(
         turned,
@@ -513,20 +534,18 @@
         first, token = project(conv_parts, sent(x2, projection), BF16, (token,))
         got = mirror_ch(first)
         own, token = project(conv_parts, kept(x2, projection), F32, (token,))
-        second, token = project(conv_parts, sent(x3, near), BF16, (token,))
+        lag_own, *lag_sent = lag_blocks(forward, mirrored, outer, ())
+        second, token = project(conv_parts, sent(x3, near), BF16, (token, lag_own))
         got2 = mirror_ch(second)
-        lag_own, *lag_sent = lag_blocks(forward, mirrored, outer, (token,))
         lag_got = [swap_seq(block, INNER * (k + 1)) for k, block in enumerate(lag_sent)]
-        moved = spread(summed_rows(own, [got], BF16, (token,)))
+        moved = spread(summed_rows(own, got, []))
         own2, token = project(conv_parts, kept(x3, near), F32, (token,))
-        lag_pieces = summed_rows(lag_own, lag_got, F32)
-        filter_grad, filter_token = side_by_side(spread(lag_pieces))
-        moved2 = spread(summed_rows(own2, [got2], BF16, tuple(moved)))
-        grad_in = assembled(moved, moved2, width)
+        moved2 = spread(summed_rows(own2, got2, [lag_own] + lag_got, tuple(moved)))
+        grad_in, filter_grad = assembled(moved, moved2, width)
     else:
         groups = [[INNER * a + i for a in range(outer)] for i in range(INNER)]
         proj_all = lax.all_gather(projection, "seq", axis=0, axis_index_groups=groups)
-        conv_all = placed_by_source(conv_parts, q)
+        conv_all = placed_by_source([conv, conv1, conv2, jnp.concatenate(conv3, 0)], q)
         partial_value = lax.dot_general(
             conv_all.transpose(1, 0, 2).reshape(span, width),
             proj_all.reshape(-1, width),

time: 128 us -> 112 us (0.88)
  waiting for transfers between devices: 68.5 us -> 52.7 us
    ppermute x21 -> x19, waiting for transfers between devices: 35.4 us -> 25.2 us  [swap_seq(): return lax.ppermute(value, 'seq', [(i, i ^ k) for i in range(count)])]
    ppermute x5, waiting for transfers between devices: 23.5 us -> 18.5 us  [body(): lax.ppermute(v, 'seq', [(INNER * a + i, INNER * b + i) for a, b in table...]
    ppermute x1, waiting for transfers between devices: 4.78 us -> 0.01 us  [body(): lax.ppermute(final, 'seq', [(i, i + INNER) for i in range(n_seq - INNER)])]
    ppermute x1, waiting for transfers between devices: 0.01 us -> 4.15 us  [body(): lax.ppermute(turned, ('seq', 'ch'), [(s * n_ch + c, (s ^ INNER - 1) * n_c...]
    ppermute x21 -> x19, starting transfers between devices: 17.1 us -> 15 us  [swap_seq(): return lax.ppermute(value, 'seq', [(i, i ^ k) for i in range(count)])]
    ppermute x5, starting transfers between devices: 8.21 us -> 10 us  [body(): lax.ppermute(v, 'seq', [(INNER * a + i, INNER * b + i) for a, b in table...]
  transfers between devices with their start and end apart: 32 -> 30, of which waited for: 12 -> 15; matrix products, arithmetic and copies ran while one was open for 0% -> 0% of each run, Pallas kernels for 10% -> 15%
where the time goes in v3:
time: 112 us; the launch traced here: 111 us
  waiting for transfers between devices  52.7 us (47%)
  starting transfers between devices  36.8 us (33%)
  Pallas kernels  18.1 us (16%)
  local copies, waits for them, and re-layouts  2.54 us (2%)
    ppermute x19, waiting for transfers between devices, swap_seq(): return lax.ppermute(value, 'seq', [(i, i ^ k) for i in range(count)])  25.2 us
    ppermute x5, waiting for transfers between devices, body(): lax.ppermute(v, 'seq', [(INNER * a + i, INNER * b + i) for a, b in table...  18.5 us
    ppermute x19, starting transfers between devices, swap_seq(): return lax.ppermute(value, 'seq', [(i, i ^ k) for i in range(count)])  15 us
    ppermute x5, starting transfers between devices, body(): lax.ppermute(v, 'seq', [(INNER * a + i, INNER * b + i) for a, b in table...  10 us
    pallas_call x4, Pallas kernels, project(): pl.pallas_call(kernel, out_shape=[shape((span, o_rows), dtype), shape(TOK...  5.97 us
    pallas_call x1, Pallas kernels, filtered(): pl.pallas_call(kernel, grid=(cq // chunk,), out_shape=[shape((PAIRS, 2 *...  5.42 us
    ppermute x1, waiting for transfers between devices, body(): lax.ppermute(initial, 'seq', [(i + INNER, i) for i in range(n_seq - INNER)])  4.59 us
    ppermute x3, starting transfers between devices, mirror_ch(): return lax.ppermute(value, 'ch', [(i, count - 1 - i) for i in range(count)])  4.59 us
  transfers between devices with their start and end apart: 30, of which 15 were waited for; matrix products, arithmetic and copies ran while one was open for 0% of the time, Pallas kernels for 15%

profile of v3, /device:TPU:0, one launch (start us, length us, event | category | flops | bytes accessed | tf_op | source)
XLA Modules:
  0.0 111.2 jit_solution(8357076124214826805)
XLA Ops:
  1.4 5.8 %collective-permute-start.7 = (bf16[256,2048]{1,0:T(8,128)(2,1)}, bf16[256,2048]{1,0:T(8,128)(2,1)S(1)}, u32[]{:S(2)}, u32[]{:S(2)}) collective-permute-start(bf16[256,2048]{1,0:T(8,128)(2,1)} %refs_7_.4), channel_id=1, source_target_pairs={{0,8},{2,10},{4,12},{6,14},{8,0},{10,2},{12,4},{14,6},{16,24},{18,... | collective-permute-start | bytes 3145736 | tf_op jit(solution)/shard_map/ppermute | solution.py:487
  9.3 1.6 %collective-permute-start.1 = (bf16[256,512]{1,0:T(8,128)(2,1)}, bf16[256,512]{1,0:T(8,128)(2,1)S(1)}, u32[]{:S(2)}, u32[]{:S(2)}) collective-permute-start(bf16[256,512]{1,0:T(8,128)(2,1)} %get-tuple-element.40), channel_id=1, source_target_pairs={{0,4},{2,6},{4,0},{6,2},{8,12},{10,14},{12,8},{14,10},{16,20},{18,... | collective-permute-start | bytes 786440 | tf_op jit(solution)/shard_map/ppermute | solution.py:35
  12.8 6.0 %collective-permute-done.1.refs_1_.refs_2_ = bf16[256,512]{1,0:T(8,128)(2,1)S(1)} collective-permute-done((bf16[256,512]{1,0:T(8,128)(2,1)}, bf16[256,512]{1,0:T(8,128)(2,1)S(1)}, u32[]{:S(2)}, u32[]{:S(2)}) %collective-permute-start.1) | collective-permute-done | bytes 262176 | tf_op jit(solution)/shard_map/ppermute | solution.py:35
  20.5 1.6 %collective-permute-start.6 = (bf16[2,256,512]{2,1,0:T(8,128)(2,1)S(1)}, bf16[2,256,512]{2,1,0:T(8,128)(2,1)S(1)}, u32[]{:S(2)}, u32[]{:S(2)}) collective-permute-start(bf16[2,256,512]{2,1,0:T(8,128)(2,1)S(1)} %get-tuple-element.45), channel_id=1, source_target_pairs={{0,4},{2,6},{4,0},{6,2},{8,12},{10,14},{12,8},{14,10},{16,20},{18,... | collective-permute-start | bytes 1572872 | tf_op jit(solution)/shard_map/ppermute | solution.py:35
  25.2 4.4 %collective-permute-start.3 = (bf16[256,512]{1,0:T(8,128)(2,1)S(1)}, bf16[256,512]{1,0:T(8,128)(2,1)S(1)}, u32[]{:S(2)}, u32[]{:S(2)}) collective-permute-start(bf16[256,512]{1,0:T(8,128)(2,1)S(1)} %get-tuple-element.75), channel_id=1, source_target_pairs={{0,8},{2,10},{4,12},{6,14},{8,16},{10,18},{12,20},{14,22},{16,24},... | collective-permute-start | bytes 786440 | tf_op jit(solution)/shard_map/ppermute | solution.py:499
  32.1 4.6 %collective-permute-done.4.refs_5_ = bf16[256,512]{1,0:T(8,128)(2,1)S(1)} collective-permute-done((bf16[256,512]{1,0:T(8,128)(2,1)S(1)}, bf16[256,512]{1,0:T(8,128)(2,1)S(1)}, u32[]{:S(2)}, u32[]{:S(2)}) %collective-permute-start.4) | collective-permute-done | bytes 262176 | tf_op jit(solution)/shard_map/ppermute | solution.py:500
  36.8 5.4 %filtered.1 = (bf16[3,512,512]{2,1,0:T(8,128)(2,1)S(1)}, bf16[1024,512]{1,0:T(8,128)(2,1)S(1)}) custom-call(bf16[256,512]{1,0:T(8,128)(2,1)S(1)} %get-tuple-element.38.refs_0_, bf16[256,512]{1,0:T(8,128)(2,1)S(1)} %collective-permute-done.refs_1_, bf16[256,512]{1,0:T(8,128)(2,1)S(1)} %collective-permute-done.1.refs_1_.refs_2_, ...), custom_call_target="tpu_custom_call" | custom-call | flops 6000000000 | bytes 6000000 | tf_op jit(solution)/shard_map/filtered/pallas_call | solution.py:214
  42.2 1.6 %collective-permute-start.10 = (bf16[1024,512]{1,0:T(8,128)(2,1)S(1)}, bf16[1024,512]{1,0:T(8,128)(2,1)S(1)}, u32[]{:S(2)}, u32[]{:S(2)}) collective-permute-start(bf16[1024,512]{1,0:T(8,128)(2,1)S(1)} %get-tuple-element.46.refs_0_), channel_id=1, source_target_pairs={{0,4},{2,6},{4,0},{6,2},{8,12},{10,14},{12,8},{14,10},{16,20},{18,... | collective-permute-start | bytes 3145736 | tf_op jit(solution)/shard_map/ppermute | solution.py:35
  45.7 1.5 %collective-permute-done.12.refs_3_ = bf16[256,512]{1,0:T(8,128)(2,1)S(1)} collective-permute-done((bf16[256,512]{1,0:T(8,128)(2,1)S(1)}, bf16[256,512]{1,0:T(8,128)(2,1)S(1)}, u32[]{:S(2)}, u32[]{:S(2)}) %collective-permute-start.12) | collective-permute-done | bytes 262176 | tf_op jit(solution)/shard_map/ppermute | solution.py:35
  47.2 11.2 %collective-permute-done.14.refs_9_.refs_5_ = bf16[256,2048]{1,0:T(8,128)(2,1)S(1)} collective-permute-done((bf16[256,2048]{1,0:T(8,128)(2,1)S(1)}, bf16[256,2048]{1,0:T(8,128)(2,1)S(1)}, u32[]{:S(2)}, u32[]{:S(2)}) %collective-permute-start.14) | collective-permute-done | bytes 1048608 | tf_op jit(solution)/shard_map/ppermute | solution.py:487
  58.4 3.9 %correlations.1 = (f32[256,512]{1,0:T(8,128)S(1)}, bf16[256,512]{1,0:T(8,128)(2,1)S(1)}, f32[8,128]{1,0:T(8,128)S(1)}) custom-call(bf16[256,512]{1,0:T(8,128)(2,1)S(1)} %get-tuple-element.47.refs_0_, bf16[256,512]{1,0:T(8,128)(2,1)S(1)} %collective-permute-done.11.refs_1_, bf16[256,512]{1,0:T(8,128)(2,1)S(1)} %get-tuple-element.77.refs_2_, ...), custom_call_target="tpu_custom_call" | custom-call | flops 100000000 | bytes 100000 | tf_op jit(solution)/shard_map/correlations/pallas_call | solution.py:261
  62.3 4.3 %collective-permute-done.10.value_ref.refs_2_ = bf16[1024,512]{1,0:T(8,128)(2,1)S(1)} collective-permute-done((bf16[1024,512]{1,0:T(8,128)(2,1)S(1)}, bf16[1024,512]{1,0:T(8,128)(2,1)S(1)}, u32[]{:S(2)}, u32[]{:S(2)}) %collective-permute-start.10) | collective-permute-done | bytes 1048608 | tf_op jit(solution)/shard_map/ppermute | solution.py:35
  70.8 1.5 %collective-permute-start.17 = (bf16[1024,256]{1,0:T(8,128)(2,1)S(1)}, bf16[1024,256]{1,0:T(8,128)(2,1)S(1)}, u32[]{:S(2)}, u32[]{:S(2)}) collective-permute-start(bf16[1024,256]{1,0:T(8,128)(2,1)S(1)} %get-tuple-element.55), channel_id=1, source_target_pairs={{0,1},{1,0},{2,3},{3,2},{4,5},{5,4},{6,7},{7,6},{8,9},{9,8},{10,11... | collective-permute-start | bytes 1572872 | tf_op jit(solution)/shard_map/ppermute | solution.py:40
  72.3 4.1 %collective-permute-done.22.mirrored_ref = bf16[256,512]{1,0:T(8,128)(2,1)S(1)} collective-permute-done((bf16[256,512]{1,0:T(8,128)(2,1)S(1)}, bf16[256,512]{1,0:T(8,128)(2,1)S(1)}, u32[]{:S(2)}, u32[]{:S(2)}) %collective-permute-start.22) | collective-permute-done | bytes 262176 | tf_op jit(solution)/shard_map/ppermute | solution.py:520
  77.9 7.3 %collective-permute-done.21.refs_5_ = bf16[256,2048]{1,0:T(8,128)(2,1)S(1)} collective-permute-done((bf16[256,2048]{1,0:T(8,128)(2,1)S(1)}, bf16[256,2048]{1,0:T(8,128)(2,1)S(1)}, u32[]{:S(2)}, u32[]{:S(2)}) %collective-permute-start.21) | collective-permute-done | bytes 1048608 | tf_op jit(solution)/shard_map/ppermute | solution.py:487
  86.7 1.6 %collective-permute-start.23 = (bf16[1024,256]{1,0:T(8,128)(2,1)S(1)}, bf16[1024,256]{1,0:T(8,128)(2,1)S(1)}, u32[]{:S(2)}, u32[]{:S(2)}) collective-permute-start(bf16[1024,256]{1,0:T(8,128)(2,1)S(1)} %get-tuple-element.66), channel_id=1, source_target_pairs={{0,1},{1,0},{2,3},{3,2},{4,5},{5,4},{6,7},{7,6},{8,9},{9,8},{10,11... | collective-permute-start | bytes 1572872 | tf_op jit(solution)/shard_map/ppermute | solution.py:40
  88.2 2.1 %collective-permute-start.25 = (bf16[64,512]{1,0:T(8,128)(2,1)S(1)}, bf16[64,512]{1,0:T(8,128)(2,1)S(1)}, u32[]{:S(2)}, u32[]{:S(2)}) collective-permute-start(bf16[64,512]{1,0:T(8,128)(2,1)S(1)} %get-tuple-element.68), channel_id=1, source_target_pairs={{0,16},{2,18},{4,20},{6,22},{8,24},{10,26},{12,28},{14,30},{16,0},... | collective-permute-start | bytes 196616 | tf_op jit(solution)/shard_map/ppermute | solution.py:35
  90.5 1.7 %collective-permute-start.19 = (bf16[256,256]{1,0:T(8,128)(2,1)S(1)}, bf16[256,256]{1,0:T(8,128)(2,1)S(1)}, u32[]{:S(2)}, u32[]{:S(2)}) collective-permute-start(bf16[256,256]{1,0:T(8,128)(2,1)S(1)} %get-tuple-element.58), channel_id=1, source_target_pairs={{0,4},{2,6},{4,0},{6,2},{8,12},{10,14},{12,8},{14,10},{16,20},{18,... | collective-permute-start | bytes 393224 | tf_op jit(solution)/shard_map/ppermute | solution.py:35
  93.4 1.6 %collective-permute-start.26 = (bf16[64,512]{1,0:T(8,128)(2,1)S(1)}, bf16[64,512]{1,0:T(8,128)(2,1)S(1)}, u32[]{:S(2)}, u32[]{:S(2)}) collective-permute-start(bf16[64,512]{1,0:T(8,128)(2,1)S(1)} %get-tuple-element.69), channel_id=1, source_target_pairs={{0,24},{2,26},{4,28},{6,30},{8,16},{10,18},{12,20},{14,22},{16,8},... | collective-permute-start | bytes 196616 | tf_op jit(solution)/shard_map/ppermute | solution.py:35
  95.0 1.8 %project.7 = (f32[1024,256]{1,0:T(8,128)S(1)}, f32[8,128]{1,0:T(8,128)}) custom-call(bf16[1024,512]{1,0:T(8,128)(2,1)S(1)} %get-tuple-element.46.refs_0_, bf16[1024,512]{1,0:T(8,128)(2,1)S(1)} %collective-permute-done.9.refs_1_, bf16[1024,512]{1,0:T(8,128)(2,1)S(1)} %collective-permute-done.10.value_ref.refs_2_, ...), custom_call_target="tpu_custom_call" | custom-call | flops 1000 | bytes 1000 | tf_op jit(solution)/shard_map/project/pallas_call | solution.py:340
  96.8 3.1 %collective-permute-done.26.rest_3_ = bf16[64,512]{1,0:T(8,128)(2,1)S(1)} collective-permute-done((bf16[64,512]{1,0:T(8,128)(2,1)S(1)}, bf16[64,512]{1,0:T(8,128)(2,1)S(1)}, u32[]{:S(2)}, u32[]{:S(2)}) %collective-permute-start.26) | collective-permute-done | bytes 65568 | tf_op jit(solution)/shard_map/ppermute | solution.py:35
  100.3 2.4 %collective-permute-start.28 = (bf16[288,256]{1,0:T(8,128)(2,1)S(1)}, bf16[288,256]{1,0:T(8,128)(2,1)S(1)}, u32[]{:S(2)}, u32[]{:S(2)}) collective-permute-start(bf16[288,256]{1,0:T(8,128)(2,1)S(1)} %get-tuple-element.72), channel_id=1, source_target_pairs={{0,4},{2,6},{4,0},{6,2},{8,12},{10,14},{12,8},{14,10},{16,20},{18,... | collective-permute-start | bytes 442376 | tf_op jit(solution)/shard_map/ppermute | solution.py:35
  102.8 4.6 %collective-permute-done.28.refs_6_ = bf16[288,256]{1,0:T(8,128)(2,1)S(1)} collective-permute-done((bf16[288,256]{1,0:T(8,128)(2,1)S(1)}, bf16[288,256]{1,0:T(8,128)(2,1)S(1)}, u32[]{:S(2)}, u32[]{:S(2)}) %collective-permute-start.28) | collective-permute-done | bytes 147488 | tf_op jit(solution)/shard_map/ppermute | solution.py:35
  107.4 2.6 %collective-permute-done.29.refs_7_ = bf16[288,256]{1,0:T(8,128)(2,1)S(1)} collective-permute-done((bf16[288,256]{1,0:T(8,128)(2,1)S(1)}, bf16[288,256]{1,0:T(8,128)(2,1)S(1)}, u32[]{:S(2)}, u32[]{:S(2)}) %collective-permute-start.29) | collective-permute-done | bytes 147488 | tf_op jit(solution)/shard_map/ppermute | solution.py:35
  (77 shorter events, 23.9 us)
Async XLA Ops:
  0.6 29.3 %collective-permute-start.8 = (bf16[256,2048]{1,0:T(8,128)(2,1)}, bf16[256,2048]{1,0:T(8,128)(2,1)S(1)}, u32[]{:S(2)}, u32[]{:S(2)}) collective-permute-start(bf16[256,2048]{1,0:T(8,128)(2,1)} %refs_7_.4), channel_id=1, source_target_pairs={{8,16},{10,18},{12,20},{14,22},{16,8},{18,10},{20,12},{22,14},{9,1... | collective-permute-start | bytes 3145736 | tf_op jit(solution)/shard_map/ppermute | solution.py:487
  1.4 30.0 %collective-permute-start.7 = (bf16[256,2048]{1,0:T(8,128)(2,1)}, bf16[256,2048]{1,0:T(8,128)(2,1)S(1)}, u32[]{:S(2)}, u32[]{:S(2)}) collective-permute-start(bf16[256,2048]{1,0:T(8,128)(2,1)} %refs_7_.4), channel_id=1, source_target_pairs={{0,8},{2,10},{4,12},{6,14},{8,0},{10,2},{12,4},{14,6},{16,24},{18,... | collective-permute-start | bytes 3145736 | tf_op jit(solution)/shard_map/ppermute | solution.py:487
  9.3 9.5 %collective-permute-start.1 = (bf16[256,512]{1,0:T(8,128)(2,1)}, bf16[256,512]{1,0:T(8,128)(2,1)S(1)}, u32[]{:S(2)}, u32[]{:S(2)}) collective-permute-start(bf16[256,512]{1,0:T(8,128)(2,1)} %get-tuple-element.40), channel_id=1, source_target_pairs={{0,4},{2,6},{4,0},{6,2},{8,12},{10,14},{12,8},{14,10},{16,20},{18,... | collective-permute-start | bytes 786440 | tf_op jit(solution)/shard_map/ppermute | solution.py:35
  10.9 9.6 %collective-permute-start = (bf16[256,512]{1,0:T(8,128)(2,1)}, bf16[256,512]{1,0:T(8,128)(2,1)S(1)}, u32[]{:S(2)}, u32[]{:S(2)}) collective-permute-start(bf16[256,512]{1,0:T(8,128)(2,1)} %get-tuple-element.39), channel_id=1, source_target_pairs={{0,2},{2,0},{4,6},{6,4},{8,10},{10,8},{12,14},{14,12},{16,18},{18,... | collective-permute-start | bytes 786440 | tf_op jit(solution)/shard_map/ppermute | solution.py:35
  10.9 12.6 %collective-permute-start.2 = (bf16[256,512]{1,0:T(8,128)(2,1)S(1)}, bf16[256,512]{1,0:T(8,128)(2,1)S(1)}, u32[]{:S(2)}, u32[]{:S(2)}) collective-permute-start(bf16[256,512]{1,0:T(8,128)(2,1)S(1)} %get-tuple-element.41), channel_id=1, source_target_pairs={{0,6},{2,4},{4,2},{6,0},{8,14},{10,12},{12,10},{14,8},{16,22},{18,... | collective-permute-start | bytes 786440 | tf_op jit(solution)/shard_map/ppermute | solution.py:35
  18.8 6.4 %collective-permute-start.5 = (bf16[256,512]{1,0:T(8,128)(2,1)S(1)}, bf16[256,512]{1,0:T(8,128)(2,1)S(1)}, u32[]{:S(2)}, u32[]{:S(2)}) collective-permute-start(bf16[256,512]{1,0:T(8,128)(2,1)S(1)} %quarters.4), channel_id=1, source_target_pairs={{0,1},{1,0},{2,3},{3,2},{4,5},{5,4},{6,7},{7,6},{8,9},{9,8},{10,11... | collective-permute-start | bytes 786440 | tf_op jit(solution)/shard_map/ppermute | solution.py:40
  20.5 16.2 %collective-permute-start.6 = (bf16[2,256,512]{2,1,0:T(8,128)(2,1)S(1)}, bf16[2,256,512]{2,1,0:T(8,128)(2,1)S(1)}, u32[]{:S(2)}, u32[]{:S(2)}) collective-permute-start(bf16[2,256,512]{2,1,0:T(8,128)(2,1)S(1)} %get-tuple-element.45), channel_id=1, source_target_pairs={{0,4},{2,6},{4,0},{6,2},{8,12},{10,14},{12,8},{14,10},{16,20},{18,... | collective-permute-start | bytes 1572872 | tf_op jit(solution)/shard_map/ppermute | solution.py:35
  23.5 13.2 %collective-permute-start.4 = (bf16[256,512]{1,0:T(8,128)(2,1)S(1)}, bf16[256,512]{1,0:T(8,128)(2,1)S(1)}, u32[]{:S(2)}, u32[]{:S(2)}) collective-permute-start(bf16[256,512]{1,0:T(8,128)(2,1)S(1)} %get-tuple-element.74), channel_id=1, source_target_pairs={{8,0},{10,2},{12,4},{14,6},{16,8},{18,10},{20,12},{22,14},{24,16},... | collective-permute-start | bytes 786440 | tf_op jit(solution)/shard_map/ppermute | solution.py:500
  25.2 11.5 %collective-permute-start.3 = (bf16[256,512]{1,0:T(8,128)(2,1)S(1)}, bf16[256,512]{1,0:T(8,128)(2,1)S(1)}, u32[]{:S(2)}, u32[]{:S(2)}) collective-permute-start(bf16[256,512]{1,0:T(8,128)(2,1)S(1)} %get-tuple-element.75), channel_id=1, source_target_pairs={{0,8},{2,10},{4,12},{6,14},{8,16},{10,18},{12,20},{14,22},{16,24},... | collective-permute-start | bytes 786440 | tf_op jit(solution)/shard_map/ppermute | solution.py:499
  29.9 28.5 %collective-permute-start.14 = (bf16[256,2048]{1,0:T(8,128)(2,1)S(1)}, bf16[256,2048]{1,0:T(8,128)(2,1)S(1)}, u32[]{:S(2)}, u32[]{:S(2)}) collective-permute-start(bf16[256,2048]{1,0:T(8,128)(2,1)S(1)} %collective-permute-done.8.refs_14_.refs_6_), channel_id=1, source_target_pairs={{8,0},{10,2},{12,4},{14,6},{16,24},{18,26},{20,28},{22,30},{9,1},{... | collective-permute-start | bytes 3145736 | tf_op jit(solution)/shard_map/ppermute | solution.py:487
  31.4 12.9 %collective-permute-start.13 = (bf16[256,2048]{1,0:T(8,128)(2,1)S(1)}, bf16[256,2048]{1,0:T(8,128)(2,1)S(1)}, u32[]{:S(2)}, u32[]{:S(2)}) collective-permute-start(bf16[256,2048]{1,0:T(8,128)(2,1)S(1)} %collective-permute-done.7.refs_13_.refs_7_), channel_id=1, source_target_pairs={{16,8},{18,10},{20,12},{22,14},{8,16},{10,18},{12,20},{14,22},{17,... | collective-permute-start | bytes 3145736 | tf_op jit(solution)/shard_map/ppermute | solution.py:487
  42.2 24.4 %collective-permute-start.10 = (bf16[1024,512]{1,0:T(8,128)(2,1)S(1)}, bf16[1024,512]{1,0:T(8,128)(2,1)S(1)}, u32[]{:S(2)}, u32[]{:S(2)}) collective-permute-start(bf16[1024,512]{1,0:T(8,128)(2,1)S(1)} %get-tuple-element.46.refs_0_), channel_id=1, source_target_pairs={{0,4},{2,6},{4,0},{6,2},{8,12},{10,14},{12,8},{14,10},{16,20},{18,... | collective-permute-start | bytes 3145736 | tf_op jit(solution)/shard_map/ppermute | solution.py:35
  43.8 24.9 %collective-permute-start.9 = (bf16[1024,512]{1,0:T(8,128)(2,1)S(1)}, bf16[1024,512]{1,0:T(8,128)(2,1)S(1)}, u32[]{:S(2)}, u32[]{:S(2)}) collective-permute-start(bf16[1024,512]{1,0:T(8,128)(2,1)S(1)} %get-tuple-element.46.refs_0_), channel_id=1, source_target_pairs={{0,2},{2,0},{4,6},{6,4},{8,10},{10,8},{12,14},{14,12},{16,18},{18,... | collective-permute-start | bytes 3145736 | tf_op jit(solution)/shard_map/ppermute | solution.py:35
  44.3 41.0 %collective-permute-start.21 = (bf16[256,2048]{1,0:T(8,128)(2,1)S(1)}, bf16[256,2048]{1,0:T(8,128)(2,1)S(1)}, u32[]{:S(2)}, u32[]{:S(2)}) collective-permute-start(bf16[256,2048]{1,0:T(8,128)(2,1)S(1)} %collective-permute-done.13.refs_8_.refs_6_), channel_id=1, source_target_pairs={{8,0},{10,2},{12,4},{14,6},{16,24},{18,26},{20,28},{22,30},{9,1},{... | collective-permute-start | bytes 3145736 | tf_op jit(solution)/shard_map/ppermute | solution.py:487
  67.2 9.2 %collective-permute-start.22 = (bf16[256,512]{1,0:T(8,128)(2,1)S(1)}, bf16[256,512]{1,0:T(8,128)(2,1)S(1)}, u32[]{:S(2)}, u32[]{:S(2)}) collective-permute-start(bf16[256,512]{1,0:T(8,128)(2,1)S(1)} %get-tuple-element.62), channel_id=1, source_target_pairs={{0,7},{1,6},{2,5},{3,4},{4,3},{5,2},{6,1},{7,0},{8,15},{9,14},{10,... | collective-permute-start | bytes 786440 | tf_op jit(solution)/shard_map/ppermute | solution.py:520
  70.8 19.5 %collective-permute-start.17 = (bf16[1024,256]{1,0:T(8,128)(2,1)S(1)}, bf16[1024,256]{1,0:T(8,128)(2,1)S(1)}, u32[]{:S(2)}, u32[]{:S(2)}) collective-permute-start(bf16[1024,256]{1,0:T(8,128)(2,1)S(1)} %get-tuple-element.55), channel_id=1, source_target_pairs={{0,1},{1,0},{2,3},{3,2},{4,5},{5,4},{6,7},{7,6},{8,9},{9,8},{10,11... | collective-permute-start | bytes 1572872 | tf_op jit(solution)/shard_map/ppermute | solution.py:40
  86.7 13.2 %collective-permute-start.23 = (bf16[1024,256]{1,0:T(8,128)(2,1)S(1)}, bf16[1024,256]{1,0:T(8,128)(2,1)S(1)}, u32[]{:S(2)}, u32[]{:S(2)}) collective-permute-start(bf16[1024,256]{1,0:T(8,128)(2,1)S(1)} %get-tuple-element.66), channel_id=1, source_target_pairs={{0,1},{1,0},{2,3},{3,2},{4,5},{5,4},{6,7},{7,6},{8,9},{9,8},{10,11... | collective-permute-start | bytes 1572872 | tf_op jit(solution)/shard_map/ppermute | solution.py:40
  88.2 5.2 %collective-permute-start.25 = (bf16[64,512]{1,0:T(8,128)(2,1)S(1)}, bf16[64,512]{1,0:T(8,128)(2,1)S(1)}, u32[]{:S(2)}, u32[]{:S(2)}) collective-permute-start(bf16[64,512]{1,0:T(8,128)(2,1)S(1)} %get-tuple-element.68), channel_id=1, source_target_pairs={{0,16},{2,18},{4,20},{6,22},{8,24},{10,26},{12,28},{14,30},{16,0},... | collective-permute-start | bytes 196616 | tf_op jit(solution)/shard_map/ppermute | solution.py:35
  90.4 9.5 %collective-permute-start.18 = (bf16[256,256]{1,0:T(8,128)(2,1)S(1)}, bf16[256,256]{1,0:T(8,128)(2,1)S(1)}, u32[]{:S(2)}, u32[]{:S(2)}) collective-permute-start(bf16[256,256]{1,0:T(8,128)(2,1)S(1)} %get-tuple-element.57), channel_id=1, source_target_pairs={{0,2},{2,0},{4,6},{6,4},{8,10},{10,8},{12,14},{14,12},{16,18},{18,... | collective-permute-start | bytes 393224 | tf_op jit(solution)/shard_map/ppermute | solution.py:35
  90.5 9.4 %collective-permute-start.19 = (bf16[256,256]{1,0:T(8,128)(2,1)S(1)}, bf16[256,256]{1,0:T(8,128)(2,1)S(1)}, u32[]{:S(2)}, u32[]{:S(2)}) collective-permute-start(bf16[256,256]{1,0:T(8,128)(2,1)S(1)} %get-tuple-element.58), channel_id=1, source_target_pairs={{0,4},{2,6},{4,0},{6,2},{8,12},{10,14},{12,8},{14,10},{16,20},{18,... | collective-permute-start | bytes 393224 | tf_op jit(solution)/shard_map/ppermute | solution.py:35
  92.5 7.4 %collective-permute-start.20 = (bf16[256,256]{1,0:T(8,128)(2,1)S(1)}, bf16[256,256]{1,0:T(8,128)(2,1)S(1)}, u32[]{:S(2)}, u32[]{:S(2)}) collective-permute-start(bf16[256,256]{1,0:T(8,128)(2,1)S(1)} %get-tuple-element.59), channel_id=1, source_target_pairs={{0,6},{2,4},{4,2},{6,0},{8,14},{10,12},{12,10},{14,8},{16,22},{18,... | collective-permute-start | bytes 393224 | tf_op jit(solution)/shard_map/ppermute | solution.py:35
  93.4 6.5 %collective-permute-start.26 = (bf16[64,512]{1,0:T(8,128)(2,1)S(1)}, bf16[64,512]{1,0:T(8,128)(2,1)S(1)}, u32[]{:S(2)}, u32[]{:S(2)}) collective-permute-start(bf16[64,512]{1,0:T(8,128)(2,1)S(1)} %get-tuple-element.69), channel_id=1, source_target_pairs={{0,24},{2,26},{4,28},{6,30},{8,16},{10,18},{12,20},{14,22},{16,8},... | collective-permute-start | bytes 196616 | tf_op jit(solution)/shard_map/ppermute | solution.py:35
  100.3 7.1 %collective-permute-start.28 = (bf16[288,256]{1,0:T(8,128)(2,1)S(1)}, bf16[288,256]{1,0:T(8,128)(2,1)S(1)}, u32[]{:S(2)}, u32[]{:S(2)}) collective-permute-start(bf16[288,256]{1,0:T(8,128)(2,1)S(1)} %get-tuple-element.72), channel_id=1, source_target_pairs={{0,4},{2,6},{4,0},{6,2},{8,12},{10,14},{12,8},{14,10},{16,20},{18,... | collective-permute-start | bytes 442376 | tf_op jit(solution)/shard_map/ppermute | solution.py:35
  102.7 7.3 %collective-permute-start.29 = (bf16[288,256]{1,0:T(8,128)(2,1)S(1)}, bf16[288,256]{1,0:T(8,128)(2,1)S(1)}, u32[]{:S(2)}, u32[]{:S(2)}) collective-permute-start(bf16[288,256]{1,0:T(8,128)(2,1)S(1)} %get-tuple-element.73), channel_id=1, source_target_pairs={{0,6},{2,4},{4,2},{6,0},{8,14},{10,12},{12,10},{14,8},{16,22},{18,... | collective-permute-start | bytes 442376 | tf_op jit(solution)/shard_map/ppermute | solution.py:35
  (18 other events, 125.1 us)

commit v4 on v3

--- a/solution.py
+++ b/solution.py
@@ -540,7 +540,7 @@
         lag_got = [swap_seq(block, INNER * (k + 1)) for k, block in enumerate(lag_sent)]
         moved = spread(summed_rows(own, got, []))
         own2, token = project(conv_parts, kept(x3, near), F32, (token,))
-        moved2 = spread(summed_rows(own2, got2, [lag_own] + lag_got, tuple(moved)))
+        moved2 = spread(summed_rows(own2, got2, [lag_own] + lag_got))
         grad_in, filter_grad = assembled(moved, moved2, width)
     else:
         groups = [[INNER * a + i for a in range(outer)] for i in range(INNER)]

time: 112 us -> 117 us (1.045)
  waiting for transfers between devices: 52.7 us -> 57.3 us
    ppermute x3, waiting for transfers between devices: 0.22 us -> 3.23 us  [mirror_ch(): return lax.ppermute(value, 'ch', [(i, count - 1 - i) for i in range(count)])]
    ppermute x19, waiting for transfers between devices: 25.2 us -> 26.8 us  [swap_seq(): return lax.ppermute(value, 'seq', [(i, i ^ k) for i in range(count)])]
  transfers between devices with their start and end apart: 30 -> 30, of which waited for: 15 -> 14; matrix products, arithmetic and copies ran while one was open for 0% -> 0% of each run, Pallas kernels for 15% -> 15%
where the time goes in v4:
time: 117 us
  waiting for transfers between devices  57.3 us (49%)
  starting transfers between devices  37.8 us (32%)
  Pallas kernels  18.1 us (15%)
  local copies, waits for them, and re-layouts  2.54 us (2%)
    ppermute x19, waiting for transfers between devices, swap_seq(): return lax.ppermute(value, 'seq', [(i, i ^ k) for i in range(count)])  26.8 us
    ppermute x5, waiting for transfers between devices, body(): lax.ppermute(v, 'seq', [(INNER * a + i, INNER * b + i) for a, b in table...  18.5 us
    ppermute x19, starting transfers between devices, swap_seq(): return lax.ppermute(value, 'seq', [(i, i ^ k) for i in range(count)])  16 us
    ppermute x5, starting transfers between devices, body(): lax.ppermute(v, 'seq', [(INNER * a + i, INNER * b + i) for a, b in table...  10 us
    pallas_call x4, Pallas kernels, project(): pl.pallas_call(kernel, out_shape=[shape((span, o_rows), dtype), shape(TOK...  6 us
    pallas_call x1, Pallas kernels, filtered(): pl.pallas_call(kernel, grid=(cq // chunk,), out_shape=[shape((PAIRS, 2 *...  5.42 us
    ppermute x1, waiting for transfers between devices, body(): lax.ppermute(initial, 'seq', [(i + INNER, i) for i in range(n_seq - INNER)])  4.59 us
    ppermute x3, starting transfers between devices, mirror_ch(): return lax.ppermute(value, 'ch', [(i, count - 1 - i) for i in range(count)])  4.59 us
  transfers between devices with their start and end apart: 30, of which 14 were waited for; matrix products, arithmetic and copies ran while one was open for 0% of the time, Pallas kernels for 15%

profile of v4, /device:TPU:0, one launch (start us, length us, event | category | flops | bytes accessed | tf_op | source)
XLA Modules:
  0.0 116.8 jit_solution(15590947360834975218)
XLA Ops:
  1.4 5.8 %collective-permute-start.7 = (bf16[256,2048]{1,0:T(8,128)(2,1)}, bf16[256,2048]{1,0:T(8,128)(2,1)S(1)}, u32[]{:S(2)}, u32[]{:S(2)}) collective-permute-start(bf16[256,2048]{1,0:T(8,128)(2,1)} %refs_7_.4), channel_id=1, source_target_pairs={{0,8},{2,10},{4,12},{6,14},{8,0},{10,2},{12,4},{14,6},{16,24},{18,... | collective-permute-start | bytes 3145736 | tf_op jit(solution)/shard_map/ppermute | solution.py:487
  9.3 1.6 %collective-permute-start.1 = (bf16[256,512]{1,0:T(8,128)(2,1)}, bf16[256,512]{1,0:T(8,128)(2,1)S(1)}, u32[]{:S(2)}, u32[]{:S(2)}) collective-permute-start(bf16[256,512]{1,0:T(8,128)(2,1)} %get-tuple-element.40), channel_id=1, source_target_pairs={{0,4},{2,6},{4,0},{6,2},{8,12},{10,14},{12,8},{14,10},{16,20},{18,... | collective-permute-start | bytes 786440 | tf_op jit(solution)/shard_map/ppermute | solution.py:35
  12.8 6.0 %collective-permute-done.1.refs_1_.refs_2_ = bf16[256,512]{1,0:T(8,128)(2,1)S(1)} collective-permute-done((bf16[256,512]{1,0:T(8,128)(2,1)}, bf16[256,512]{1,0:T(8,128)(2,1)S(1)}, u32[]{:S(2)}, u32[]{:S(2)}) %collective-permute-start.1) | collective-permute-done | bytes 262176 | tf_op jit(solution)/shard_map/ppermute | solution.py:35
  20.5 1.6 %collective-permute-start.6 = (bf16[2,256,512]{2,1,0:T(8,128)(2,1)S(1)}, bf16[2,256,512]{2,1,0:T(8,128)(2,1)S(1)}, u32[]{:S(2)}, u32[]{:S(2)}) collective-permute-start(bf16[2,256,512]{2,1,0:T(8,128)(2,1)S(1)} %get-tuple-element.45), channel_id=1, source_target_pairs={{0,4},{2,6},{4,0},{6,2},{8,12},{10,14},{12,8},{14,10},{16,20},{18,... | collective-permute-start | bytes 1572872 | tf_op jit(solution)/shard_map/ppermute | solution.py:35
  25.2 4.4 %collective-permute-start.3 = (bf16[256,512]{1,0:T(8,128)(2,1)S(1)}, bf16[256,512]{1,0:T(8,128)(2,1)S(1)}, u32[]{:S(2)}, u32[]{:S(2)}) collective-permute-start(bf16[256,512]{1,0:T(8,128)(2,1)S(1)} %get-tuple-element.75), channel_id=1, source_target_pairs={{0,8},{2,10},{4,12},{6,14},{8,16},{10,18},{12,20},{14,22},{16,24},... | collective-permute-start | bytes 786440 | tf_op jit(solution)/shard_map/ppermute | solution.py:499
  32.1 4.6 %collective-permute-done.4.refs_5_ = bf16[256,512]{1,0:T(8,128)(2,1)S(1)} collective-permute-done((bf16[256,512]{1,0:T(8,128)(2,1)S(1)}, bf16[256,512]{1,0:T(8,128)(2,1)S(1)}, u32[]{:S(2)}, u32[]{:S(2)}) %collective-permute-start.4) | collective-permute-done | bytes 262176 | tf_op jit(solution)/shard_map/ppermute | solution.py:500
  36.8 5.4 %filtered.1 = (bf16[3,512,512]{2,1,0:T(8,128)(2,1)S(1)}, bf16[1024,512]{1,0:T(8,128)(2,1)S(1)}) custom-call(bf16[256,512]{1,0:T(8,128)(2,1)S(1)} %get-tuple-element.38.refs_0_, bf16[256,512]{1,0:T(8,128)(2,1)S(1)} %collective-permute-done.refs_1_, bf16[256,512]{1,0:T(8,128)(2,1)S(1)} %collective-permute-done.1.refs_1_.refs_2_, ...), custom_call_target="tpu_custom_call" | custom-call | flops 6000000000 | bytes 6000000 | tf_op jit(solution)/shard_map/filtered/pallas_call | solution.py:214
  42.2 1.6 %collective-permute-start.10 = (bf16[1024,512]{1,0:T(8,128)(2,1)S(1)}, bf16[1024,512]{1,0:T(8,128)(2,1)S(1)}, u32[]{:S(2)}, u32[]{:S(2)}) collective-permute-start(bf16[1024,512]{1,0:T(8,128)(2,1)S(1)} %get-tuple-element.46.refs_0_), channel_id=1, source_target_pairs={{0,4},{2,6},{4,0},{6,2},{8,12},{10,14},{12,8},{14,10},{16,20},{18,... | collective-permute-start | bytes 3145736 | tf_op jit(solution)/shard_map/ppermute | solution.py:35
  47.2 11.2 %collective-permute-done.14.refs_9_.refs_5_ = bf16[256,2048]{1,0:T(8,128)(2,1)S(1)} collective-permute-done((bf16[256,2048]{1,0:T(8,128)(2,1)S(1)}, bf16[256,2048]{1,0:T(8,128)(2,1)S(1)}, u32[]{:S(2)}, u32[]{:S(2)}) %collective-permute-start.14) | collective-permute-done | bytes 1048608 | tf_op jit(solution)/shard_map/ppermute | solution.py:487
  58.4 3.9 %correlations.1 = (f32[256,512]{1,0:T(8,128)S(1)}, bf16[256,512]{1,0:T(8,128)(2,1)S(1)}, f32[8,128]{1,0:T(8,128)S(1)}) custom-call(bf16[256,512]{1,0:T(8,128)(2,1)S(1)} %get-tuple-element.47.refs_0_, bf16[256,512]{1,0:T(8,128)(2,1)S(1)} %collective-permute-done.11.refs_1_, bf16[256,512]{1,0:T(8,128)(2,1)S(1)} %get-tuple-element.77.refs_2_, ...), custom_call_target="tpu_custom_call" | custom-call | flops 100000000 | bytes 100000 | tf_op jit(solution)/shard_map/correlations/pallas_call | solution.py:261
  62.3 4.3 %collective-permute-done.10.value_ref.refs_2_ = bf16[1024,512]{1,0:T(8,128)(2,1)S(1)} collective-permute-done((bf16[1024,512]{1,0:T(8,128)(2,1)S(1)}, bf16[1024,512]{1,0:T(8,128)(2,1)S(1)}, u32[]{:S(2)}, u32[]{:S(2)}) %collective-permute-start.10) | collective-permute-done | bytes 1048608 | tf_op jit(solution)/shard_map/ppermute | solution.py:35
  70.8 1.5 %collective-permute-start.17 = (bf16[1024,256]{1,0:T(8,128)(2,1)S(1)}, bf16[1024,256]{1,0:T(8,128)(2,1)S(1)}, u32[]{:S(2)}, u32[]{:S(2)}) collective-permute-start(bf16[1024,256]{1,0:T(8,128)(2,1)S(1)} %get-tuple-element.55), channel_id=1, source_target_pairs={{0,1},{1,0},{2,3},{3,2},{4,5},{5,4},{6,7},{7,6},{8,9},{9,8},{10,11... | collective-permute-start | bytes 1572872 | tf_op jit(solution)/shard_map/ppermute | solution.py:40
  72.3 4.1 %collective-permute-done.22.mirrored_ref = bf16[256,512]{1,0:T(8,128)(2,1)S(1)} collective-permute-done((bf16[256,512]{1,0:T(8,128)(2,1)S(1)}, bf16[256,512]{1,0:T(8,128)(2,1)S(1)}, u32[]{:S(2)}, u32[]{:S(2)}) %collective-permute-start.22) | collective-permute-done | bytes 262176 | tf_op jit(solution)/shard_map/ppermute | solution.py:520
  77.9 7.3 %collective-permute-done.21.refs_5_ = bf16[256,2048]{1,0:T(8,128)(2,1)S(1)} collective-permute-done((bf16[256,2048]{1,0:T(8,128)(2,1)S(1)}, bf16[256,2048]{1,0:T(8,128)(2,1)S(1)}, u32[]{:S(2)}, u32[]{:S(2)}) %collective-permute-start.21) | collective-permute-done | bytes 1048608 | tf_op jit(solution)/shard_map/ppermute | solution.py:487
  86.7 1.6 %collective-permute-start.23 = (bf16[1024,256]{1,0:T(8,128)(2,1)S(1)}, bf16[1024,256]{1,0:T(8,128)(2,1)S(1)}, u32[]{:S(2)}, u32[]{:S(2)}) collective-permute-start(bf16[1024,256]{1,0:T(8,128)(2,1)S(1)} %get-tuple-element.66), channel_id=1, source_target_pairs={{0,1},{1,0},{2,3},{3,2},{4,5},{5,4},{6,7},{7,6},{8,9},{9,8},{10,11... | collective-permute-start | bytes 1572872 | tf_op jit(solution)/shard_map/ppermute | solution.py:40
  88.2 2.1 %collective-permute-start.25 = (bf16[64,512]{1,0:T(8,128)(2,1)S(1)}, bf16[64,512]{1,0:T(8,128)(2,1)S(1)}, u32[]{:S(2)}, u32[]{:S(2)}) collective-permute-start(bf16[64,512]{1,0:T(8,128)(2,1)S(1)} %get-tuple-element.68), channel_id=1, source_target_pairs={{0,16},{2,18},{4,20},{6,22},{8,24},{10,26},{12,28},{14,30},{16,0},... | collective-permute-start | bytes 196616 | tf_op jit(solution)/shard_map/ppermute | solution.py:35
  90.3 2.3 %collective-permute-start.26 = (bf16[64,512]{1,0:T(8,128)(2,1)S(1)}, bf16[64,512]{1,0:T(8,128)(2,1)S(1)}, u32[]{:S(2)}, u32[]{:S(2)}) collective-permute-start(bf16[64,512]{1,0:T(8,128)(2,1)S(1)} %get-tuple-element.69), channel_id=1, source_target_pairs={{0,24},{2,26},{4,28},{6,30},{8,16},{10,18},{12,20},{14,22},{16,8},... | collective-permute-start | bytes 196616 | tf_op jit(solution)/shard_map/ppermute | solution.py:35
  92.8 1.8 %project.7 = (f32[1024,256]{1,0:T(8,128)S(1)}, f32[8,128]{1,0:T(8,128)}) custom-call(bf16[1024,512]{1,0:T(8,128)(2,1)S(1)} %get-tuple-element.46.refs_0_, bf16[1024,512]{1,0:T(8,128)(2,1)S(1)} %collective-permute-done.9.refs_1_, bf16[1024,512]{1,0:T(8,128)(2,1)S(1)} %collective-permute-done.10.value_ref.refs_2_, ...), custom_call_target="tpu_custom_call" | custom-call | flops 1000 | bytes 1000 | tf_op jit(solution)/shard_map/project/pallas_call | solution.py:340
  94.7 1.7 %collective-permute-done.26.rest_3_ = bf16[64,512]{1,0:T(8,128)(2,1)S(1)} collective-permute-done((bf16[64,512]{1,0:T(8,128)(2,1)S(1)}, bf16[64,512]{1,0:T(8,128)(2,1)S(1)}, u32[]{:S(2)}, u32[]{:S(2)}) %collective-permute-start.26) | collective-permute-done | bytes 65568 | tf_op jit(solution)/shard_map/ppermute | solution.py:35
  96.4 3.0 %collective-permute-done.23.got_ref = bf16[1024,256]{1,0:T(8,128)(2,1)S(1)} collective-permute-done((bf16[1024,256]{1,0:T(8,128)(2,1)S(1)}, bf16[1024,256]{1,0:T(8,128)(2,1)S(1)}, u32[]{:S(2)}, u32[]{:S(2)}) %collective-permute-start.23) | collective-permute-done | bytes 524320 | tf_op jit(solution)/shard_map/ppermute | solution.py:40
  99.6 3.1 %collective-permute-start.28 = (bf16[288,256]{1,0:T(8,128)(2,1)S(1)}, bf16[288,256]{1,0:T(8,128)(2,1)S(1)}, u32[]{:S(2)}, u32[]{:S(2)}) collective-permute-start(bf16[288,256]{1,0:T(8,128)(2,1)S(1)} %get-tuple-element.72), channel_id=1, source_target_pairs={{0,4},{2,6},{4,0},{6,2},{8,12},{10,14},{12,8},{14,10},{16,20},{18,... | collective-permute-start | bytes 442376 | tf_op jit(solution)/shard_map/ppermute | solution.py:35
  102.8 1.7 %collective-permute-start.19 = (bf16[256,256]{1,0:T(8,128)(2,1)S(1)}, bf16[256,256]{1,0:T(8,128)(2,1)S(1)}, u32[]{:S(2)}, u32[]{:S(2)}) collective-permute-start(bf16[256,256]{1,0:T(8,128)(2,1)S(1)} %get-tuple-element.58), channel_id=1, source_target_pairs={{0,4},{2,6},{4,0},{6,2},{8,12},{10,14},{12,8},{14,10},{16,20},{18,... | collective-permute-start | bytes 393224 | tf_op jit(solution)/shard_map/ppermute | solution.py:35
  104.5 8.8 %collective-permute-done.19.refs_2_ = bf16[256,256]{1,0:T(8,128)(2,1)S(1)} collective-permute-done((bf16[256,256]{1,0:T(8,128)(2,1)S(1)}, bf16[256,256]{1,0:T(8,128)(2,1)S(1)}, u32[]{:S(2)}, u32[]{:S(2)}) %collective-permute-start.19) | collective-permute-done | bytes 131104 | tf_op jit(solution)/shard_map/ppermute | solution.py:35
  113.4 2.3 %collective-permute-done.20.refs_3_ = bf16[256,256]{1,0:T(8,128)(2,1)S(1)} collective-permute-done((bf16[256,256]{1,0:T(8,128)(2,1)S(1)}, bf16[256,256]{1,0:T(8,128)(2,1)S(1)}, u32[]{:S(2)}, u32[]{:S(2)}) %collective-permute-start.20) | collective-permute-done | bytes 131104 | tf_op jit(solution)/shard_map/ppermute | solution.py:35
  (77 shorter events, 24.0 us)
Async XLA Ops:
  0.6 29.3 %collective-permute-start.8 = (bf16[256,2048]{1,0:T(8,128)(2,1)}, bf16[256,2048]{1,0:T(8,128)(2,1)S(1)}, u32[]{:S(2)}, u32[]{:S(2)}) collective-permute-start(bf16[256,2048]{1,0:T(8,128)(2,1)} %refs_7_.4), channel_id=1, source_target_pairs={{8,16},{10,18},{12,20},{14,22},{16,8},{18,10},{20,12},{22,14},{9,1... | collective-permute-start | bytes 3145736 | tf_op jit(solution)/shard_map/ppermute | solution.py:487
  1.4 30.0 %collective-permute-start.7 = (bf16[256,2048]{1,0:T(8,128)(2,1)}, bf16[256,2048]{1,0:T(8,128)(2,1)S(1)}, u32[]{:S(2)}, u32[]{:S(2)}) collective-permute-start(bf16[256,2048]{1,0:T(8,128)(2,1)} %refs_7_.4), channel_id=1, source_target_pairs={{0,8},{2,10},{4,12},{6,14},{8,0},{10,2},{12,4},{14,6},{16,24},{18,... | collective-permute-start | bytes 3145736 | tf_op jit(solution)/shard_map/ppermute | solution.py:487
  9.3 9.5 %collective-permute-start.1 = (bf16[256,512]{1,0:T(8,128)(2,1)}, bf16[256,512]{1,0:T(8,128)(2,1)S(1)}, u32[]{:S(2)}, u32[]{:S(2)}) collective-permute-start(bf16[256,512]{1,0:T(8,128)(2,1)} %get-tuple-element.40), channel_id=1, source_target_pairs={{0,4},{2,6},{4,0},{6,2},{8,12},{10,14},{12,8},{14,10},{16,20},{18,... | collective-permute-start | bytes 786440 | tf_op jit(solution)/shard_map/ppermute | solution.py:35
  10.9 9.6 %collective-permute-start = (bf16[256,512]{1,0:T(8,128)(2,1)}, bf16[256,512]{1,0:T(8,128)(2,1)S(1)}, u32[]{:S(2)}, u32[]{:S(2)}) collective-permute-start(bf16[256,512]{1,0:T(8,128)(2,1)} %get-tuple-element.39), channel_id=1, source_target_pairs={{0,2},{2,0},{4,6},{6,4},{8,10},{10,8},{12,14},{14,12},{16,18},{18,... | collective-permute-start | bytes 786440 | tf_op jit(solution)/shard_map/ppermute | solution.py:35
  10.9 12.6 %collective-permute-start.2 = (bf16[256,512]{1,0:T(8,128)(2,1)S(1)}, bf16[256,512]{1,0:T(8,128)(2,1)S(1)}, u32[]{:S(2)}, u32[]{:S(2)}) collective-permute-start(bf16[256,512]{1,0:T(8,128)(2,1)S(1)} %get-tuple-element.41), channel_id=1, source_target_pairs={{0,6},{2,4},{4,2},{6,0},{8,14},{10,12},{12,10},{14,8},{16,22},{18,... | collective-permute-start | bytes 786440 | tf_op jit(solution)/shard_map/ppermute | solution.py:35
  20.5 16.2 %collective-permute-start.6 = (bf16[2,256,512]{2,1,0:T(8,128)(2,1)S(1)}, bf16[2,256,512]{2,1,0:T(8,128)(2,1)S(1)}, u32[]{:S(2)}, u32[]{:S(2)}) collective-permute-start(bf16[2,256,512]{2,1,0:T(8,128)(2,1)S(1)} %get-tuple-element.45), channel_id=1, source_target_pairs={{0,4},{2,6},{4,0},{6,2},{8,12},{10,14},{12,8},{14,10},{16,20},{18,... | collective-permute-start | bytes 1572872 | tf_op jit(solution)/shard_map/ppermute | solution.py:35
  23.5 13.2 %collective-permute-start.4 = (bf16[256,512]{1,0:T(8,128)(2,1)S(1)}, bf16[256,512]{1,0:T(8,128)(2,1)S(1)}, u32[]{:S(2)}, u32[]{:S(2)}) collective-permute-start(bf16[256,512]{1,0:T(8,128)(2,1)S(1)} %get-tuple-element.74), channel_id=1, source_target_pairs={{8,0},{10,2},{12,4},{14,6},{16,8},{18,10},{20,12},{22,14},{24,16},... | collective-permute-start | bytes 786440 | tf_op jit(solution)/shard_map/ppermute | solution.py:500
  25.2 11.5 %collective-permute-start.3 = (bf16[256,512]{1,0:T(8,128)(2,1)S(1)}, bf16[256,512]{1,0:T(8,128)(2,1)S(1)}, u32[]{:S(2)}, u32[]{:S(2)}) collective-permute-start(bf16[256,512]{1,0:T(8,128)(2,1)S(1)} %get-tuple-element.75), channel_id=1, source_target_pairs={{0,8},{2,10},{4,12},{6,14},{8,16},{10,18},{12,20},{14,22},{16,24},... | collective-permute-start | bytes 786440 | tf_op jit(solution)/shard_map/ppermute | solution.py:499
  29.9 28.5 %collective-permute-start.14 = (bf16[256,2048]{1,0:T(8,128)(2,1)S(1)}, bf16[256,2048]{1,0:T(8,128)(2,1)S(1)}, u32[]{:S(2)}, u32[]{:S(2)}) collective-permute-start(bf16[256,2048]{1,0:T(8,128)(2,1)S(1)} %collective-permute-done.8.refs_14_.refs_6_), channel_id=1, source_target_pairs={{8,0},{10,2},{12,4},{14,6},{16,24},{18,26},{20,28},{22,30},{9,1},{... | collective-permute-start | bytes 3145736 | tf_op jit(solution)/shard_map/ppermute | solution.py:487
  31.4 12.9 %collective-permute-start.13 = (bf16[256,2048]{1,0:T(8,128)(2,1)S(1)}, bf16[256,2048]{1,0:T(8,128)(2,1)S(1)}, u32[]{:S(2)}, u32[]{:S(2)}) collective-permute-start(bf16[256,2048]{1,0:T(8,128)(2,1)S(1)} %collective-permute-done.7.refs_13_.refs_7_), channel_id=1, source_target_pairs={{16,8},{18,10},{20,12},{22,14},{8,16},{10,18},{12,20},{14,22},{17,... | collective-permute-start | bytes 3145736 | tf_op jit(solution)/shard_map/ppermute | solution.py:487
  42.2 24.4 %collective-permute-start.10 = (bf16[1024,512]{1,0:T(8,128)(2,1)S(1)}, bf16[1024,512]{1,0:T(8,128)(2,1)S(1)}, u32[]{:S(2)}, u32[]{:S(2)}) collective-permute-start(bf16[1024,512]{1,0:T(8,128)(2,1)S(1)} %get-tuple-element.46.refs_0_), channel_id=1, source_target_pairs={{0,4},{2,6},{4,0},{6,2},{8,12},{10,14},{12,8},{14,10},{16,20},{18,... | collective-permute-start | bytes 3145736 | tf_op jit(solution)/shard_map/ppermute | solution.py:35
  43.8 24.9 %collective-permute-start.9 = (bf16[1024,512]{1,0:T(8,128)(2,1)S(1)}, bf16[1024,512]{1,0:T(8,128)(2,1)S(1)}, u32[]{:S(2)}, u32[]{:S(2)}) collective-permute-start(bf16[1024,512]{1,0:T(8,128)(2,1)S(1)} %get-tuple-element.46.refs_0_), channel_id=1, source_target_pairs={{0,2},{2,0},{4,6},{6,4},{8,10},{10,8},{12,14},{14,12},{16,18},{18,... | collective-permute-start | bytes 3145736 | tf_op jit(solution)/shard_map/ppermute | solution.py:35
  44.3 41.0 %collective-permute-start.21 = (bf16[256,2048]{1,0:T(8,128)(2,1)S(1)}, bf16[256,2048]{1,0:T(8,128)(2,1)S(1)}, u32[]{:S(2)}, u32[]{:S(2)}) collective-permute-start(bf16[256,2048]{1,0:T(8,128)(2,1)S(1)} %collective-permute-done.13.refs_8_.refs_6_), channel_id=1, source_target_pairs={{8,0},{10,2},{12,4},{14,6},{16,24},{18,26},{20,28},{22,30},{9,1},{... | collective-permute-start | bytes 3145736 | tf_op jit(solution)/shard_map/ppermute | solution.py:487
  67.2 9.2 %collective-permute-start.22 = (bf16[256,512]{1,0:T(8,128)(2,1)S(1)}, bf16[256,512]{1,0:T(8,128)(2,1)S(1)}, u32[]{:S(2)}, u32[]{:S(2)}) collective-permute-start(bf16[256,512]{1,0:T(8,128)(2,1)S(1)} %get-tuple-element.62), channel_id=1, source_target_pairs={{0,7},{1,6},{2,5},{3,4},{4,3},{5,2},{6,1},{7,0},{8,15},{9,14},{10,... | collective-permute-start | bytes 786440 | tf_op jit(solution)/shard_map/ppermute | solution.py:520
  70.8 21.8 %collective-permute-start.17 = (bf16[1024,256]{1,0:T(8,128)(2,1)S(1)}, bf16[1024,256]{1,0:T(8,128)(2,1)S(1)}, u32[]{:S(2)}, u32[]{:S(2)}) collective-permute-start(bf16[1024,256]{1,0:T(8,128)(2,1)S(1)} %get-tuple-element.55), channel_id=1, source_target_pairs={{0,1},{1,0},{2,3},{3,2},{4,5},{5,4},{6,7},{7,6},{8,9},{9,8},{10,11... | collective-permute-start | bytes 1572872 | tf_op jit(solution)/shard_map/ppermute | solution.py:40
  86.7 12.7 %collective-permute-start.23 = (bf16[1024,256]{1,0:T(8,128)(2,1)S(1)}, bf16[1024,256]{1,0:T(8,128)(2,1)S(1)}, u32[]{:S(2)}, u32[]{:S(2)}) collective-permute-start(bf16[1024,256]{1,0:T(8,128)(2,1)S(1)} %get-tuple-element.66), channel_id=1, source_target_pairs={{0,1},{1,0},{2,3},{3,2},{4,5},{5,4},{6,7},{7,6},{8,9},{9,8},{10,11... | collective-permute-start | bytes 1572872 | tf_op jit(solution)/shard_map/ppermute | solution.py:40
  88.2 6.4 %collective-permute-start.24 = (bf16[64,512]{1,0:T(8,128)(2,1)S(1)}, bf16[64,512]{1,0:T(8,128)(2,1)S(1)}, u32[]{:S(2)}, u32[]{:S(2)}) collective-permute-start(bf16[64,512]{1,0:T(8,128)(2,1)S(1)} %get-tuple-element.67), channel_id=1, source_target_pairs={{0,8},{2,10},{4,12},{6,14},{8,0},{10,2},{12,4},{14,6},{16,24},{18,... | collective-permute-start | bytes 196616 | tf_op jit(solution)/shard_map/ppermute | solution.py:35
  88.2 6.4 %collective-permute-start.25 = (bf16[64,512]{1,0:T(8,128)(2,1)S(1)}, bf16[64,512]{1,0:T(8,128)(2,1)S(1)}, u32[]{:S(2)}, u32[]{:S(2)}) collective-permute-start(bf16[64,512]{1,0:T(8,128)(2,1)S(1)} %get-tuple-element.68), channel_id=1, source_target_pairs={{0,16},{2,18},{4,20},{6,22},{8,24},{10,26},{12,28},{14,30},{16,0},... | collective-permute-start | bytes 196616 | tf_op jit(solution)/shard_map/ppermute | solution.py:35
  92.7 11.8 %collective-permute-start.18 = (bf16[256,256]{1,0:T(8,128)(2,1)S(1)}, bf16[256,256]{1,0:T(8,128)(2,1)S(1)}, u32[]{:S(2)}, u32[]{:S(2)}) collective-permute-start(bf16[256,256]{1,0:T(8,128)(2,1)S(1)} %get-tuple-element.57), channel_id=1, source_target_pairs={{0,2},{2,0},{4,6},{6,4},{8,10},{10,8},{12,14},{14,12},{16,18},{18,... | collective-permute-start | bytes 393224 | tf_op jit(solution)/shard_map/ppermute | solution.py:35
  99.5 16.1 %collective-permute-start.27 = (bf16[288,256]{1,0:T(8,128)(2,1)S(1)}, bf16[288,256]{1,0:T(8,128)(2,1)S(1)}, u32[]{:S(2)}, u32[]{:S(2)}) collective-permute-start(bf16[288,256]{1,0:T(8,128)(2,1)S(1)} %get-tuple-element.71), channel_id=1, source_target_pairs={{0,2},{2,0},{4,6},{6,4},{8,10},{10,8},{12,14},{14,12},{16,18},{18,... | collective-permute-start | bytes 442376 | tf_op jit(solution)/shard_map/ppermute | solution.py:35
  99.6 16.1 %collective-permute-start.28 = (bf16[288,256]{1,0:T(8,128)(2,1)S(1)}, bf16[288,256]{1,0:T(8,128)(2,1)S(1)}, u32[]{:S(2)}, u32[]{:S(2)}) collective-permute-start(bf16[288,256]{1,0:T(8,128)(2,1)S(1)} %get-tuple-element.72), channel_id=1, source_target_pairs={{0,4},{2,6},{4,0},{6,2},{8,12},{10,14},{12,8},{14,10},{16,20},{18,... | collective-permute-start | bytes 442376 | tf_op jit(solution)/shard_map/ppermute | solution.py:35
  102.7 13.0 %collective-permute-start.29 = (bf16[288,256]{1,0:T(8,128)(2,1)S(1)}, bf16[288,256]{1,0:T(8,128)(2,1)S(1)}, u32[]{:S(2)}, u32[]{:S(2)}) collective-permute-start(bf16[288,256]{1,0:T(8,128)(2,1)S(1)} %get-tuple-element.73), channel_id=1, source_target_pairs={{0,6},{2,4},{4,2},{6,0},{8,14},{10,12},{12,10},{14,8},{16,22},{18,... | collective-permute-start | bytes 442376 | tf_op jit(solution)/shard_map/ppermute | solution.py:35
  102.8 10.6 %collective-permute-start.19 = (bf16[256,256]{1,0:T(8,128)(2,1)S(1)}, bf16[256,256]{1,0:T(8,128)(2,1)S(1)}, u32[]{:S(2)}, u32[]{:S(2)}) collective-permute-start(bf16[256,256]{1,0:T(8,128)(2,1)S(1)} %get-tuple-element.58), channel_id=1, source_target_pairs={{0,4},{2,6},{4,0},{6,2},{8,12},{10,14},{12,8},{14,10},{16,20},{18,... | collective-permute-start | bytes 393224 | tf_op jit(solution)/shard_map/ppermute | solution.py:35
  104.5 11.1 %collective-permute-start.20 = (bf16[256,256]{1,0:T(8,128)(2,1)S(1)}, bf16[256,256]{1,0:T(8,128)(2,1)S(1)}, u32[]{:S(2)}, u32[]{:S(2)}) collective-permute-start(bf16[256,256]{1,0:T(8,128)(2,1)S(1)} %get-tuple-element.59), channel_id=1, source_target_pairs={{0,6},{2,4},{4,2},{6,0},{8,14},{10,12},{12,10},{14,8},{16,22},{18,... | collective-permute-start | bytes 393224 | tf_op jit(solution)/shard_map/ppermute | solution.py:35
  (18 other events, 130.6 us)
